TPU v7x, 128 devices: a whole 4x4x4 slice. The times are simulated.
128 devices in a mesh: row: 16 (over y, x_hi, core), col: 8 (over x_lo, z).
Axes of the slice: x: 4 (x_hi: 2, x_lo: 2; x = x_hi * 2 + x_lo), y: 4, z: 4, core: 2. Of those that a mesh axis runs over, the one named last changes fastest.
Arguments:
- tokens: bfloat16 [32, 16384], P(None, ('row', 'col')), may hold values from -40 to 40
- norm_gain: bfloat16 [16384], P('row'), may hold values from 0.099609375 to 1.8984375
- query_weight: bfloat16 [16384, 16384], P('row', 'col'), may hold values from -0.046875 to 0.046875
- keyval_weight: bfloat16 [16384, 2048], P('row', 'col'), may hold values from -0.046875 to 0.046875
- out_weight: bfloat16 [16384, 16384], P('col', 'row'), may hold values from -0.375 to 0.375
- key_cache: bfloat16 [32, 8192, 1024], P('row', None, 'col'), may hold values from -68 to 68
- value_cache: bfloat16 [32, 8192, 1024], P('row', None, 'col'), may hold values from -6 to 6
- lengths: int32 [32], P('row'), may hold values from 1 to 8192, as said below
- next_query: bfloat16 [16384, 16384], P(None, ('col', 'row')), may hold values from -0.046875 to 0.046875
Outputs:
- mixed: bfloat16 [32, 16384], P(None, ('row', 'col'))
- relaid: bfloat16 [16384, 16384], P('row', 'col')
Inputs may be any that keep to these rules, and one draw needn't show every extreme that they name: `lengths`: one row holds exactly 8192 positions.
All inputs are finite; a program needn't handle non-finite values.
Results may differ from a plain program's by a relative error of at most 0.012.
The roundings to bfloat16 on the way count: a program that leaves them out, or rounds other values in their place, can miss the bound.
Values may be sent and summed in bfloat16 or wider, within the bound.
No kernel may reach another device: no remote copies, remote signals or barrier semaphores. Data moves between devices by JAX's collectives and lax.ppermute only.
A program may use at most 128 MiB of HBM per device.

v0:
```python
import jax
import jax.numpy as jnp
from jax import lax
from jax.sharding import PartitionSpec as P

HD = 128


masked_score = -1e30


def rotary(vectors, positions):
    half_dim = vectors.shape[-1] // 2
    freqs = 500000.0 ** (-(jnp.arange(half_dim).astype(jnp.float32) * 2.0 / vectors.shape[-1]))
    angles = positions.astype(jnp.float32)[:, None] * freqs[None, :]
    cosine = jnp.cos(angles)[:, None, :]
    sine_part = jnp.sin(angles)[:, None, :]
    front_half = vectors[..., :half_dim]
    back_half = vectors[..., half_dim:]
    return jnp.concatenate(
        [front_half * cosine - back_half * sine_part, back_half * cosine + front_half * sine_part],
        axis=-1,
    )


def relay_weights(next_query):
    return lax.all_to_all(next_query, "row", split_axis=0, concat_axis=1, tiled=True)


def body(
    tokens,
    norm_gain,
    query_weight,
    keyval_weight,
    out_weight,
    key_cache,
    value_cache,
    lengths,
    next_query,
):
    rows_here = lengths.shape[0]
    head_dim = HD
    row_index = lax.axis_index("row")
    in_rows = query_weight.shape[0]
    everything = lax.all_gather(tokens, ("row", "col"), axis=1, tiled=True)
    every_f = everything.astype(jnp.float32)
    mean_square = jnp.mean(every_f * every_f, axis=1)
    local_feats = lax.dynamic_slice_in_dim(everything, row_index * in_rows, in_rows, 1)
    own_square = lax.dynamic_slice_in_dim(mean_square, row_index * rows_here, rows_here, 0)
    inv_scale = lax.rsqrt(own_square + 1e-05)[:, None]
    normed = (local_feats.astype(jnp.float32) * norm_gain.astype(jnp.float32)[None, :]).astype(
        jnp.bfloat16
    )
    projected = lax.psum_scatter(
        jnp.concatenate(
            [
                jnp.dot(normed, query_weight, preferred_element_type=jnp.float32),
                jnp.dot(normed, keyval_weight, preferred_element_type=jnp.float32),
            ],
            axis=1,
        ),
        "row",
        scatter_dimension=0,
        tiled=True,
    )
    query_cols = query_weight.shape[1]
    query_heads = query_cols // head_dim
    kv_heads = keyval_weight.shape[1] // (2 * head_dim)
    group = query_heads // kv_heads
    proj_query = projected[:, :query_cols] * inv_scale
    proj_keyval = projected[:, query_cols:] * inv_scale
    queries = rotary(proj_query.reshape(rows_here, query_heads, head_dim), lengths).astype(
        jnp.bfloat16
    )
    queries = queries.reshape(rows_here, kv_heads, group, head_dim)
    keyval = proj_keyval.reshape(rows_here, kv_heads, 2, head_dim)
    new_key = rotary(keyval[:, :, 0], lengths).astype(jnp.bfloat16)
    new_value = keyval[:, :, 1].astype(jnp.bfloat16)
    positions = key_cache.shape[1]
    score_scale = head_dim ** (-0.5)
    key_rows = key_cache.reshape(rows_here, positions, kv_heads, head_dim)
    value_rows = value_cache.reshape(rows_here, positions, kv_heads, head_dim)
    scores = (
        jnp.einsum("rkgd,rpkd->rkgp", queries, key_rows, preferred_element_type=jnp.float32)
        * score_scale
    )
    visible = jnp.arange(positions)[None, :] < lengths[:, None]
    scores = jnp.where(visible[:, None, None, :], scores, masked_score)
    self_score = (
        jnp.einsum("rkgd,rkd->rkg", queries, new_key, preferred_element_type=jnp.float32)
        * score_scale
    )
    highest = jnp.maximum(jnp.max(scores, axis=-1), self_score)
    expos = jnp.exp(scores - highest[..., None])
    self_expo = jnp.exp(self_score - highest)
    totals = jnp.sum(expos, axis=-1) + self_expo
    rounded = expos.astype(jnp.bfloat16)
    numer = jnp.einsum("rkgp,rpkd->rkgd", rounded, value_rows, preferred_element_type=jnp.float32)
    numer = numer + self_expo[..., None] * new_value.astype(jnp.float32)[:, :, None, :]
    attended = (numer / totals[..., None]).astype(jnp.bfloat16).reshape(rows_here, query_cols)
    partial_out = jnp.dot(
        lax.all_gather(attended, "row", axis=0, tiled=True),
        out_weight,
        preferred_element_type=jnp.float32,
    )
    mixed = lax.psum_scatter(partial_out, "col", scatter_dimension=1, tiled=True).astype(
        jnp.bfloat16
    )
    relaid = relay_weights(next_query)
    return (mixed, relaid)


def solution(mesh):
    in_specs = (
        P(None, ("row", "col")),
        P("row"),
        P("row", "col"),
        P("row", "col"),
        P("col", "row"),
        P("row", None, "col"),
        P("row", None, "col"),
        P("row"),
        P(None, ("col", "row")),
    )
    out_specs = (P(None, ("row", "col")), P("row", "col"))
    return jax.shard_map(body, mesh=mesh, in_specs=in_specs, out_specs=out_specs, check_vma=False)
```

profile of v0, /device:TPU:0, one launch (start us, length us, event | category | flops | bytes accessed | tf_op | source)
XLA Modules:
  0.0 518.0 jit_solution(15884785339634356787)
XLA Ops:
  7.2 0.0 all-gather.3.cloned.1.call-start
  7.2 0.7 all-gather.3.cloned.1.call-update
  7.9 7.3 %all-to-all-start = ((bf16[16,1024,128]{2,1,0:T(8,128)(2,1)}), bf16[16,1024,128]{2,1,0:T(8,128)(2,1)}, u32[]{:S(2)}, u32[]{:S(2)}) async-start(bf16[16,1024,128]{2,1,0:T(8,128)(2,1)} %bitcast.35), calls=%async_computation.1 | async-start | bytes 8388608 | tf_op jit(solution)/shard_map/all_to_all | solution.py:27
  15.3 0.0 all-reduce.3.cloned.1.call-start
  15.4 0.6 dynamic-slice
  16.6 0.1 multiply_cosine_fusion.1
  16.8 0.1 iota_compare_fusion
  16.9 275.3 %all-gather.3.cloned.1.call-done = bf16[32,16384]{1,0:T(8,128)(2,1)} async-done(((bf16[32,128]{1,0:T(8,128)(2,1)}), bf16[32,16384]{1,0:T(8,128)(2,1)}) %all-gather.3.cloned.1.call-update) | async-done | bytes 1048592 | tf_op jit(solution)/shard_map/all_gather | solution.py:45
  292.1 3.1 fusion.8
  295.3 0.2 fusion.7
  295.5 0.7 pad_maximum_fusion
  296.2 0.0 all-reduce.3.cloned.1.call-update
  296.3 0.0 reduce-scatter.2.cloned.1.call-start
  296.3 0.3 multiply_reduce_fusion
  296.6 0.1 add_rsqrt_fusion
  296.7 132.7 %all-reduce.3.cloned.1.call-done = f32[32,2304]{1,0:T(8,128)} async-done(((f32[32,2304]{1,0:T(8,128)}), f32[32,2304]{1,0:T(8,128)}) %all-reduce.3.cloned.1.call-update) | async-done | bytes 294928
  429.4 1.1 fusion.9
  430.5 1.0 fusion.10
  431.5 0.1 fusion.23
  431.6 0.1 maximum_bitcast_fusion
  431.7 0.1 subtract_convert_fusion
  431.7 0.2 fusion.11
  431.9 3.5 fusion.30
  435.5 0.3 fusion.3
  435.8 0.7 fusion.2
  436.6 19.6 %all-gather = bf16[16,2,2048]{2,1,0:T(2,128)(2,1)S(1)} all-gather(bf16[1,2,2048]{2,1,0:T(2,128)(2,1)S(1)} %reshape.217), channel_id=1, replica_groups=mesh['row'=16,'col'=8] {'row'}, dimensions={0}, use_global_device_ids=true | all-gather | bytes 139264 | tf_op jit(solution)/shard_map/all_gather | solution.py:102
  456.2 0.1 reshape.218
  456.2 3.7 fusion.31
  459.9 37.3 %reduce-scatter.2.cloned.1.call-done = f32[32,128]{1,0:T(8,128)} async-done(((f32[32,1024]{1,0:T(8,128)}), f32[32,128]{1,0:T(8,128)}) %reduce-scatter.2.cloned.1.call-update) | async-done | bytes 16400 | tf_op jit(solution)/shard_map/reduce_scatter | solution.py:106
  497.2 1.3 convert_element_type.61
  498.6 6.4 %copy.17 = bf16[16,1024,128]{1,2,0:T(8,128)(2,1)} copy(bf16[16,1024,128]{2,1,0:T(8,128)(2,1)} %all-to-all-done) | data formatting | bytes 8388608 | tf_op jit(solution)/shard_map/all_to_all | solution.py:27
  505.0 6.4 %copy.18 = bf16[1024,2048]{1,0:T(8,128)(2,1)} copy(bf16[1024,2048]{0,1:T(8,128)(2,1)} %bitcast.34) | data formatting | bytes 8388608
  (24 shorter events, 0.1 us)
Async XLA Ops:
  7.2 288.1 %copy-start = (bf16[1024,256]{1,0:T(8,128)(2,1)S(1)}, bf16[1024,256]{1,0:T(8,128)(2,1)}, u32[]{:S(2)}) copy-start(bf16[1024,256]{1,0:T(8,128)(2,1)} %param.12) | copy-start | bytes 1572868
  7.2 285.0 %all-gather.3.cloned.1.call-start = ((), (), s32[]{:S(2)}) async-start(), calls=%async_computation.2 | async-start | bytes 1056768 | tf_op jit(solution)/shard_map/all_gather | solution.py:45
  7.9 7.4 %copy-start.3 = (bf16[1024]{0:T(1024)(128)(2,1)S(1)}, bf16[1024]{0:T(1024)(128)(2,1)}, u32[]{:S(2)}) copy-start(bf16[1024]{0:T(1024)(128)(2,1)} %param.10) | copy-start | bytes 6148
  7.9 7.4 %copy-start.4 = (s32[2]{0:T(128)S(1)}, s32[2]{0:T(128)}, u32[]{:S(2)}) copy-start(s32[2]{0:T(128)} %param.16) | copy-start | bytes 28
  7.9 7.5 %copy-start.5 = (u32[128]{0:T(128)S(1)}, u32[128]{0:T(128)}, u32[]{:S(2)}) copy-start(u32[128]{0:T(128)} %constant.42) | copy-start | bytes 1540
  7.9 490.6 %all-to-all-start = ((bf16[16,1024,128]{2,1,0:T(8,128)(2,1)}), bf16[16,1024,128]{2,1,0:T(8,128)(2,1)}, u32[]{:S(2)}, u32[]{:S(2)}) async-start(bf16[16,1024,128]{2,1,0:T(8,128)(2,1)} %bitcast.35), calls=%async_computation.1 | async-start | bytes 8388608 | tf_op jit(solution)/shard_map/all_to_all | solution.py:27
  15.3 414.1 %all-reduce.3.cloned.1.call-start = ((), (), s32[]{:S(2)}) async-start(), calls=%async_computation.4 | async-start | bytes 589824
  292.1 3.2 copy-start.2
  296.3 201.0 %reduce-scatter.2.cloned.1.call-start = ((), (), s32[]{:S(2)}) async-start(), calls=%async_computation.3 | async-start | bytes 147456 | tf_op jit(solution)/shard_map/reduce_scatter | solution.py:106
  429.4 6.4 %copy-start.1 = (bf16[2,8192,128]{2,1,0:T(8,128)(2,1)S(1)}, bf16[2,8192,128]{2,1,0:T(8,128)(2,1)}, u32[]{:S(2)}) copy-start(bf16[2,8192,128]{2,1,0:T(8,128)(2,1)} %param.15) | copy-start | bytes 12582916
Sparse Core Ops, SparseCore 0:
  9.6 282.4 all-gather.2
  296.4 132.9 all-reduce.2
  460.0 37.1 reduce-scatter.1
where the time goes:
time: 519 us; the launch traced here: 518 us
  waiting for transfers between devices  446 us (86%)
  blocking collectives  19.6 us (4%)
  between operations  14.6 us (3%)
  local copies, waits for them, and re-layouts  13.6 us (3%)
  matrix products  11.4 us (2%)
  starting transfers between devices  7.43 us (1%)
  other arithmetic  5.37 us (1%)
    all_gather x1, waiting for transfers between devices, body(): everything = lax.all_gather(tokens, ('row', 'col'), axis=1, tiled=True)  275 us
    unnamed x4, waiting for transfers between devices  133 us
    reduce_scatter x1, waiting for transfers between devices, body(): lax.psum_scatter(partial_out, 'col', scatter_dimension=1, tiled=True)  37.3 us
    all_gather x1, blocking collectives, body(): lax.all_gather(attended, 'row', axis=0, tiled=True)  19.6 us
  transfers between devices with their start and end apart: 4, of which 3 were waited for; matrix products, arithmetic and copies ran while one was open for 3% of the time, Pallas kernels for 0%

commit v1 on v0

v1 whole, which is shorter than its diff:
```python
import functools

import jax
import jax.numpy as jnp
from jax import lax
from jax.experimental import pallas as pl
from jax.experimental.pallas import tpu as pltpu
from jax.sharding import PartitionSpec as P

HD = 128
masked_score = -1e30
SQUARES = 128
CHUNK = 1024

CORE, X_HALF, Y_NEAR, Y_FAR = 1, 2, 4, 12
Z_NEAR, Z_FAR, X_LOW = 1, 3, 4

COST = 1_000_000_000
VMEM = pl.BlockSpec(memory_space=pltpu.VMEM)
SMEM = pl.BlockSpec(memory_space=pltpu.SMEM)
HBM = pl.BlockSpec(memory_space=pltpu.HBM)
ANYWHERE = pl.BlockSpec(memory_space=pl.ANY)


def call(kernel, out, in_specs, out_specs, scratch=(), megabytes=16, cost=0.0, **options):
    return pl.pallas_call(
        kernel,
        out_shape=out,
        in_specs=in_specs,
        out_specs=out_specs,
        scratch_shapes=list(scratch),
        compiler_params=pltpu.CompilerParams(vmem_limit_bytes=megabytes << 20),
        cost_estimate=pl.CostEstimate(
            flops=int(cost * COST) + 1, bytes_accessed=1, transcendentals=0
        ),
        **options,
    )


def like(array, rows):
    return jax.ShapeDtypeStruct((rows,) + array.shape[1:], array.dtype)


def rotary_factors(positions, width):
    half_dim = width // 2
    freqs = 500000.0 ** (-(jnp.arange(half_dim).astype(jnp.float32) * 2.0 / width))
    angles = positions.astype(jnp.float32)[:, None] * freqs[None, :]
    cosine, sine = jnp.cos(angles), jnp.sin(angles)
    return (
        jnp.concatenate([cosine, cosine], axis=-1),
        jnp.concatenate([-sine, sine], axis=-1),
    )


def flip(block, axis, bits):
    size = lax.axis_size(axis)
    return lax.ppermute(block, axis, [(i, i ^ bits) for i in range(size)])


def shift_y(block, steps):
    size = lax.axis_size("row")
    return lax.ppermute(block, "row", [(i, (i + 4 * steps) % size) for i in range(size)])


def tie(*values):
    return lax.optimization_barrier(values)


def join_kernel(own_ref, other_ref, out_ref):
    rows = own_ref.shape[0]
    out_ref[:rows] = own_ref[...]
    out_ref[rows:] = other_ref[...]


def join(own, other, cost=0.0):
    both = like(own, 2 * own.shape[0])
    return call(join_kernel, both, [VMEM] * 2, VMEM, megabytes=2, cost=cost)(own, other)


def add_halves_kernel(kept_ref, got_ref, next_kept_ref, next_sent_ref):
    half = next_kept_ref.shape[0]
    next_kept_ref[...] = kept_ref[:half] + got_ref[:half]
    next_sent_ref[...] = kept_ref[half:] + got_ref[half:]


def add_halves(kept, got, cost=0.0):
    half = like(kept, kept.shape[0] // 2)
    return call(
        add_halves_kernel, [half, half], [VMEM] * 2, [VMEM] * 2, megabytes=2, cost=cost
    )(kept, got)


def gray(number):
    return number ^ (number >> 1)


def batch_row(me_ref, place):
    row = me_ref[0]
    y, x_half, core = row >> 2, (row >> 1) & 1, row & 1
    device = (
        ((y ^ gray((place >> 1) & 3)) << 2)
        | ((x_half ^ ((place >> 3) & 1)) << 1)
        | (core ^ (place >> 4))
    )
    return (device << 1) | (place & 1)


def project_kernel(
    me_ref, near_ref, far_ref, gain_ref, query_ref, keyval_ref, kept_ref, sent_ref, feats_scr
):
    half, rows = near_ref.shape[0], near_ref.shape[1]
    feats_scr[:half] = near_ref[...]
    feats_scr[half:] = far_ref[...]
    x_low, z = me_ref[1] >> 2, me_ref[1] & 3
    blocks = [
        feats_scr[gray((part & 3) ^ z) * 2 + ((part >> 2) ^ x_low)] for part in range(2 * half)
    ]
    shape = (rows, rows)
    order = batch_row(me_ref, lax.broadcasted_iota(jnp.int32, shape, 0))
    order = jnp.where(order == lax.broadcasted_iota(jnp.int32, shape, 1), 1.0, 0.0)
    feats = jnp.dot(
        order.astype(jnp.bfloat16),
        jnp.concatenate(blocks, axis=1),
        preferred_element_type=jnp.float32,
    )
    square_sum = jnp.sum(feats * feats, axis=1, keepdims=True)
    normed = (feats * gain_ref[...].astype(jnp.float32)).astype(jnp.bfloat16)
    columns = query_ref.shape[1]
    cut = rows // 2

    def put(start, values):
        end = start + values.shape[1]
        kept_ref[:, start:end] = values[:cut]
        sent_ref[:, start:end] = values[cut:]

    step = 512
    for start in range(0, columns, step):
        put(
            start,
            jnp.dot(
                normed, query_ref[:, start : start + step], preferred_element_type=jnp.float32
            ),
        )
    put(columns, jnp.dot(normed, keyval_ref[...], preferred_element_type=jnp.float32))
    put(columns + keyval_ref.shape[1], jnp.broadcast_to(square_sum, (rows, SQUARES)))


def project(me, near, far, gain, query_weight, keyval_weight):
    rows = near.shape[1]
    columns = query_weight.shape[1] + keyval_weight.shape[1] + SQUARES
    half = jax.ShapeDtypeStruct((rows // 2, columns), jnp.float32)
    return call(
        project_kernel,
        [half, half],
        [SMEM] + [VMEM] * 5,
        [VMEM] * 2,
        [pltpu.VMEM((2 * near.shape[0],) + near.shape[1:], near.dtype)],
        cost=2.5,
    )(me, near, far, gain[None], query_weight, keyval_weight)


def attend_kernel(
    features, lengths_ref, kept_ref, got_ref, cos_ref, sin_ref, key_ref, value_ref, out_ref,
    proj_scr, query_scr, score_scr, rows_scr,
):
    rows, positions, head_dim = key_ref.shape
    heads = query_scr.shape[0]
    query_cols = heads * head_dim
    scale = head_dim ** (-0.5)
    proj_scr[...] = kept_ref[...] + got_ref[...]

    def rotate(vectors, b):
        return vectors * cos_ref[b : b + 1] + pltpu.roll(vectors, head_dim // 2, 1) * sin_ref[
            b : b + 1
        ]

    for b in range(rows):
        squares = proj_scr[b : b + 1, -SQUARES:]
        inv_scale = lax.rsqrt(squares / features + 1e-05)
        for h in range(heads):
            query_scr[h : h + 1, :] = (
                proj_scr[b : b + 1, h * head_dim : (h + 1) * head_dim] * inv_scale
            )
        query = rotate(query_scr[...], b).astype(jnp.bfloat16)
        new_key = proj_scr[b : b + 1, query_cols : query_cols + head_dim] * inv_scale
        new_key = rotate(jnp.broadcast_to(new_key, (8, head_dim)), b)[:1].astype(jnp.bfloat16)
        new_value = proj_scr[b : b + 1, query_cols + head_dim : query_cols + 2 * head_dim]
        new_value = (new_value * inv_scale).astype(jnp.bfloat16).astype(jnp.float32)
        self_score = (
            jnp.sum(
                query.astype(jnp.float32) * new_key.astype(jnp.float32), axis=1, keepdims=True
            )
            * scale
        )
        length = lengths_ref[b]
        top = self_score
        for start in range(0, positions, CHUNK):
            scores = (
                lax.dot_general(
                    query,
                    key_ref[b, start : start + CHUNK, :],
                    (((1,), (1,)), ((), ())),
                    preferred_element_type=jnp.float32,
                )
                * scale
            )
            place = start + lax.broadcasted_iota(jnp.int32, scores.shape, 1)
            scores = jnp.where(place < length, scores, masked_score)
            score_scr[:, start : start + CHUNK] = scores
            top = jnp.maximum(top, jnp.max(scores, axis=1, keepdims=True))
        self_expo = jnp.exp(self_score - top)
        totals = self_expo
        numer = self_expo * new_value
        for start in range(0, positions, CHUNK):
            expos = jnp.exp(score_scr[:, start : start + CHUNK] - top)
            totals = totals + jnp.sum(expos, axis=1, keepdims=True)
            numer = numer + jnp.dot(
                expos.astype(jnp.bfloat16),
                value_ref[b, start : start + CHUNK, :],
                preferred_element_type=jnp.float32,
            )
        attended = numer / totals
        for h in range(heads):
            rows_scr[b : b + 1, h * head_dim : (h + 1) * head_dim] = attended[h : h + 1, :]
    out_ref[...] = rows_scr[...].astype(jnp.bfloat16)


def attend(lengths, kept, got, cosine, sine, key_cache, value_cache, features, heads):
    rows, positions, head_dim = key_cache.shape
    return call(
        functools.partial(attend_kernel, features),
        jax.ShapeDtypeStruct((rows, heads * head_dim), jnp.bfloat16),
        [SMEM] + [VMEM] * 6,
        VMEM,
        [
            pltpu.VMEM(kept.shape, jnp.float32),
            pltpu.VMEM((heads, head_dim), jnp.float32),
            pltpu.VMEM((heads, positions), jnp.float32),
            pltpu.VMEM((rows, heads * head_dim), jnp.float32),
        ],
    )(lengths, kept, got, cosine, sine, key_cache, value_cache)


def mix_kernel(me_ref, own_ref, other_ref, weight_ref, kept_ref, sent_ref, blocks_scr):
    rows = 2 * own_ref.shape[0]
    shape = (rows, rows)
    order = batch_row(me_ref, lax.broadcasted_iota(jnp.int32, shape, 1))
    order = jnp.where(order == lax.broadcasted_iota(jnp.int32, shape, 0), 1.0, 0.0)
    attended = jnp.dot(
        order.astype(jnp.bfloat16),
        jnp.concatenate([own_ref[...], other_ref[...]], axis=0),
        preferred_element_type=jnp.float32,
    ).astype(jnp.bfloat16)
    x_low, z = me_ref[1] >> 2, me_ref[1] & 3
    step, width = 256, kept_ref.shape[2]
    for start in range(0, weight_ref.shape[1], step):
        mixed = jnp.dot(
            attended, weight_ref[:, start : start + step], preferred_element_type=jnp.float32
        )
        for k in range(step // width):
            part = start // width + k
            place = gray((part & 3) ^ z) * 2 + ((part >> 2) ^ x_low)
            blocks_scr[place] = mixed[:, k * width : (k + 1) * width]
    half = kept_ref.shape[0]
    kept_ref[...] = blocks_scr[:half]
    sent_ref[...] = blocks_scr[half:]


def mix(me, own, other, out_weight):
    rows, width = 2 * own.shape[0], out_weight.shape[1] // 8
    half = jax.ShapeDtypeStruct((4, rows, width), jnp.float32)
    return call(
        mix_kernel,
        [half, half],
        [SMEM] + [VMEM] * 3,
        [VMEM] * 2,
        [pltpu.VMEM((8, rows, width), jnp.float32)],
    )(me, own, other, out_weight)


def start_and_wait(copies):
    for copy in copies:
        copy.start()
    for copy in copies:
        copy.wait()


def stage_kernel(groups, me_ref, chunks_ref, *refs):
    pieces, (buffer, in_sems, out_sems) = refs[: len(groups)], refs[len(groups) :]
    row = me_ref[0]
    copies = []
    for piece, group in zip(pieces, groups):
        for i, (dy, dx, other) in enumerate(group):
            chip = ((((row >> 2) + dy) & 3) << 1) | (((row >> 1) & 1) ^ dx)
            chunk = chunks_ref.at[(chip << 1) | ((row & 1) ^ other)]
            k = len(copies)
            copies.append(
                (
                    pltpu.make_async_copy(chunk, buffer.at[k], in_sems.at[k]),
                    pltpu.make_async_copy(buffer.at[k], piece.at[i], out_sems.at[k]),
                )
            )
    for fetch, _ in copies:
        fetch.start()
    for fetch, store in copies:
        fetch.wait()
        store.start()
    for _, store in copies:
        store.wait()


def stage(me, chunks, groups):
    count = sum(len(group) for group in groups)
    return call(
        functools.partial(stage_kernel, groups),
        [like(chunks, len(group)) for group in groups],
        [SMEM, HBM],
        [HBM] * len(groups),
        [
            pltpu.VMEM((count,) + chunks.shape[1:], chunks.dtype),
            pltpu.SemaphoreType.DMA((count,)),
            pltpu.SemaphoreType.DMA((count,)),
        ],
        60,
    )(me, chunks)


def pack_kernel(count, slots, *refs):
    pieces, out_ref, sems = refs[:count], refs[-2], refs[-1]
    start_and_wait(
        [
            pltpu.make_async_copy(pieces[p].at[i], out_ref.at[k], sems.at[k])
            for k, (p, i) in enumerate(slots)
        ]
    )


def pack(pieces, slots):
    return call(
        functools.partial(pack_kernel, len(pieces), slots),
        like(pieces[0], len(slots)),
        [ANYWHERE] * len(pieces),
        ANYWHERE,
        [pltpu.SemaphoreType.DMA((len(slots),))],
        1,
    )(*pieces)


def place_kernel(count, slots, me_ref, *refs):
    pieces, relaid_ref, sems = refs[:count], refs[-2], refs[-1]
    row = me_ref[0]
    copies = []
    for k, (piece, slot, dy, dx, other) in enumerate(slots):
        chip = ((((row >> 2) - dy) & 3) << 1) | (((row >> 1) & 1) ^ dx)
        column = pl.multiple_of(((chip << 1) | ((row & 1) ^ other)) * HD, HD)
        copies.append(
            pltpu.make_async_copy(
                pieces[piece].at[slot], relaid_ref.at[:, pl.ds(column, HD)], sems.at[k]
            )
        )
    start_and_wait(copies)


def place(me, pieces, slots, relaid):
    rows, width = pieces[0].shape[1:]
    first = relaid is None
    return call(
        functools.partial(place_kernel, len(pieces), slots),
        jax.ShapeDtypeStruct((rows, 16 * width), jnp.bfloat16),
        [SMEM] + [VMEM] * len(pieces) + ([] if first else [HBM]),
        HBM,
        [pltpu.SemaphoreType.DMA((len(slots),))],
        6,
        input_output_aliases={} if first else {len(pieces) + 1: 0},
    )(me, *pieces, *([] if first else [relaid]))


def body(
    tokens,
    norm_gain,
    query_weight,
    keyval_weight,
    out_weight,
    key_cache,
    value_cache,
    lengths,
    next_query,
):
    heads = query_weight.shape[1] // HD
    features = query_weight.shape[0] * lax.axis_size("row")
    me = jnp.stack([lax.axis_index("row"), lax.axis_index("col")]).astype(jnp.int32)
    cosine, sine = rotary_factors(lengths, HD)
    chunks = next_query.reshape(16, -1, next_query.shape[1])

    def pair(dy, dx):
        return [(dy, dx, 0), (dy, dx, 1)]

    to_a, to_b = stage(me, chunks, [pair(1, 0), pair(3, 0)])
    got_a, got_b = shift_y(to_a, 1), shift_y(to_b, 3)
    own, to_own, to_c, to_d, to_e, to_f, to_g = stage(
        me,
        chunks,
        [[(0, 0, 0)], [(0, 0, 1)], pair(2, 0), pair(0, 1), pair(1, 1), pair(3, 1), pair(2, 1)],
    )
    got_own = flip(to_own, "row", CORE)

    feats = tokens[None]
    other = flip(feats, "col", X_LOW)
    other, to_e, cosine, sine, to_c, to_d, to_f, to_g = tie(
        other, to_e, cosine, sine, to_c, to_d, to_f, to_g
    )
    via_e = flip(to_e, "row", X_HALF)
    feats = join(feats, other)
    other = flip(feats, "col", Z_NEAR)
    other, got_own = tie(other, got_own)
    feats = join(feats, other)
    other = flip(feats, "col", Z_FAR)
    got_c = shift_y(to_c, 2)
    kept, sent = project(me, feats, other, norm_gain, query_weight, keyval_weight)
    got_a, got_b, sent = tie(got_a, got_b, sent)
    got = flip(sent, "row", CORE)
    got, via_e = tie(got, via_e)
    kept, sent = add_halves(kept, got, 5)
    got = flip(sent, "row", X_HALF)
    via_f, via_g = flip(to_f, "row", X_HALF), flip(to_g, "row", X_HALF)
    got, got_c = tie(got, got_c)
    swap_first = flip(pack([got_a, got_b, got_c], [(k, 1) for k in range(3)]), "row", CORE)
    kept, sent = add_halves(kept, got, 10)
    got = flip(sent, "row", Y_FAR)
    kept, sent = add_halves(kept, got)
    got = flip(sent, "row", Y_NEAR)
    attended = attend(
        lengths, kept, got, cosine, sine, key_cache, value_cache, features, heads
    )
    other = flip(attended, "row", Y_NEAR)
    other, via_f = tie(other, via_f)
    attended = join(attended, other)
    other = flip(attended, "row", Y_FAR)
    got_e, got_f = shift_y(via_e, 1), shift_y(via_f, 3)
    via_g, swap_first, other = tie(via_g, swap_first, other)
    swap_g = flip(pack([via_g], [(0, 1)]), "row", CORE)
    attended = join(attended, other, 4.5)
    other = flip(attended, "row", X_HALF)
    got_d = flip(to_d, "row", X_HALF)
    attended = join(attended, other, 2.4)
    other = flip(attended, "row", CORE)
    relaid = place(
        me,
        [own, got_own, got_a, got_b, got_c, swap_first],
        [(0, 0, 0, 0, 0), (1, 0, 0, 0, 1)]
        + [(k + 2, 0, dy, 0, 0) for k, dy in enumerate((1, 3, 2))]
        + [(5, k, dy, 0, 1) for k, dy in enumerate((1, 3, 2))],
        None,
    )
    kept, sent = mix(me, attended, other, out_weight)
    via_g = pack([via_g, swap_g], [(0, 0), (1, 0)])
    got = flip(sent, "col", Z_FAR)
    got_g = shift_y(via_g, 2)
    got, got_e, got_f, relaid = tie(got, got_e, got_f, relaid)
    kept, sent = add_halves(kept, got, 3.2)
    got = flip(sent, "col", Z_NEAR)
    got, got_d = tie(got, got_d)
    swap_last = flip(pack([got_d, got_e, got_f], [(k, 1) for k in range(3)]), "row", CORE)
    kept, sent = add_halves(kept, got, 3.2)
    got = flip(sent, "col", X_LOW)
    mixed = (kept + got)[0].astype(jnp.bfloat16)
    relaid = place(
        me,
        [got_d, got_e, got_f, swap_last],
        [(k, 0, dy, 1, 0) for k, dy in enumerate((0, 1, 3))]
        + [(3, k, dy, 1, 1) for k, dy in enumerate((0, 1, 3))],
        relaid,
    )
    relaid = place(me, [got_g], [(0, 0, 2, 1, 0), (0, 1, 2, 1, 1)], relaid)
    return (mixed, relaid)


def solution(mesh):
    in_specs = (
        P(None, ("row", "col")),
        P("row"),
        P("row", "col"),
        P("row", "col"),
        P("col", "row"),
        P("row", None, "col"),
        P("row", None, "col"),
        P("row"),
        P(None, ("col", "row")),
    )
    out_specs = (P(None, ("row", "col")), P("row", "col"))
    return jax.shard_map(body, mesh=mesh, in_specs=in_specs, out_specs=out_specs, check_vma=False)
```

time: 519 us -> 103 us (0.20)
  waiting for transfers between devices: 446 us -> 44.7 us
  starting transfers between devices: 7.43 us -> 35.2 us
  blocking collectives: 19.6 us -> 0 us
  Pallas kernels: 0 us -> 17.5 us
  between operations: 14.6 us -> 0.97 us
  matrix products: 11.4 us -> 0 us
  local copies, waits for them, and re-layouts: 13.6 us -> 2.37 us
    all_gather x1 -> x0, waiting for transfers between devices: 275 us -> none  [body(): everything = lax.all_gather(tokens, ('row', 'col'), axis=1, tiled=True)]
    unnamed x4 -> x0, waiting for transfers between devices: 133 us -> none
    ppermute x0 -> x28, waiting for transfers between devices: none -> 44.7 us  [the longest x22 25.9 us: flip(): return lax.ppermute(block, axis, [(i, i ^ bits) for i in range(size)])]
    reduce_scatter x1 -> x0, waiting for transfers between devices: 37.3 us -> none  [body(): lax.psum_scatter(partial_out, 'col', scatter_dimension=1, tiled=True)]
    ppermute x0 -> x28, starting transfers between devices: none -> 35.2 us  [the longest x22 26.5 us: flip(): return lax.ppermute(block, axis, [(i, i ^ bits) for i in range(size)])]
    all_gather x1 -> x0, blocking collectives: 19.6 us -> none  [body(): lax.all_gather(attended, 'row', axis=0, tiled=True)]
    pallas_call x0 -> x22, Pallas kernels: none -> 17.5 us  [the longest x2 6.29 us: stage(): call(functools.partial(stage_kernel, groups), [like(chunks, len(group)) f...]
    dot_general x6 -> x0, matrix products: 11.4 us -> none  [the longest x1 3.67 us: body(): jnp.dot(lax.all_gather(attended, 'row', axis=0, tiled=True), out_weight,...]
  transfers between devices with their start and end apart: 4 -> 28, of which waited for: 3 -> 13; matrix products, arithmetic and copies ran while one was open for 3% -> 1% of each run, Pallas kernels for 0% -> 16%
where the time goes in v1:
time: 103 us; the launch traced here: 102 us
  waiting for transfers between devices  44.7 us (43%)
  starting transfers between devices  35.2 us (34%)
  Pallas kernels  17.5 us (17%)
  local copies, waits for them, and re-layouts  2.37 us (2%)
  other arithmetic  1.45 us (1%)
    ppermute x22, starting transfers between devices, flip(): return lax.ppermute(block, axis, [(i, i ^ bits) for i in range(size)])  26.5 us
    ppermute x22, waiting for transfers between devices, flip(): return lax.ppermute(block, axis, [(i, i ^ bits) for i in range(size)])  25.9 us
    ppermute x6, waiting for transfers between devices, shift_y(): lax.ppermute(block, 'row', [(i, (i + 4 * steps) % size) for i in range(si...  18.8 us
    ppermute x6, starting transfers between devices, shift_y(): lax.ppermute(block, 'row', [(i, (i + 4 * steps) % size) for i in range(si...  8.72 us
    pallas_call x2, Pallas kernels, stage(): call(functools.partial(stage_kernel, groups), [like(chunks, len(group)) f...  6.29 us
    pallas_call x3, Pallas kernels, place(): call(functools.partial(place_kernel, len(pieces), slots), jax.ShapeDtypeS...  5.01 us
    pallas_call x1, Pallas kernels, attend(): call(functools.partial(attend_kernel, features), jax.ShapeDtypeStruct((ro...  2.87 us
    unnamed x28, local copies, waits for them, and re-layouts  2.37 us
  transfers between devices with their start and end apart: 28, of which 13 were waited for; matrix products, arithmetic and copies ran while one was open for 1% of the time, Pallas kernels for 16%

profile of v1, /device:TPU:0, one launch (start us, length us, event | category | flops | bytes accessed | tf_op | source)
XLA Modules:
  0.0 102.3 jit_solution(13782636478889846559)
XLA Ops:
  0.6 1.7 %collective-permute-start = (bf16[1,32,128]{2,1,0:T(8,128)(2,1)}, bf16[1,32,128]{2,1,0:T(8,128)(2,1)S(1)}, u32[]{:S(2)}, u32[]{:S(2)}) collective-permute-start(bf16[1,32,128]{2,1,0:T(8,128)(2,1)} %bitcast.6), channel_id=1, source_target_pairs={{0,4},{1,5},{2,6},{3,7},{4,0},{5,1},{6,2},{7,3},{8,12},{9,13},{10,... | collective-permute-start | bytes 24584 | tf_op jit(solution)/shard_map/ppermute | solution.py:57
  3.0 2.8 %shard_map.108 = (bf16[2,1024,128]{2,1,0:T(8,128)(2,1)}, bf16[2,1024,128]{2,1,0:T(8,128)(2,1)}) custom-call(s32[2]{0:T(128)} %pad_add_fusion.me_ref, bf16[16,1024,128]{2,1,0:T(8,128)(2,1)} %bitcast.8), custom_call_target="tpu_custom_call" | custom-call | flops 1 | bytes 1 | tf_op jit(solution)/shard_map/pallas_call | solution.py:314
  5.8 1.6 %collective-permute-start.4 = (bf16[2,1024,128]{2,1,0:T(8,128)(2,1)}, bf16[2,1024,128]{2,1,0:T(8,128)(2,1)S(1)}, u32[]{:S(2)}, u32[]{:S(2)}) collective-permute-start(bf16[2,1024,128]{2,1,0:T(8,128)(2,1)} %get-tuple-element.62), channel_id=1, source_target_pairs={{0,32},{8,40},{16,48},{24,56},{32,64},{40,72},{48,80},{56,88},{64,... | collective-permute-start | bytes 1572872 | tf_op jit(solution)/shard_map/ppermute | solution.py:62
  7.4 1.7 %collective-permute-start.5 = (bf16[2,1024,128]{2,1,0:T(8,128)(2,1)}, bf16[2,1024,128]{2,1,0:T(8,128)(2,1)S(1)}, u32[]{:S(2)}, u32[]{:S(2)}) collective-permute-start(bf16[2,1024,128]{2,1,0:T(8,128)(2,1)} %get-tuple-element.63), channel_id=1, source_target_pairs={{0,96},{8,104},{16,112},{24,120},{32,0},{40,8},{48,16},{56,24},{64... | collective-permute-start | bytes 1572872 | tf_op jit(solution)/shard_map/ppermute | solution.py:62
  9.1 3.5 %shard_map.104 = (bf16[1,1024,128]{2,1,0:T(8,128)(2,1)}, bf16[1,1024,128]{2,1,0:T(8,128)(2,1)}, bf16[2,1024,128]{2,1,0:T(8,128)(2,1)}, bf16[2,1024,128]{2,1,0:T(...) custom-call(s32[2]{0:T(128)} %pad_add_fusion.me_ref, ...), custom_call_target="tpu_custom_call" | custom-call | flops 1 | bytes 1 | tf_op jit(solution)/shard_map/pallas_call | solution.py:314
  12.9 2.8 %collective-permute-start.7 = (bf16[2,1024,128]{2,1,0:T(8,128)(2,1)}, bf16[2,1024,128]{2,1,0:T(8,128)(2,1)S(1)}, u32[]{:S(2)}, u32[]{:S(2)}) collective-permute-start(bf16[2,1024,128]{2,1,0:T(8,128)(2,1)} %get-tuple-element.66), channel_id=1, source_target_pairs={{0,16},{8,24},{16,0},{24,8},{32,48},{40,56},{48,32},{56,40},{64,80... | collective-permute-start | bytes 1572872 | tf_op jit(solution)/shard_map/ppermute | solution.py:57
  15.7 1.9 %collective-permute-start.1 = (bf16[2,32,128]{2,1,0:T(8,128)(2,1)S(1)}, bf16[2,32,128]{2,1,0:T(8,128)(2,1)S(1)}, u32[]{:S(2)}, u32[]{:S(2)}) collective-permute-start(bf16[2,32,128]{2,1,0:T(8,128)(2,1)S(1)} %shard_map.105.own_ref), channel_id=1, source_target_pairs={{0,1},{1,0},{2,3},{3,2},{4,5},{5,4},{6,7},{7,6},{8,9},{9,8},{10,11... | collective-permute-start | bytes 49160 | tf_op jit(solution)/shard_map/ppermute | solution.py:57
  17.6 1.8 %collective-permute-done.1.other_ref = bf16[2,32,128]{2,1,0:T(8,128)(2,1)S(1)} collective-permute-done((bf16[2,32,128]{2,1,0:T(8,128)(2,1)S(1)}, bf16[2,32,128]{2,1,0:T(8,128)(2,1)S(1)}, u32[]{:S(2)}, u32[]{:S(2)}) %collective-permute-start.1) | collective-permute-done | bytes 16416 | tf_op jit(solution)/shard_map/ppermute | solution.py:57
  19.4 4.0 %collective-permute-start.3 = (bf16[4,32,128]{2,1,0:T(8,128)(2,1)S(1)}, bf16[4,32,128]{2,1,0:T(8,128)(2,1)S(1)}, u32[]{:S(2)}, u32[]{:S(2)}) collective-permute-start(bf16[4,32,128]{2,1,0:T(8,128)(2,1)S(1)} %shard_map.106.near_ref), channel_id=1, source_target_pairs={{0,3},{1,2},{2,1},{3,0},{4,7},{5,6},{6,5},{7,4},{8,11},{9,10},{10,... | collective-permute-start | bytes 98312 | tf_op jit(solution)/shard_map/ppermute | solution.py:57
  23.4 1.9 %collective-permute-done.3.far_ref = bf16[4,32,128]{2,1,0:T(8,128)(2,1)S(1)} collective-permute-done((bf16[4,32,128]{2,1,0:T(8,128)(2,1)S(1)}, bf16[4,32,128]{2,1,0:T(8,128)(2,1)S(1)}, u32[]{:S(2)}, u32[]{:S(2)}) %collective-permute-start.3) | collective-permute-done | bytes 32800 | tf_op jit(solution)/shard_map/ppermute | solution.py:57
  25.3 2.2 %copy-done.7 = bf16[1024,2048]{1,0:T(8,128)(2,1)S(1)} copy-done((bf16[1024,2048]{1,0:T(8,128)(2,1)S(1)}, bf16[1024,2048]{1,0:T(8,128)(2,1)}, u32[]{:S(2)}) %copy-start.7) | copy-done | bytes 4194328
  27.5 1.4 %shard_map.107 = (f32[16,2432]{1,0:T(8,128)S(1)}, f32[16,2432]{1,0:T(8,128)S(1)}) custom-call(s32[2]{0:T(128)S(1)} %copy-done.4, bf16[4,32,128]{2,1,0:T(8,128)(2,1)S(1)} %shard_map.106.near_ref, bf16[4,32,128]{2,1,0:T(8,128)(2,1)S(1)} %collective-permute-done.3.far_ref, bf16[1,1024]{1,0:T(2,128)(2,1)S(1)} %broadcast_in_dim.9.gain_ref, ...), custom_call_target="tpu_custom_call" | custom-call | flops 2500000000 | bytes 1 | tf_op jit(solution)/shard_map/pallas_call | solution.py:152
  29.1 2.1 %collective-permute-start.9 = (bf16[2,1024,128]{2,1,0:T(8,128)(2,1)S(1)}, bf16[2,1024,128]{2,1,0:T(8,128)(2,1)S(1)}, u32[]{:S(2)}, u32[]{:S(2)}) collective-permute-start(bf16[2,1024,128]{2,1,0:T(8,128)(2,1)S(1)} %copy-done.13), channel_id=1, source_target_pairs={{0,64},{8,72},{16,80},{24,88},{32,96},{40,104},{48,112},{56,120},{... | collective-permute-start | bytes 1572872 | tf_op jit(solution)/shard_map/ppermute | solution.py:62
  32.2 2.6 %collective-permute-start.13 = (bf16[2,1024,128]{2,1,0:T(8,128)(2,1)S(1)}, bf16[2,1024,128]{2,1,0:T(8,128)(2,1)S(1)}, u32[]{:S(2)}, u32[]{:S(2)}) collective-permute-start(bf16[2,1024,128]{2,1,0:T(8,128)(2,1)S(1)} %copy-done.12), channel_id=1, source_target_pairs={{0,16},{8,24},{16,0},{24,8},{32,48},{40,56},{48,32},{56,40},{64,80... | collective-permute-start | bytes 1572872 | tf_op jit(solution)/shard_map/ppermute | solution.py:57
  35.7 9.2 %collective-permute-done.9.refs_2_.refs_4_ = bf16[2,1024,128]{2,1,0:T(8,128)(2,1)S(1)} collective-permute-done((bf16[2,1024,128]{2,1,0:T(8,128)(2,1)S(1)}, bf16[2,1024,128]{2,1,0:T(8,128)(2,1)S(1)}, u32[]{:S(2)}, u32[]{:S(2)}) %collective-permute-start.9) | collective-permute-done | bytes 524320 | tf_op jit(solution)/shard_map/ppermute | solution.py:62
  45.2 1.9 %collective-permute-start.10 = (f32[4,2432]{1,0:T(4,128)S(1)}, f32[4,2432]{1,0:T(4,128)S(1)}, u32[]{:S(2)}, u32[]{:S(2)}) collective-permute-start(f32[4,2432]{1,0:T(4,128)S(1)} %get-tuple-element.73), channel_id=1, source_target_pairs={{0,96},{8,104},{16,112},{24,120},{32,64},{40,72},{48,80},{56,88},{... | collective-permute-start | bytes 116744 | tf_op jit(solution)/shard_map/ppermute | solution.py:57
  47.1 3.4 %collective-permute-done.10.got_ref = f32[4,2432]{1,0:T(4,128)S(1)} collective-permute-done((f32[4,2432]{1,0:T(4,128)S(1)}, f32[4,2432]{1,0:T(4,128)S(1)}, u32[]{:S(2)}, u32[]{:S(2)}) %collective-permute-start.10) | collective-permute-done | bytes 38944 | tf_op jit(solution)/shard_map/ppermute | solution.py:57
  50.6 3.8 %collective-permute-done.11.got_ref = f32[2,2432]{1,0:T(2,128)S(1)} collective-permute-done((f32[2,2432]{1,0:T(2,128)S(1)}, f32[2,2432]{1,0:T(2,128)S(1)}, u32[]{:S(2)}, u32[]{:S(2)}) %collective-permute-start.11) | collective-permute-done | bytes 19488 | tf_op jit(solution)/shard_map/ppermute | solution.py:57
  54.3 2.9 %shard_map.112.own_ref = bf16[2,2048]{1,0:T(2,128)(2,1)S(1)} custom-call(s32[2]{0:T(128)S(1)} %copy-done.6, f32[2,2432]{1,0:T(2,128)S(1)} %get-tuple-element.74.kept_ref, f32[2,2432]{1,0:T(2,128)S(1)} %collective-permute-done.11.got_ref, f32[2,128]{1,0:T(2,128)S(1)} %get-tuple-element.76.cos_ref, f32[2,128]{1,0:T(2,128)S(1)} %get-tuple-element.77.sin_ref, ...), custom_call_target="tpu_custom_call" | custom-call | flops 1 | bytes 1 | tf_op jit(solution)/shard_map/pallas_call | solution.py:230
  57.3 3.6 %collective-permute-done.12.other_ref = bf16[2,2048]{1,0:T(2,128)(2,1)S(1)} collective-permute-done((bf16[2,2048]{1,0:T(2,128)(2,1)S(1)}, bf16[2,2048]{1,0:T(2,128)(2,1)S(1)}, u32[]{:S(2)}, u32[]{:S(2)}) %collective-permute-start.12) | collective-permute-done | bytes 8224 | tf_op jit(solution)/shard_map/ppermute | solution.py:57
  61.0 1.9 %collective-permute-start.16 = (bf16[4,2048]{1,0:T(4,128)(2,1)S(1)}, bf16[4,2048]{1,0:T(4,128)(2,1)S(1)}, u32[]{:S(2)}, u32[]{:S(2)}) collective-permute-start(bf16[4,2048]{1,0:T(4,128)(2,1)S(1)} %shard_map.113.own_ref), channel_id=1, source_target_pairs={{0,96},{8,104},{16,112},{24,120},{32,64},{40,72},{48,80},{56,88},{... | collective-permute-start | bytes 49160 | tf_op jit(solution)/shard_map/ppermute | solution.py:57
  62.8 3.2 %collective-permute-start.21 = (bf16[2,1024,128]{2,1,0:T(8,128)(2,1)S(1)}, bf16[2,1024,128]{2,1,0:T(8,128)(2,1)S(1)}, u32[]{:S(2)}, u32[]{:S(2)}) collective-permute-start(bf16[2,1024,128]{2,1,0:T(8,128)(2,1)S(1)} %collective-permute-done.13), channel_id=1, source_target_pairs={{0,96},{8,104},{16,112},{24,120},{32,0},{40,8},{48,16},{56,24},{64... | collective-permute-start | bytes 1572872 | tf_op jit(solution)/shard_map/ppermute | solution.py:62
  67.1 2.7 %collective-permute-start.23 = (bf16[2,1024,128]{2,1,0:T(8,128)(2,1)S(1)}, bf16[2,1024,128]{2,1,0:T(8,128)(2,1)S(1)}, u32[]{:S(2)}, u32[]{:S(2)}) collective-permute-start(bf16[2,1024,128]{2,1,0:T(8,128)(2,1)S(1)} %copy-done.10), channel_id=1, source_target_pairs={{0,16},{8,24},{16,0},{24,8},{32,48},{40,56},{48,32},{56,40},{64,80... | collective-permute-start | bytes 1572872 | tf_op jit(solution)/shard_map/ppermute | solution.py:57
  69.9 2.3 %collective-permute-done.17.other_ref = bf16[8,2048]{1,0:T(8,128)(2,1)S(1)} collective-permute-done((bf16[8,2048]{1,0:T(8,128)(2,1)S(1)}, bf16[8,2048]{1,0:T(8,128)(2,1)S(1)}, u32[]{:S(2)}, u32[]{:S(2)}) %collective-permute-start.17) | collective-permute-done | bytes 32800 | tf_op jit(solution)/shard_map/ppermute | solution.py:57
  73.5 1.5 %shard_map.117 = (f32[4,32,128]{2,1,0:T(8,128)S(1)}, f32[4,32,128]{2,1,0:T(8,128)S(1)}) custom-call(s32[2]{0:T(128)S(1)} %copy-done.4, bf16[16,2048]{1,0:T(8,128)(2,1)S(1)} %shard_map.116.own_ref, bf16[16,2048]{1,0:T(8,128)(2,1)S(1)} %collective-permute-done.18.other_ref, bf16[2048,1024]{1,0:T(8,128)(2,1)S(1)} %copy-done.2), custom_call_target="tpu_custom_call" | custom-call | flops 1 | bytes 1 | tf_op jit(solution)/shard_map/pallas_call | solution.py:272
  75.0 3.3 %collective-permute-start.19 = (f32[4,32,128]{2,1,0:T(8,128)S(1)}, f32[4,32,128]{2,1,0:T(8,128)S(1)}, u32[]{:S(2)}, u32[]{:S(2)}) collective-permute-start(f32[4,32,128]{2,1,0:T(8,128)S(1)} %get-tuple-element.86), channel_id=1, source_target_pairs={{0,3},{1,2},{2,1},{3,0},{4,7},{5,6},{6,5},{7,4},{8,11},{9,10},{10,... | collective-permute-start | bytes 196616 | tf_op jit(solution)/shard_map/ppermute | solution.py:57
  78.3 1.9 %shard_map.118.refs_4_ = bf16[1024,2048]{1,0:T(8,128)(2,1)} custom-call(s32[2]{0:T(128)S(1)} %copy-done.4, bf16[1,1024,128]{2,1,0:T(8,128)(2,1)S(1)} %copy-done.3, bf16[1,1024,128]{2,1,0:T(8,128)(2,1)S(1)} %collective-permute-done.2.refs_1_, bf16[2,1024,128]{2,1,0:T(8,128)(2,1)S(1)} %collective-permute-done.4.refs_0_.refs_2_, ...), custom_call_target="tpu_custom_call" | custom-call | flops 1 | bytes 1 | tf_op jit(solution)/shard_map/pallas_call | solution.py:367
  81.0 3.8 %collective-permute-done.22.got_ref = f32[2,32,128]{2,1,0:T(8,128)S(1)} collective-permute-done((f32[2,32,128]{2,1,0:T(8,128)S(1)}, f32[2,32,128]{2,1,0:T(8,128)S(1)}, u32[]{:S(2)}, u32[]{:S(2)}) %collective-permute-start.22) | collective-permute-done | bytes 32800 | tf_op jit(solution)/shard_map/ppermute | solution.py:57
  85.4 3.5 %collective-permute-done.24 = f32[1,32,128]{2,1,0:T(8,128)S(1)} collective-permute-done((f32[1,32,128]{2,1,0:T(8,128)S(1)}, f32[1,32,128]{2,1,0:T(8,128)S(1)}, u32[]{:S(2)}, u32[]{:S(2)}) %collective-permute-start.24) | collective-permute-done | bytes 16416 | tf_op jit(solution)/shard_map/ppermute | solution.py:57
  89.5 1.7 %shard_map.124.refs_1_ = bf16[1024,2048]{1,0:T(8,128)(2,1)} custom-call(s32[2]{0:T(128)S(1)} %copy-done.4, bf16[2,1024,128]{2,1,0:T(8,128)(2,1)S(1)} %collective-permute-done.23.refs_0_, bf16[2,1024,128]{2,1,0:T(8,128)(2,1)S(1)} %collective-permute-done.20.refs_1_, ...), custom_call_target="tpu_custom_call", output_to_operand_aliasing={{}: (5, {})} | custom-call | flops 1 | bytes 1 | tf_op jit(solution)/shard_map/pallas_call | solution.py:367
  91.3 9.6 %collective-permute-done.26.refs_0_ = bf16[2,1024,128]{2,1,0:T(8,128)(2,1)S(1)} collective-permute-done((bf16[2,1024,128]{2,1,0:T(8,128)(2,1)S(1)}, bf16[2,1024,128]{2,1,0:T(8,128)(2,1)S(1)}, u32[]{:S(2)}, u32[]{:S(2)}) %collective-permute-start.26) | collective-permute-done | bytes 524320 | tf_op jit(solution)/shard_map/ppermute | solution.py:62
  100.9 1.4 %shard_map.125 = bf16[1024,2048]{1,0:T(8,128)(2,1)} custom-call(s32[2]{0:T(128)S(1)} %copy-done.4, bf16[2,1024,128]{2,1,0:T(8,128)(2,1)S(1)} %collective-permute-done.26.refs_0_, bf16[1024,2048]{1,0:T(8,128)(2,1)} %shard_map.124.refs_1_), custom_call_target="tpu_custom_call", output_to_operand_aliasing={{}: (2, {})} | custom-call | flops 1 | bytes 1 | tf_op jit(solution)/shard_map/pallas_call | solution.py:367
  (81 shorter events, 7.8 us)
Async XLA Ops:
  0.6 12.3 %collective-permute-start = (bf16[1,32,128]{2,1,0:T(8,128)(2,1)}, bf16[1,32,128]{2,1,0:T(8,128)(2,1)S(1)}, u32[]{:S(2)}, u32[]{:S(2)}) collective-permute-start(bf16[1,32,128]{2,1,0:T(8,128)(2,1)} %bitcast.6), channel_id=1, source_target_pairs={{0,4},{1,5},{2,6},{3,7},{4,0},{5,1},{6,2},{7,3},{8,12},{9,13},{10,... | collective-permute-start | bytes 24584 | tf_op jit(solution)/shard_map/ppermute | solution.py:57
  2.9 12.7 %copy-start.5 = (bf16[32,128]{1,0:T(8,128)(2,1)S(1)}, bf16[32,128]{1,0:T(8,128)(2,1)}, u32[]{:S(2)}) copy-start(bf16[32,128]{1,0:T(8,128)(2,1)} %param.9) | copy-start | bytes 24580
  2.9 20.5 %copy-start.9 = (bf16[1024]{0:T(1024)(128)(2,1)S(1)}, bf16[1024]{0:T(1024)(128)(2,1)}, u32[]{:S(2)}) copy-start(bf16[1024]{0:T(1024)(128)(2,1)} %param.10) | copy-start | bytes 6148
  2.9 22.4 %copy-start.4 = (s32[2]{0:T(128)S(1)}, s32[2]{0:T(128)}, u32[]{:S(2)}) copy-start(s32[2]{0:T(128)} %pad_add_fusion.me_ref) | copy-start | bytes 28
  2.9 22.4 %copy-start.8 = (bf16[1024,256]{1,0:T(8,128)(2,1)S(1)}, bf16[1024,256]{1,0:T(8,128)(2,1)}, u32[]{:S(2)}) copy-start(bf16[1024,256]{1,0:T(8,128)(2,1)} %keyval_ref.1) | copy-start | bytes 1572868
  5.8 23.2 %collective-permute-start.4 = (bf16[2,1024,128]{2,1,0:T(8,128)(2,1)}, bf16[2,1024,128]{2,1,0:T(8,128)(2,1)S(1)}, u32[]{:S(2)}, u32[]{:S(2)}) collective-permute-start(bf16[2,1024,128]{2,1,0:T(8,128)(2,1)} %get-tuple-element.62), channel_id=1, source_target_pairs={{0,32},{8,40},{16,48},{24,56},{32,64},{40,72},{48,80},{56,88},{64,... | collective-permute-start | bytes 1572872 | tf_op jit(solution)/shard_map/ppermute | solution.py:62
  7.4 21.6 %collective-permute-start.5 = (bf16[2,1024,128]{2,1,0:T(8,128)(2,1)}, bf16[2,1024,128]{2,1,0:T(8,128)(2,1)S(1)}, u32[]{:S(2)}, u32[]{:S(2)}) collective-permute-start(bf16[2,1024,128]{2,1,0:T(8,128)(2,1)} %get-tuple-element.63), channel_id=1, source_target_pairs={{0,96},{8,104},{16,112},{24,120},{32,0},{40,8},{48,16},{56,24},{64... | collective-permute-start | bytes 1572872 | tf_op jit(solution)/shard_map/ppermute | solution.py:62
  12.6 6.8 %collective-permute-start.2 = (bf16[1,1024,128]{2,1,0:T(8,128)(2,1)}, bf16[1,1024,128]{2,1,0:T(8,128)(2,1)S(1)}, u32[]{:S(2)}, u32[]{:S(2)}) collective-permute-start(bf16[1,1024,128]{2,1,0:T(8,128)(2,1)} %get-tuple-element.59), channel_id=1, source_target_pairs={{0,8},{8,0},{16,24},{24,16},{32,40},{40,32},{48,56},{56,48},{64,72... | collective-permute-start | bytes 786440 | tf_op jit(solution)/shard_map/ppermute | solution.py:57
  12.9 18.3 %collective-permute-start.7 = (bf16[2,1024,128]{2,1,0:T(8,128)(2,1)}, bf16[2,1024,128]{2,1,0:T(8,128)(2,1)S(1)}, u32[]{:S(2)}, u32[]{:S(2)}) collective-permute-start(bf16[2,1024,128]{2,1,0:T(8,128)(2,1)} %get-tuple-element.66), channel_id=1, source_target_pairs={{0,16},{8,24},{16,0},{24,8},{32,48},{40,56},{48,32},{56,40},{64,80... | collective-permute-start | bytes 1572872 | tf_op jit(solution)/shard_map/ppermute | solution.py:57
  15.7 3.7 %collective-permute-start.1 = (bf16[2,32,128]{2,1,0:T(8,128)(2,1)S(1)}, bf16[2,32,128]{2,1,0:T(8,128)(2,1)S(1)}, u32[]{:S(2)}, u32[]{:S(2)}) collective-permute-start(bf16[2,32,128]{2,1,0:T(8,128)(2,1)S(1)} %shard_map.105.own_ref), channel_id=1, source_target_pairs={{0,1},{1,0},{2,3},{3,2},{4,5},{5,4},{6,7},{7,6},{8,9},{9,8},{10,11... | collective-permute-start | bytes 49160 | tf_op jit(solution)/shard_map/ppermute | solution.py:57
  19.4 5.9 %collective-permute-start.3 = (bf16[4,32,128]{2,1,0:T(8,128)(2,1)S(1)}, bf16[4,32,128]{2,1,0:T(8,128)(2,1)S(1)}, u32[]{:S(2)}, u32[]{:S(2)}) collective-permute-start(bf16[4,32,128]{2,1,0:T(8,128)(2,1)S(1)} %shard_map.106.near_ref), channel_id=1, source_target_pairs={{0,3},{1,2},{2,1},{3,0},{4,7},{5,6},{6,5},{7,4},{8,11},{9,10},{10,... | collective-permute-start | bytes 98312 | tf_op jit(solution)/shard_map/ppermute | solution.py:57
  29.0 2.2 %collective-permute-start.6 = (f32[16,2432]{1,0:T(8,128)S(1)}, f32[16,2432]{1,0:T(8,128)S(1)}, u32[]{:S(2)}, u32[]{:S(2)}) collective-permute-start(f32[16,2432]{1,0:T(8,128)S(1)} %get-tuple-element.65), channel_id=1, source_target_pairs={{0,8},{8,0},{16,24},{24,16},{32,40},{40,32},{48,56},{56,48},{64,72... | collective-permute-start | bytes 466952 | tf_op jit(solution)/shard_map/ppermute | solution.py:57
  29.1 15.8 %collective-permute-start.9 = (bf16[2,1024,128]{2,1,0:T(8,128)(2,1)S(1)}, bf16[2,1024,128]{2,1,0:T(8,128)(2,1)S(1)}, u32[]{:S(2)}, u32[]{:S(2)}) collective-permute-start(bf16[2,1024,128]{2,1,0:T(8,128)(2,1)S(1)} %copy-done.13), channel_id=1, source_target_pairs={{0,64},{8,72},{16,80},{24,88},{32,96},{40,104},{48,112},{56,120},{... | collective-permute-start | bytes 1572872 | tf_op jit(solution)/shard_map/ppermute | solution.py:62
  31.2 13.7 %collective-permute-start.8 = (f32[8,2432]{1,0:T(8,128)S(1)}, f32[8,2432]{1,0:T(8,128)S(1)}, u32[]{:S(2)}, u32[]{:S(2)}) collective-permute-start(f32[8,2432]{1,0:T(8,128)S(1)} %get-tuple-element.69), channel_id=1, source_target_pairs={{0,16},{8,24},{16,0},{24,8},{32,48},{40,56},{48,32},{56,40},{64,80... | collective-permute-start | bytes 233480 | tf_op jit(solution)/shard_map/ppermute | solution.py:57
  32.2 25.1 %collective-permute-start.13 = (bf16[2,1024,128]{2,1,0:T(8,128)(2,1)S(1)}, bf16[2,1024,128]{2,1,0:T(8,128)(2,1)S(1)}, u32[]{:S(2)}, u32[]{:S(2)}) collective-permute-start(bf16[2,1024,128]{2,1,0:T(8,128)(2,1)S(1)} %copy-done.12), channel_id=1, source_target_pairs={{0,16},{8,24},{16,0},{24,8},{32,48},{40,56},{48,32},{56,40},{64,80... | collective-permute-start | bytes 1572872 | tf_op jit(solution)/shard_map/ppermute | solution.py:57
  34.8 31.2 %collective-permute-start.14 = (bf16[2,1024,128]{2,1,0:T(8,128)(2,1)S(1)}, bf16[2,1024,128]{2,1,0:T(8,128)(2,1)S(1)}, u32[]{:S(2)}, u32[]{:S(2)}) collective-permute-start(bf16[2,1024,128]{2,1,0:T(8,128)(2,1)S(1)} %copy-done.11), channel_id=1, source_target_pairs={{0,16},{8,24},{16,0},{24,8},{32,48},{40,56},{48,32},{56,40},{64,80... | collective-permute-start | bytes 1572872 | tf_op jit(solution)/shard_map/ppermute | solution.py:57
  45.0 21.2 %collective-permute-start.15 = (bf16[3,1024,128]{2,1,0:T(8,128)(2,1)S(1)}, bf16[3,1024,128]{2,1,0:T(8,128)(2,1)S(1)}, u32[]{:S(2)}, u32[]{:S(2)}) collective-permute-start(bf16[3,1024,128]{2,1,0:T(8,128)(2,1)S(1)} %shard_map.114), channel_id=1, source_target_pairs={{0,8},{8,0},{16,24},{24,16},{32,40},{40,32},{48,56},{56,48},{64,72... | collective-permute-start | bytes 2359304 | tf_op jit(solution)/shard_map/ppermute | solution.py:57
  45.2 5.3 %collective-permute-start.10 = (f32[4,2432]{1,0:T(4,128)S(1)}, f32[4,2432]{1,0:T(4,128)S(1)}, u32[]{:S(2)}, u32[]{:S(2)}) collective-permute-start(f32[4,2432]{1,0:T(4,128)S(1)} %get-tuple-element.73), channel_id=1, source_target_pairs={{0,96},{8,104},{16,112},{24,120},{32,64},{40,72},{48,80},{56,88},{... | collective-permute-start | bytes 116744 | tf_op jit(solution)/shard_map/ppermute | solution.py:57
  50.5 3.9 %collective-permute-start.11 = (f32[2,2432]{1,0:T(2,128)S(1)}, f32[2,2432]{1,0:T(2,128)S(1)}, u32[]{:S(2)}, u32[]{:S(2)}) collective-permute-start(f32[2,2432]{1,0:T(2,128)S(1)} %get-tuple-element.75), channel_id=1, source_target_pairs={{0,32},{8,40},{16,48},{24,56},{32,0},{40,8},{48,16},{56,24},{64,96... | collective-permute-start | bytes 58376 | tf_op jit(solution)/shard_map/ppermute | solution.py:57
  57.2 3.7 %collective-permute-start.12 = (bf16[2,2048]{1,0:T(2,128)(2,1)S(1)}, bf16[2,2048]{1,0:T(2,128)(2,1)S(1)}, u32[]{:S(2)}, u32[]{:S(2)}) collective-permute-start(bf16[2,2048]{1,0:T(2,128)(2,1)S(1)} %shard_map.112.own_ref), channel_id=1, source_target_pairs={{0,32},{8,40},{16,48},{24,56},{32,0},{40,8},{48,16},{56,24},{64,96... | collective-permute-start | bytes 24584 | tf_op jit(solution)/shard_map/ppermute | solution.py:57
  61.0 5.3 %collective-permute-start.16 = (bf16[4,2048]{1,0:T(4,128)(2,1)S(1)}, bf16[4,2048]{1,0:T(4,128)(2,1)S(1)}, u32[]{:S(2)}, u32[]{:S(2)}) collective-permute-start(bf16[4,2048]{1,0:T(4,128)(2,1)S(1)} %shard_map.113.own_ref), channel_id=1, source_target_pairs={{0,96},{8,104},{16,112},{24,120},{32,64},{40,72},{48,80},{56,88},{... | collective-permute-start | bytes 49160 | tf_op jit(solution)/shard_map/ppermute | solution.py:57
  62.8 17.4 %collective-permute-start.20 = (bf16[2,1024,128]{2,1,0:T(8,128)(2,1)S(1)}, bf16[2,1024,128]{2,1,0:T(8,128)(2,1)S(1)}, u32[]{:S(2)}, u32[]{:S(2)}) collective-permute-start(bf16[2,1024,128]{2,1,0:T(8,128)(2,1)S(1)} %collective-permute-done.7), channel_id=1, source_target_pairs={{0,32},{8,40},{16,48},{24,56},{32,64},{40,72},{48,80},{56,88},{64,... | collective-permute-start | bytes 1572872 | tf_op jit(solution)/shard_map/ppermute | solution.py:62
  62.8 17.4 %collective-permute-start.21 = (bf16[2,1024,128]{2,1,0:T(8,128)(2,1)S(1)}, bf16[2,1024,128]{2,1,0:T(8,128)(2,1)S(1)}, u32[]{:S(2)}, u32[]{:S(2)}) collective-permute-start(bf16[2,1024,128]{2,1,0:T(8,128)(2,1)S(1)} %collective-permute-done.13), channel_id=1, source_target_pairs={{0,96},{8,104},{16,112},{24,120},{32,0},{40,8},{48,16},{56,24},{64... | collective-permute-start | bytes 1572872 | tf_op jit(solution)/shard_map/ppermute | solution.py:62
  66.2 5.9 %collective-permute-start.17 = (bf16[8,2048]{1,0:T(8,128)(2,1)S(1)}, bf16[8,2048]{1,0:T(8,128)(2,1)S(1)}, u32[]{:S(2)}, u32[]{:S(2)}) collective-permute-start(bf16[8,2048]{1,0:T(8,128)(2,1)S(1)} %shard_map.115.own_ref), channel_id=1, source_target_pairs={{0,16},{8,24},{16,0},{24,8},{32,48},{40,56},{48,32},{56,40},{64,80... | collective-permute-start | bytes 98312 | tf_op jit(solution)/shard_map/ppermute | solution.py:57
  67.1 13.8 %collective-permute-start.23 = (bf16[2,1024,128]{2,1,0:T(8,128)(2,1)S(1)}, bf16[2,1024,128]{2,1,0:T(8,128)(2,1)S(1)}, u32[]{:S(2)}, u32[]{:S(2)}) collective-permute-start(bf16[2,1024,128]{2,1,0:T(8,128)(2,1)S(1)} %copy-done.10), channel_id=1, source_target_pairs={{0,16},{8,24},{16,0},{24,8},{32,48},{40,56},{48,32},{56,40},{64,80... | collective-permute-start | bytes 1572872 | tf_op jit(solution)/shard_map/ppermute | solution.py:57
  72.2 1.3 %collective-permute-start.18 = (bf16[16,2048]{1,0:T(8,128)(2,1)S(1)}, bf16[16,2048]{1,0:T(8,128)(2,1)S(1)}, u32[]{:S(2)}, u32[]{:S(2)}) collective-permute-start(bf16[16,2048]{1,0:T(8,128)(2,1)S(1)} %shard_map.116.own_ref), channel_id=1, source_target_pairs={{0,8},{8,0},{16,24},{24,16},{32,40},{40,32},{48,56},{56,48},{64,72... | collective-permute-start | bytes 196616 | tf_op jit(solution)/shard_map/ppermute | solution.py:57
  75.0 5.7 %collective-permute-start.19 = (f32[4,32,128]{2,1,0:T(8,128)S(1)}, f32[4,32,128]{2,1,0:T(8,128)S(1)}, u32[]{:S(2)}, u32[]{:S(2)}) collective-permute-start(f32[4,32,128]{2,1,0:T(8,128)S(1)} %get-tuple-element.86), channel_id=1, source_target_pairs={{0,3},{1,2},{2,1},{3,0},{4,7},{5,6},{6,5},{7,4},{8,11},{9,10},{10,... | collective-permute-start | bytes 196616 | tf_op jit(solution)/shard_map/ppermute | solution.py:57
  80.7 4.0 %collective-permute-start.22 = (f32[2,32,128]{2,1,0:T(8,128)S(1)}, f32[2,32,128]{2,1,0:T(8,128)S(1)}, u32[]{:S(2)}, u32[]{:S(2)}) collective-permute-start(f32[2,32,128]{2,1,0:T(8,128)S(1)} %get-tuple-element.94), channel_id=1, source_target_pairs={{0,1},{1,0},{2,3},{3,2},{4,5},{5,4},{6,7},{7,6},{8,9},{9,8},{10,11... | collective-permute-start | bytes 98312 | tf_op jit(solution)/shard_map/ppermute | solution.py:57
  80.9 4.1 %collective-permute-start.25 = (bf16[1,1024,128]{2,1,0:T(8,128)(2,1)S(1)}, bf16[1,1024,128]{2,1,0:T(8,128)(2,1)S(1)}, u32[]{:S(2)}, u32[]{:S(2)}) collective-permute-start(bf16[1,1024,128]{2,1,0:T(8,128)(2,1)S(1)} %shard_map.121), channel_id=1, source_target_pairs={{0,8},{8,0},{16,24},{24,16},{32,40},{40,32},{48,56},{56,48},{64,72... | collective-permute-start | bytes 786440 | tf_op jit(solution)/shard_map/ppermute | solution.py:57
  84.8 4.7 %collective-permute-start.27 = (bf16[3,1024,128]{2,1,0:T(8,128)(2,1)S(1)}, bf16[3,1024,128]{2,1,0:T(8,128)(2,1)S(1)}, u32[]{:S(2)}, u32[]{:S(2)}) collective-permute-start(bf16[3,1024,128]{2,1,0:T(8,128)(2,1)S(1)} %shard_map.123), channel_id=1, source_target_pairs={{0,8},{8,0},{16,24},{24,16},{32,40},{40,32},{48,56},{56,48},{64,72... | collective-permute-start | bytes 2359304 | tf_op jit(solution)/shard_map/ppermute | solution.py:57
  85.0 15.9 %collective-permute-start.26 = (bf16[2,1024,128]{2,1,0:T(8,128)(2,1)S(1)}, bf16[2,1024,128]{2,1,0:T(8,128)(2,1)S(1)}, u32[]{:S(2)}, u32[]{:S(2)}) collective-permute-start(bf16[2,1024,128]{2,1,0:T(8,128)(2,1)S(1)} %shard_map.122), channel_id=1, source_target_pairs={{0,64},{8,72},{16,80},{24,88},{32,96},{40,104},{48,112},{56,120},{... | collective-permute-start | bytes 1572872 | tf_op jit(solution)/shard_map/ppermute | solution.py:62
  85.1 3.8 %collective-permute-start.24 = (f32[1,32,128]{2,1,0:T(8,128)S(1)}, f32[1,32,128]{2,1,0:T(8,128)S(1)}, u32[]{:S(2)}, u32[]{:S(2)}) collective-permute-start(f32[1,32,128]{2,1,0:T(8,128)S(1)} %get-tuple-element.98), channel_id=1, source_target_pairs={{0,4},{1,5},{2,6},{3,7},{4,0},{5,1},{6,2},{7,3},{8,12},{9,13},{10,... | collective-permute-start | bytes 49160 | tf_op jit(solution)/shard_map/ppermute | solution.py:57
  (10 other events, 56.2 us)

commit v2 on v1

--- a/solution.py
+++ b/solution.py
@@ -13,7 +13,7 @@
 CHUNK = 1024
 
 CORE, X_HALF, Y_NEAR, Y_FAR = 1, 2, 4, 12
-Z_NEAR, Z_FAR, X_LOW = 1, 3, 4
+Z_NEAR, Z_FAR, X_LOW = 1, 2, 4
 
 COST = 1_000_000_000
 VMEM = pl.BlockSpec(memory_space=pltpu.VMEM)
@@ -29,7 +29,7 @@
         in_specs=in_specs,
         out_specs=out_specs,
         scratch_shapes=list(scratch),
-        compiler_params=pltpu.CompilerParams(vmem_limit_bytes=megabytes << 20),
+        compiler_params=pltpu.CompilerParams(vmem_limit_bytes=int(megabytes * 2**20)),
         cost_estimate=pl.CostEstimate(
             flops=int(cost * COST) + 1, bytes_accessed=1, transcendentals=0
         ),
@@ -72,6 +72,23 @@
     out_ref[rows:] = other_ref[...]
 
 
+def fetch_kernel(block_ref, out_ref, sem):
+    copy = pltpu.make_async_copy(block_ref, out_ref, sem)
+    copy.start()
+    copy.wait()
+
+
+def fetch(block):
+    return call(
+        fetch_kernel,
+        like(block, block.shape[0]),
+        [ANYWHERE],
+        VMEM,
+        [pltpu.SemaphoreType.DMA],
+        megabytes=1,
+    )(block)
+
+
 def join(own, other, cost=0.0):
     both = like(own, 2 * own.shape[0])
     return call(join_kernel, both, [VMEM] * 2, VMEM, megabytes=2, cost=cost)(own, other)
@@ -113,7 +130,7 @@
     feats_scr[half:] = far_ref[...]
     x_low, z = me_ref[1] >> 2, me_ref[1] & 3
     blocks = [
-        feats_scr[gray((part & 3) ^ z) * 2 + ((part >> 2) ^ x_low)] for part in range(2 * half)
+        feats_scr[((part & 3) ^ z) * 2 + ((part >> 2) ^ x_low)] for part in range(2 * half)
     ]
     shape = (rows, rows)
     order = batch_row(me_ref, lax.broadcasted_iota(jnp.int32, shape, 0))
@@ -155,7 +172,6 @@
         [SMEM] + [VMEM] * 5,
         [VMEM] * 2,
         [pltpu.VMEM((2 * near.shape[0],) + near.shape[1:], near.dtype)],
-        cost=2.5,
     )(me, near, far, gain[None], query_weight, keyval_weight)
 
 
@@ -164,7 +180,7 @@
     proj_scr, query_scr, score_scr, rows_scr,
 ):
     rows, positions, head_dim = key_ref.shape
-    heads = query_scr.shape[0]
+    heads = query_scr.shape[1]
     query_cols = heads * head_dim
     scale = head_dim ** (-0.5)
     proj_scr[...] = kept_ref[...] + got_ref[...]
@@ -174,14 +190,15 @@
             b : b + 1
         ]
 
+    queries, tops, news = [], [], []
     for b in range(rows):
         squares = proj_scr[b : b + 1, -SQUARES:]
         inv_scale = lax.rsqrt(squares / features + 1e-05)
         for h in range(heads):
-            query_scr[h : h + 1, :] = (
+            query_scr[b, h : h + 1, :] = (
                 proj_scr[b : b + 1, h * head_dim : (h + 1) * head_dim] * inv_scale
             )
-        query = rotate(query_scr[...], b).astype(jnp.bfloat16)
+        query = rotate(query_scr[b], b).astype(jnp.bfloat16)
         new_key = proj_scr[b : b + 1, query_cols : query_cols + head_dim] * inv_scale
         new_key = rotate(jnp.broadcast_to(new_key, (8, head_dim)), b)[:1].astype(jnp.bfloat16)
         new_value = proj_scr[b : b + 1, query_cols + head_dim : query_cols + 2 * head_dim]
@@ -192,12 +209,14 @@
             )
             * scale
         )
-        length = lengths_ref[b]
-        top = self_score
-        for start in range(0, positions, CHUNK):
+        queries.append(query)
+        news.append((self_score, new_value))
+        tops.append(jnp.full((heads, CHUNK), masked_score, jnp.float32))
+    for start in range(0, positions, CHUNK):
+        for b in range(rows):
             scores = (
                 lax.dot_general(
-                    query,
+                    queries[b],
                     key_ref[b, start : start + CHUNK, :],
                     (((1,), (1,)), ((), ())),
                     preferred_element_type=jnp.float32,
@@ -205,21 +224,26 @@
                 * scale
             )
             place = start + lax.broadcasted_iota(jnp.int32, scores.shape, 1)
-            scores = jnp.where(place < length, scores, masked_score)
-            score_scr[:, start : start + CHUNK] = scores
-            top = jnp.maximum(top, jnp.max(scores, axis=1, keepdims=True))
-        self_expo = jnp.exp(self_score - top)
-        totals = self_expo
-        numer = self_expo * new_value
-        for start in range(0, positions, CHUNK):
-            expos = jnp.exp(score_scr[:, start : start + CHUNK] - top)
-            totals = totals + jnp.sum(expos, axis=1, keepdims=True)
-            numer = numer + jnp.dot(
+            scores = jnp.where(place < lengths_ref[b], scores, masked_score)
+            score_scr[b, :, start : start + CHUNK] = scores
+            tops[b] = jnp.maximum(tops[b], scores)
+    sums, numers = [], []
+    for b, (self_score, new_value) in enumerate(news):
+        tops[b] = jnp.maximum(jnp.max(tops[b], axis=1, keepdims=True), self_score)
+        sums.append(jnp.zeros((heads, CHUNK), jnp.float32))
+        numers.append(jnp.exp(self_score - tops[b]) * new_value)
+    for start in range(0, positions, CHUNK):
+        for b in range(rows):
+            expos = jnp.exp(score_scr[b, :, start : start + CHUNK] - tops[b])
+            sums[b] = sums[b] + expos
+            numers[b] = numers[b] + jnp.dot(
                 expos.astype(jnp.bfloat16),
                 value_ref[b, start : start + CHUNK, :],
                 preferred_element_type=jnp.float32,
             )
-        attended = numer / totals
+    for b, (self_score, new_value) in enumerate(news):
+        totals = jnp.sum(sums[b], axis=1, keepdims=True) + jnp.exp(self_score - tops[b])
+        attended = numers[b] / totals
         for h in range(heads):
             rows_scr[b : b + 1, h * head_dim : (h + 1) * head_dim] = attended[h : h + 1, :]
     out_ref[...] = rows_scr[...].astype(jnp.bfloat16)
@@ -234,8 +258,8 @@
         VMEM,
         [
             pltpu.VMEM(kept.shape, jnp.float32),
-            pltpu.VMEM((heads, head_dim), jnp.float32),
-            pltpu.VMEM((heads, positions), jnp.float32),
+            pltpu.VMEM((rows, heads, head_dim), jnp.float32),
+            pltpu.VMEM((rows, heads, positions), jnp.float32),
             pltpu.VMEM((rows, heads * head_dim), jnp.float32),
         ],
     )(lengths, kept, got, cosine, sine, key_cache, value_cache)
@@ -259,7 +283,7 @@
         )
         for k in range(step // width):
             part = start // width + k
-            place = gray((part & 3) ^ z) * 2 + ((part >> 2) ^ x_low)
+            place = ((part & 3) ^ z) * 2 + ((part >> 2) ^ x_low)
             blocks_scr[place] = mixed[:, k * width : (k + 1) * width]
     half = kept_ref.shape[0]
     kept_ref[...] = blocks_scr[:half]
@@ -275,7 +299,19 @@
         [SMEM] + [VMEM] * 3,
         [VMEM] * 2,
         [pltpu.VMEM((8, rows, width), jnp.float32)],
+        cost=2.2,
     )(me, own, other, out_weight)
+
+
+SAME, OTHER = "same", "other"
+
+
+def pick(piece_ref, slot):
+    if slot == SAME:
+        return piece_ref.at[lax.axis_index("row") & 1]
+    if slot == OTHER:
+        return piece_ref.at[(lax.axis_index("row") & 1) ^ 1]
+    return piece_ref.at[slot]
 
 
 def start_and_wait(copies):
@@ -285,51 +321,17 @@
         copy.wait()
 
 
-def stage_kernel(groups, me_ref, chunks_ref, *refs):
-    pieces, (buffer, in_sems, out_sems) = refs[: len(groups)], refs[len(groups) :]
-    row = me_ref[0]
-    copies = []
-    for piece, group in zip(pieces, groups):
-        for i, (dy, dx, other) in enumerate(group):
-            chip = ((((row >> 2) + dy) & 3) << 1) | (((row >> 1) & 1) ^ dx)
-            chunk = chunks_ref.at[(chip << 1) | ((row & 1) ^ other)]
-            k = len(copies)
-            copies.append(
-                (
-                    pltpu.make_async_copy(chunk, buffer.at[k], in_sems.at[k]),
-                    pltpu.make_async_copy(buffer.at[k], piece.at[i], out_sems.at[k]),
-                )
-            )
-    for fetch, _ in copies:
-        fetch.start()
-    for fetch, store in copies:
-        fetch.wait()
-        store.start()
-    for _, store in copies:
-        store.wait()
-
-
-def stage(me, chunks, groups):
-    count = sum(len(group) for group in groups)
-    return call(
-        functools.partial(stage_kernel, groups),
-        [like(chunks, len(group)) for group in groups],
-        [SMEM, HBM],
-        [HBM] * len(groups),
-        [
-            pltpu.VMEM((count,) + chunks.shape[1:], chunks.dtype),
-            pltpu.SemaphoreType.DMA((count,)),
-            pltpu.SemaphoreType.DMA((count,)),
-        ],
-        60,
-    )(me, chunks)
+def chip_pair(chunks, dy, dx):
+    row = lax.axis_index("row")
+    chip = ((((row >> 2) + dy) & 3) << 1) | (((row >> 1) & 1) ^ dx)
+    return lax.dynamic_slice_in_dim(chunks, chip * 2, 2, 0)
 
 
 def pack_kernel(count, slots, *refs):
     pieces, out_ref, sems = refs[:count], refs[-2], refs[-1]
     start_and_wait(
         [
-            pltpu.make_async_copy(pieces[p].at[i], out_ref.at[k], sems.at[k])
+            pltpu.make_async_copy(pick(pieces[p], i), out_ref.at[k], sems.at[k])
             for k, (p, i) in enumerate(slots)
         ]
     )
@@ -355,7 +357,7 @@
         column = pl.multiple_of(((chip << 1) | ((row & 1) ^ other)) * HD, HD)
         copies.append(
             pltpu.make_async_copy(
-                pieces[piece].at[slot], relaid_ref.at[:, pl.ds(column, HD)], sems.at[k]
+                pick(pieces[piece], slot), relaid_ref.at[:, pl.ds(column, HD)], sems.at[k]
             )
         )
     start_and_wait(copies)
@@ -395,83 +397,82 @@
     def pair(dy, dx):
         return [(dy, dx, 0), (dy, dx, 1)]
 
-    to_a, to_b = stage(me, chunks, [pair(1, 0), pair(3, 0)])
-    got_a, got_b = shift_y(to_a, 1), shift_y(to_b, 3)
-    own, to_own, to_c, to_d, to_e, to_f, to_g = stage(
-        me,
-        chunks,
-        [[(0, 0, 0)], [(0, 0, 1)], pair(2, 0), pair(0, 1), pair(1, 1), pair(3, 1), pair(2, 1)],
-    )
-    got_own = flip(to_own, "row", CORE)
-
-    feats = tokens[None]
-    other = flip(feats, "col", X_LOW)
-    other, to_e, cosine, sine, to_c, to_d, to_f, to_g = tie(
-        other, to_e, cosine, sine, to_c, to_d, to_f, to_g
-    )
+    to_a, to_b, to_c, to_e = [chip_pair(chunks, *at) for at in ((1, 0), (3, 0), (2, 0), (1, 1))]
+    got_a, got_b, got_c = shift_y(to_a, 1), shift_y(to_b, 3), shift_y(to_c, 2)
+
+    other = flip(tokens[None], "col", X_LOW)
+    feats = fetch(tokens[None])
+    other, feats, to_e, cosine, sine = tie(other, feats, to_e, cosine, sine)
     via_e = flip(to_e, "row", X_HALF)
-    feats = join(feats, other)
+    feats = join(feats, other, 3)
     other = flip(feats, "col", Z_NEAR)
-    other, got_own = tie(other, got_own)
-    feats = join(feats, other)
+    other, chunks = tie(other, chunks)
+    own, to_d, to_f, to_g = [chip_pair(chunks, *at) for at in ((0, 0), (0, 1), (3, 1), (2, 1))]
+    feats = join(feats, other, 1.2)
     other = flip(feats, "col", Z_FAR)
-    got_c = shift_y(to_c, 2)
     kept, sent = project(me, feats, other, norm_gain, query_weight, keyval_weight)
-    got_a, got_b, sent = tie(got_a, got_b, sent)
     got = flip(sent, "row", CORE)
-    got, via_e = tie(got, via_e)
-    kept, sent = add_halves(kept, got, 5)
+    got, via_e, own, to_d, to_f, to_g = tie(got, via_e, own, to_d, to_f, to_g)
+    kept, sent = add_halves(kept, got)
     got = flip(sent, "row", X_HALF)
-    via_f, via_g = flip(to_f, "row", X_HALF), flip(to_g, "row", X_HALF)
-    got, got_c = tie(got, got_c)
-    swap_first = flip(pack([got_a, got_b, got_c], [(k, 1) for k in range(3)]), "row", CORE)
-    kept, sent = add_halves(kept, got, 10)
+    via_f = flip(to_f, "row", X_HALF)
+    got, got_a, got_b, got_c = tie(got, got_a, got_b, got_c)
+    swap_first = pack([own, got_a, got_b, got_c, to_d], [(k, OTHER) for k in range(5)])
+    swap_first = flip(swap_first, "row", CORE)
+    kept, sent = add_halves(kept, got, 8)
     got = flip(sent, "row", Y_FAR)
-    kept, sent = add_halves(kept, got)
+    via_g = flip(to_g, "row", X_HALF)
+    swap_e = flip(pack([via_e], [(0, OTHER)]), "row", CORE)
+    kept, sent = add_halves(kept, got, 3)
     got = flip(sent, "row", Y_NEAR)
     attended = attend(
         lengths, kept, got, cosine, sine, key_cache, value_cache, features, heads
     )
     other = flip(attended, "row", Y_NEAR)
-    other, via_f = tie(other, via_f)
-    attended = join(attended, other)
+    other, via_f, swap_e = tie(other, via_f, swap_e)
+    via_e = pack([via_e, swap_e], [(0, SAME), (1, 0)])
+    attended = join(attended, other, 3)
     other = flip(attended, "row", Y_FAR)
     got_e, got_f = shift_y(via_e, 1), shift_y(via_f, 3)
     via_g, swap_first, other = tie(via_g, swap_first, other)
-    swap_g = flip(pack([via_g], [(0, 1)]), "row", CORE)
+    swap_g = flip(pack([via_g], [(0, OTHER)]), "row", CORE)
     attended = join(attended, other, 4.5)
     other = flip(attended, "row", X_HALF)
-    got_d = flip(to_d, "row", X_HALF)
-    attended = join(attended, other, 2.4)
+    got_d = flip(pack([to_d, swap_first], [(0, SAME), (1, 4)]), "row", X_HALF)
+    attended = join(attended, other, 1.2)
     other = flip(attended, "row", CORE)
     relaid = place(
         me,
-        [own, got_own, got_a, got_b, got_c, swap_first],
-        [(0, 0, 0, 0, 0), (1, 0, 0, 0, 1)]
-        + [(k + 2, 0, dy, 0, 0) for k, dy in enumerate((1, 3, 2))]
-        + [(5, k, dy, 0, 1) for k, dy in enumerate((1, 3, 2))],
+        [own, got_a, got_b, got_c, swap_first],
+        [(k, SAME, dy, 0, 0) for k, dy in enumerate((0, 1, 3, 2))]
+        + [(4, k, dy, 0, 1) for k, dy in enumerate((0, 1, 3, 2))],
         None,
     )
     kept, sent = mix(me, attended, other, out_weight)
-    via_g = pack([via_g, swap_g], [(0, 0), (1, 0)])
+    via_g = pack([via_g, swap_g], [(0, SAME), (1, 0)])
     got = flip(sent, "col", Z_FAR)
     got_g = shift_y(via_g, 2)
-    got, got_e, got_f, relaid = tie(got, got_e, got_f, relaid)
-    kept, sent = add_halves(kept, got, 3.2)
+    got, got_e, got_f = tie(got, got_e, got_f)
+    swap_last = flip(pack([got_f], [(0, OTHER)]), "row", CORE)
+    kept, sent = add_halves(kept, got, 0.3)
     got = flip(sent, "col", Z_NEAR)
-    got, got_d = tie(got, got_d)
-    swap_last = flip(pack([got_d, got_e, got_f], [(k, 1) for k in range(3)]), "row", CORE)
-    kept, sent = add_halves(kept, got, 3.2)
+    got, got_d, relaid = tie(got, got_d, relaid)
+    kept, sent = add_halves(kept, got)
     got = flip(sent, "col", X_LOW)
+    relaid = place(
+        me,
+        [got_d, got_e, got_f],
+        [(0, 0, 0, 1, 0), (1, 0, 1, 1, 0), (2, SAME, 3, 1, 0), (0, 1, 0, 1, 1), (1, 1, 1, 1, 1)],
+        relaid,
+    )
+    got, relaid = tie(got, relaid)
     mixed = (kept + got)[0].astype(jnp.bfloat16)
     relaid = place(
         me,
-        [got_d, got_e, got_f, swap_last],
-        [(k, 0, dy, 1, 0) for k, dy in enumerate((0, 1, 3))]
-        + [(3, k, dy, 1, 1) for k, dy in enumerate((0, 1, 3))],
+        [got_g, swap_last],
+        [(0, 0, 2, 1, 0), (0, 1, 2, 1, 1), (1, 0, 3, 1, 1)],
         relaid,
     )
-    relaid = place(me, [got_g], [(0, 0, 2, 1, 0), (0, 1, 2, 1, 1)], relaid)
     return (mixed, relaid)
 
 

time: 103 us -> 81.5 us (0.79)
  waiting for transfers between devices: 44.7 us -> 25.5 us
  Pallas kernels: 17.5 us -> 11.1 us
  local copies, waits for them, and re-layouts: 2.37 us -> 5.74 us
  starting transfers between devices: 35.2 us -> 37.1 us
    ppermute x6, waiting for transfers between devices: 18.8 us -> 0.74 us  [shift_y(): lax.ppermute(block, 'row', [(i, (i + 4 * steps) % size) for i in range(si...]
    pallas_call x2 -> x1, Pallas kernels: 6.29 us -> 0.02 us  [fetch(): call(fetch_kernel, like(block, block.shape[0]), [ANYWHERE], VMEM, [pltpu....]
    dynamic_slice x0 -> x2, local copies, waits for them, and re-layouts: none -> 2.87 us  [chip_pair(): return lax.dynamic_slice_in_dim(chunks, chip * 2, 2, 0)]
    ppermute x6, starting transfers between devices: 8.72 us -> 10.1 us  [shift_y(): lax.ppermute(block, 'row', [(i, (i + 4 * steps) % size) for i in range(si...]
    ppermute x22, waiting for transfers between devices: 25.9 us -> 24.8 us  [flip(): return lax.ppermute(block, axis, [(i, i ^ bits) for i in range(size)])]
    unnamed x28 -> x18, local copies, waits for them, and re-layouts: 2.37 us -> 2.86 us
  transfers between devices with their start and end apart: 28 -> 28, of which waited for: 13 -> 13; matrix products, arithmetic and copies ran while one was open for 1% -> 5% of each run, Pallas kernels for 16% -> 12%
where the time goes in v2:
time: 81.5 us; the launch traced here: 81.3 us
  starting transfers between devices  37.1 us (46%)
  waiting for transfers between devices  25.5 us (31%)
  Pallas kernels  11.1 us (14%)
  local copies, waits for them, and re-layouts  5.74 us (7%)
  between operations  0.91 us (1%)
  other arithmetic  0.87 us (1%)
    ppermute x22, starting transfers between devices, flip(): return lax.ppermute(block, axis, [(i, i ^ bits) for i in range(size)])  27 us
    ppermute x22, waiting for transfers between devices, flip(): return lax.ppermute(block, axis, [(i, i ^ bits) for i in range(size)])  24.8 us
    ppermute x6, starting transfers between devices, shift_y(): lax.ppermute(block, 'row', [(i, (i + 4 * steps) % size) for i in range(si...  10.1 us
    pallas_call x3, Pallas kernels, place(): call(functools.partial(place_kernel, len(pieces), slots), jax.ShapeDtypeS...  5.02 us
    dynamic_slice x2, local copies, waits for them, and re-layouts, chip_pair(): return lax.dynamic_slice_in_dim(chunks, chip * 2, 2, 0)  2.87 us
    unnamed x18, local copies, waits for them, and re-layouts  2.86 us
    pallas_call x1, Pallas kernels, attend(): call(functools.partial(attend_kernel, features), jax.ShapeDtypeStruct((ro...  2.62 us
  transfers between devices with their start and end apart: 28, of which 13 were waited for; matrix products, arithmetic and copies ran while one was open for 5% of the time, Pallas kernels for 12%

profile of v2, /device:TPU:0, one launch (start us, length us, event | category | flops | bytes accessed | tf_op | source)
XLA Modules:
  0.0 81.3 jit_solution(4872344703763468813)
XLA Ops:
  0.6 1.7 %collective-permute-start = (bf16[1,32,128]{2,1,0:T(8,128)(2,1)}, bf16[1,32,128]{2,1,0:T(8,128)(2,1)S(1)}, u32[]{:S(2)}, u32[]{:S(2)}) collective-permute-start(bf16[1,32,128]{2,1,0:T(8,128)(2,1)} %bitcast.6), channel_id=1, source_target_pairs={{0,4},{1,5},{2,6},{3,7},{4,0},{5,1},{6,2},{7,3},{8,12},{9,13},{10,... | collective-permute-start | bytes 24584 | tf_op jit(solution)/shard_map/ppermute | solution.py:57
  2.3 2.7 %constant_dynamic-slice_fusion = (bf16[2,1024,128]{2,1,0:T(8,128)(2,1)S(1)}, bf16[2,1024,128]{2,1,0:T(8,128)(2,1)}, bf16[2,1024,128]{2,1,0:T(8,128)(2,1)}, bf16[2,1024,128]{2,1,0:T(8,128)(2,1)}) fusion(bf16[16,1024,128]{2,1,0:T(8,128)(2,1)} %bitcast.8, s32[]{:T(128)S(6)} %select_n.31, s32[]{:T(128)S(6)} %select_n.30, s32[]{:T(128)S(6)} %select_n.29, ...), kind=kLoop, calls=%fused_computation.2 | loop fusion | bytes 4194320 | tf_op jit(solution)/shard_map/dynamic_slice | solution.py:327
  5.0 1.6 %collective-permute-start.6 = (bf16[2,1024,128]{2,1,0:T(8,128)(2,1)}, bf16[2,1024,128]{2,1,0:T(8,128)(2,1)S(1)}, u32[]{:S(2)}, u32[]{:S(2)}) collective-permute-start(bf16[2,1024,128]{2,1,0:T(8,128)(2,1)} %get-tuple-element.94), channel_id=1, source_target_pairs={{0,32},{8,40},{16,48},{24,56},{32,64},{40,72},{48,80},{56,88},{64,... | collective-permute-start | bytes 1572872 | tf_op jit(solution)/shard_map/ppermute | solution.py:62
  6.6 1.7 %collective-permute-start.7 = (bf16[2,1024,128]{2,1,0:T(8,128)(2,1)}, bf16[2,1024,128]{2,1,0:T(8,128)(2,1)S(1)}, u32[]{:S(2)}, u32[]{:S(2)}) collective-permute-start(bf16[2,1024,128]{2,1,0:T(8,128)(2,1)} %get-tuple-element.93), channel_id=1, source_target_pairs={{0,96},{8,104},{16,112},{24,120},{32,0},{40,8},{48,16},{56,24},{64... | collective-permute-start | bytes 1572872 | tf_op jit(solution)/shard_map/ppermute | solution.py:62
  8.3 2.0 %collective-permute-start.8 = (bf16[2,1024,128]{2,1,0:T(8,128)(2,1)S(1)}, bf16[2,1024,128]{2,1,0:T(8,128)(2,1)S(1)}, u32[]{:S(2)}, u32[]{:S(2)}) collective-permute-start(bf16[2,1024,128]{2,1,0:T(8,128)(2,1)S(1)} %get-tuple-element.92), channel_id=1, source_target_pairs={{0,64},{8,72},{16,80},{24,88},{32,96},{40,104},{48,112},{56,120},{... | collective-permute-start | bytes 1572872 | tf_op jit(solution)/shard_map/ppermute | solution.py:62
  10.5 2.8 %collective-permute-start.4 = (bf16[2,1024,128]{2,1,0:T(8,128)(2,1)}, bf16[2,1024,128]{2,1,0:T(8,128)(2,1)S(1)}, u32[]{:S(2)}, u32[]{:S(2)}) collective-permute-start(bf16[2,1024,128]{2,1,0:T(8,128)(2,1)} %get-tuple-element.52), channel_id=1, source_target_pairs={{0,16},{8,24},{16,0},{24,8},{32,48},{40,56},{48,32},{56,40},{64,80... | collective-permute-start | bytes 1572872 | tf_op jit(solution)/shard_map/ppermute | solution.py:57
  13.3 1.9 %collective-permute-start.1 = (bf16[2,32,128]{2,1,0:T(8,128)(2,1)S(1)}, bf16[2,32,128]{2,1,0:T(8,128)(2,1)S(1)}, u32[]{:S(2)}, u32[]{:S(2)}) collective-permute-start(bf16[2,32,128]{2,1,0:T(8,128)(2,1)S(1)} %shard_map.105.own_ref), channel_id=1, source_target_pairs={{0,1},{1,0},{2,3},{3,2},{4,5},{5,4},{6,7},{7,6},{8,9},{9,8},{10,11... | collective-permute-start | bytes 49160 | tf_op jit(solution)/shard_map/ppermute | solution.py:57
  15.2 1.8 %collective-permute-done.1.other_ref = bf16[2,32,128]{2,1,0:T(8,128)(2,1)S(1)} collective-permute-done((bf16[2,32,128]{2,1,0:T(8,128)(2,1)S(1)}, bf16[2,32,128]{2,1,0:T(8,128)(2,1)S(1)}, u32[]{:S(2)}, u32[]{:S(2)}) %collective-permute-start.1) | collective-permute-done | bytes 16416 | tf_op jit(solution)/shard_map/ppermute | solution.py:57
  17.1 3.9 %collective-permute-start.2 = (bf16[4,32,128]{2,1,0:T(8,128)(2,1)S(1)}, bf16[4,32,128]{2,1,0:T(8,128)(2,1)S(1)}, u32[]{:S(2)}, u32[]{:S(2)}) collective-permute-start(bf16[4,32,128]{2,1,0:T(8,128)(2,1)S(1)} %shard_map.106.near_ref), channel_id=1, source_target_pairs={{0,2},{1,3},{2,0},{3,1},{4,6},{5,7},{6,4},{7,5},{8,10},{9,11},{10,... | collective-permute-start | bytes 98312 | tf_op jit(solution)/shard_map/ppermute | solution.py:57
  21.0 1.8 %collective-permute-done.2.far_ref = bf16[4,32,128]{2,1,0:T(8,128)(2,1)S(1)} collective-permute-done((bf16[4,32,128]{2,1,0:T(8,128)(2,1)S(1)}, bf16[4,32,128]{2,1,0:T(8,128)(2,1)S(1)}, u32[]{:S(2)}, u32[]{:S(2)}) %collective-permute-start.2) | collective-permute-done | bytes 32800 | tf_op jit(solution)/shard_map/ppermute | solution.py:57
  22.8 2.2 %copy-done = bf16[1024,2048]{1,0:T(8,128)(2,1)S(1)} copy-done((bf16[1024,2048]{1,0:T(8,128)(2,1)S(1)}, bf16[1024,2048]{1,0:T(8,128)(2,1)}, u32[]{:S(2)}) %copy-start) | copy-done | bytes 4194328
  25.0 1.4 %shard_map.107 = (f32[16,2432]{1,0:T(8,128)S(1)}, f32[16,2432]{1,0:T(8,128)S(1)}) custom-call(s32[2]{0:T(128)S(1)} %pad_add_fusion.me_ref, bf16[4,32,128]{2,1,0:T(8,128)(2,1)S(1)} %shard_map.106.near_ref, bf16[4,32,128]{2,1,0:T(8,128)(2,1)S(1)} %collective-permute-done.2.far_ref, bf16[1,1024]{1,0:T(2,128)(2,1)S(1)} %broadcast_in_dim.10.gain_ref, ...), custom_call_target="tpu_custom_call" | custom-call | flops 1 | bytes 1 | tf_op jit(solution)/shard_map/pallas_call | solution.py:169
  28.8 2.7 %collective-permute-start.12 = (bf16[2,1024,128]{2,1,0:T(8,128)(2,1)S(1)}, bf16[2,1024,128]{2,1,0:T(8,128)(2,1)S(1)}, u32[]{:S(2)}, u32[]{:S(2)}) collective-permute-start(bf16[2,1024,128]{2,1,0:T(8,128)(2,1)S(1)} %get-tuple-element.64), channel_id=1, source_target_pairs={{0,16},{8,24},{16,0},{24,8},{32,48},{40,56},{48,32},{56,40},{64,80... | collective-permute-start | bytes 1572872 | tf_op jit(solution)/shard_map/ppermute | solution.py:57
  32.3 2.4 %collective-permute-done.5.got_ref = f32[8,2432]{1,0:T(8,128)S(1)} collective-permute-done((f32[8,2432]{1,0:T(8,128)S(1)}, f32[8,2432]{1,0:T(8,128)S(1)}, u32[]{:S(2)}, u32[]{:S(2)}) %collective-permute-start.5) | collective-permute-done | bytes 77856 | tf_op jit(solution)/shard_map/ppermute | solution.py:57
  37.5 2.8 %collective-permute-done.9.got_ref = f32[4,2432]{1,0:T(4,128)S(1)} collective-permute-done((f32[4,2432]{1,0:T(4,128)S(1)}, f32[4,2432]{1,0:T(4,128)S(1)}, u32[]{:S(2)}, u32[]{:S(2)}) %collective-permute-start.9) | collective-permute-done | bytes 38944 | tf_op jit(solution)/shard_map/ppermute | solution.py:57
  40.4 3.8 %collective-permute-done.10.got_ref = f32[2,2432]{1,0:T(2,128)S(1)} collective-permute-done((f32[2,2432]{1,0:T(2,128)S(1)}, f32[2,2432]{1,0:T(2,128)S(1)}, u32[]{:S(2)}, u32[]{:S(2)}) %collective-permute-start.10) | collective-permute-done | bytes 19488 | tf_op jit(solution)/shard_map/ppermute | solution.py:57
  44.2 2.6 %shard_map.111.own_ref = bf16[2,2048]{1,0:T(2,128)(2,1)S(1)} custom-call(s32[2]{0:T(128)S(1)} %copy-done.5, f32[2,2432]{1,0:T(2,128)S(1)} %get-tuple-element.60.kept_ref, f32[2,2432]{1,0:T(2,128)S(1)} %collective-permute-done.10.got_ref, f32[2,128]{1,0:T(2,128)S(1)} %get-tuple-element.62.cos_ref, f32[2,128]{1,0:T(2,128)S(1)} %get-tuple-element.63.sin_ref, ...), custom_call_target="tpu_custom_call" | custom-call | flops 1 | bytes 1 | tf_op jit(solution)/shard_map/pallas_call | solution.py:254
  46.9 3.6 %collective-permute-done.11.other_ref = bf16[2,2048]{1,0:T(2,128)(2,1)S(1)} collective-permute-done((bf16[2,2048]{1,0:T(2,128)(2,1)S(1)}, bf16[2,2048]{1,0:T(2,128)(2,1)S(1)}, u32[]{:S(2)}, u32[]{:S(2)}) %collective-permute-start.11) | collective-permute-done | bytes 8224 | tf_op jit(solution)/shard_map/ppermute | solution.py:57
  51.8 3.2 %collective-permute-start.21 = (bf16[2,1024,128]{2,1,0:T(8,128)(2,1)S(1)}, bf16[2,1024,128]{2,1,0:T(8,128)(2,1)S(1)}, u32[]{:S(2)}, u32[]{:S(2)}) collective-permute-start(bf16[2,1024,128]{2,1,0:T(8,128)(2,1)S(1)} %collective-permute-done.12), channel_id=1, source_target_pairs={{0,96},{8,104},{16,112},{24,120},{32,0},{40,8},{48,16},{56,24},{64... | collective-permute-start | bytes 1572872 | tf_op jit(solution)/shard_map/ppermute | solution.py:62
  55.0 1.4 %collective-permute-done.14.refs_0_ = bf16[2,1024,128]{2,1,0:T(8,128)(2,1)S(1)} collective-permute-done((bf16[2,1024,128]{2,1,0:T(8,128)(2,1)S(1)}, bf16[2,1024,128]{2,1,0:T(8,128)(2,1)S(1)}, u32[]{:S(2)}, u32[]{:S(2)}) %collective-permute-start.14) | collective-permute-done | bytes 524320 | tf_op jit(solution)/shard_map/ppermute | solution.py:57
  56.6 1.7 %collective-permute-start.17 = (bf16[8,2048]{1,0:T(8,128)(2,1)S(1)}, bf16[8,2048]{1,0:T(8,128)(2,1)S(1)}, u32[]{:S(2)}, u32[]{:S(2)}) collective-permute-start(bf16[8,2048]{1,0:T(8,128)(2,1)S(1)} %shard_map.115.own_ref), channel_id=1, source_target_pairs={{0,16},{8,24},{16,0},{24,8},{32,48},{40,56},{48,32},{56,40},{64,80... | collective-permute-start | bytes 98312 | tf_op jit(solution)/shard_map/ppermute | solution.py:57
  58.3 2.0 %collective-permute-start.23 = (bf16[2,1024,128]{2,1,0:T(8,128)(2,1)S(1)}, bf16[2,1024,128]{2,1,0:T(8,128)(2,1)S(1)}, u32[]{:S(2)}, u32[]{:S(2)}) collective-permute-start(bf16[2,1024,128]{2,1,0:T(8,128)(2,1)S(1)} %shard_map.120), channel_id=1, source_target_pairs={{0,16},{8,24},{16,0},{24,8},{32,48},{40,56},{48,32},{56,40},{64,80... | collective-permute-start | bytes 1572872 | tf_op jit(solution)/shard_map/ppermute | solution.py:57
  60.4 1.7 %collective-permute-done.17.other_ref = bf16[8,2048]{1,0:T(8,128)(2,1)S(1)} collective-permute-done((bf16[8,2048]{1,0:T(8,128)(2,1)S(1)}, bf16[8,2048]{1,0:T(8,128)(2,1)S(1)}, u32[]{:S(2)}, u32[]{:S(2)}) %collective-permute-start.17) | collective-permute-done | bytes 32800 | tf_op jit(solution)/shard_map/ppermute | solution.py:57
  62.2 1.6 %collective-permute-start.26 = (bf16[2,1024,128]{2,1,0:T(8,128)(2,1)S(1)}, bf16[2,1024,128]{2,1,0:T(8,128)(2,1)S(1)}, u32[]{:S(2)}, u32[]{:S(2)}) collective-permute-start(bf16[2,1024,128]{2,1,0:T(8,128)(2,1)S(1)} %shard_map.125), channel_id=1, source_target_pairs={{0,64},{8,72},{16,80},{24,88},{32,96},{40,104},{48,112},{56,120},{... | collective-permute-start | bytes 1572872 | tf_op jit(solution)/shard_map/ppermute | solution.py:62
  63.8 1.5 %shard_map.117 = (f32[4,32,128]{2,1,0:T(8,128)S(1)}, f32[4,32,128]{2,1,0:T(8,128)S(1)}) custom-call(s32[2]{0:T(128)S(1)} %pad_add_fusion.me_ref, bf16[16,2048]{1,0:T(8,128)(2,1)S(1)} %shard_map.116.own_ref, bf16[16,2048]{1,0:T(8,128)(2,1)S(1)} %collective-permute-done.18.other_ref, bf16[2048,1024]{1,0:T(8,128)(2,1)S(1)} %copy-done.6), custom_call_target="tpu_custom_call" | custom-call | flops 2200000000 | bytes 1 | tf_op jit(solution)/shard_map/pallas_call | solution.py:296
  65.3 3.6 %collective-permute-start.19 = (f32[4,32,128]{2,1,0:T(8,128)S(1)}, f32[4,32,128]{2,1,0:T(8,128)S(1)}, u32[]{:S(2)}, u32[]{:S(2)}) collective-permute-start(f32[4,32,128]{2,1,0:T(8,128)S(1)} %get-tuple-element.75), channel_id=1, source_target_pairs={{0,2},{1,3},{2,0},{3,1},{4,6},{5,7},{6,4},{7,5},{8,10},{9,11},{10,... | collective-permute-start | bytes 196616 | tf_op jit(solution)/shard_map/ppermute | solution.py:57
  68.9 2.5 %collective-permute-done.19.got_ref = f32[4,32,128]{2,1,0:T(8,128)S(1)} collective-permute-done((f32[4,32,128]{2,1,0:T(8,128)S(1)}, f32[4,32,128]{2,1,0:T(8,128)S(1)}, u32[]{:S(2)}, u32[]{:S(2)}) %collective-permute-start.19) | collective-permute-done | bytes 65568 | tf_op jit(solution)/shard_map/ppermute | solution.py:57
  71.4 1.4 %collective-permute-start.22 = (f32[2,32,128]{2,1,0:T(8,128)S(1)}, f32[2,32,128]{2,1,0:T(8,128)S(1)}, u32[]{:S(2)}, u32[]{:S(2)}) collective-permute-start(f32[2,32,128]{2,1,0:T(8,128)S(1)} %get-tuple-element.80), channel_id=1, source_target_pairs={{0,1},{1,0},{2,3},{3,2},{4,5},{5,4},{6,7},{7,6},{8,9},{9,8},{10,11... | collective-permute-start | bytes 98312 | tf_op jit(solution)/shard_map/ppermute | solution.py:57
  73.0 1.9 %shard_map.121.refs_3_ = bf16[1024,2048]{1,0:T(8,128)(2,1)} custom-call(s32[2]{0:T(128)S(1)} %pad_add_fusion.me_ref, bf16[2,1024,128]{2,1,0:T(8,128)(2,1)S(1)} %get-tuple-element.68.refs_0_, bf16[2,1024,128]{2,1,0:T(8,128)(2,1)S(1)} %collective-permute-done.6.refs_1_, bf16[2,1024,128]{2,1,0:T(8,128)(2,1)S(1)} %collective-permute-done.7.refs_2_, ...), custom_call_target="tpu_custom_call" | custom-call | flops 1 | bytes 1 | tf_op jit(solution)/shard_map/pallas_call | solution.py:369
  75.7 1.6 %shard_map.123.refs_2_ = bf16[1024,2048]{1,0:T(8,128)(2,1)} custom-call(s32[2]{0:T(128)S(1)} %pad_add_fusion.me_ref, bf16[2,1024,128]{2,1,0:T(8,128)(2,1)S(1)} %collective-permute-done.23.refs_0_, bf16[2,1024,128]{2,1,0:T(8,128)(2,1)S(1)} %collective-permute-done.20.refs_1_, ...), custom_call_target="tpu_custom_call", output_to_operand_aliasing={{}: (4, {})} | custom-call | flops 1 | bytes 1 | tf_op jit(solution)/shard_map/pallas_call | solution.py:369
  77.4 1.9 %collective-permute-done.24 = f32[1,32,128]{2,1,0:T(8,128)S(1)} collective-permute-done((f32[1,32,128]{2,1,0:T(8,128)S(1)}, f32[1,32,128]{2,1,0:T(8,128)S(1)}, u32[]{:S(2)}, u32[]{:S(2)}) %collective-permute-start.24) | collective-permute-done | bytes 16416 | tf_op jit(solution)/shard_map/ppermute | solution.py:57
  79.8 1.5 %shard_map.127 = bf16[1024,2048]{1,0:T(8,128)(2,1)} custom-call(s32[2]{0:T(128)S(1)} %pad_add_fusion.me_ref, bf16[2,1024,128]{2,1,0:T(8,128)(2,1)S(1)} %collective-permute-done.26.refs_0_, bf16[1,1024,128]{2,1,0:T(8,128)(2,1)S(1)} %collective-permute-done.27.refs_1_, bf16[1024,2048]{1,0:T(8,128)(2,1)} %shard_map.123.refs_2_), custom_call_target="tpu_custom_call", output_to_operand_aliasing={{}: (3, {})} | custom-call | flops 1 | bytes 1 | tf_op jit(solution)/shard_map/pallas_call | solution.py:369
  (75 shorter events, 9.4 us)
Async XLA Ops:
  0.6 9.8 %copy-start.4 = (bf16[32,128]{1,0:T(8,128)(2,1)S(1)}, bf16[32,128]{1,0:T(8,128)(2,1)}, u32[]{:S(2)}) copy-start(bf16[32,128]{1,0:T(8,128)(2,1)} %param.9) | copy-start | bytes 24580
  0.6 9.6 %copy-start.5 = (s32[2]{0:T(128)S(1)}, s32[2]{0:T(128)}, u32[]{:S(2)}) copy-start(s32[2]{0:T(128)} %lengths_ref.1) | copy-start | bytes 28
  0.6 9.8 %collective-permute-start = (bf16[1,32,128]{2,1,0:T(8,128)(2,1)}, bf16[1,32,128]{2,1,0:T(8,128)(2,1)S(1)}, u32[]{:S(2)}, u32[]{:S(2)}) collective-permute-start(bf16[1,32,128]{2,1,0:T(8,128)(2,1)} %bitcast.6), channel_id=1, source_target_pairs={{0,4},{1,5},{2,6},{3,7},{4,0},{5,1},{6,2},{7,3},{8,12},{9,13},{10,... | collective-permute-start | bytes 24584 | tf_op jit(solution)/shard_map/ppermute | solution.py:57
  5.0 26.6 %collective-permute-start.6 = (bf16[2,1024,128]{2,1,0:T(8,128)(2,1)}, bf16[2,1024,128]{2,1,0:T(8,128)(2,1)S(1)}, u32[]{:S(2)}, u32[]{:S(2)}) collective-permute-start(bf16[2,1024,128]{2,1,0:T(8,128)(2,1)} %get-tuple-element.94), channel_id=1, source_target_pairs={{0,32},{8,40},{16,48},{24,56},{32,64},{40,72},{48,80},{56,88},{64,... | collective-permute-start | bytes 1572872 | tf_op jit(solution)/shard_map/ppermute | solution.py:62
  6.6 25.0 %collective-permute-start.7 = (bf16[2,1024,128]{2,1,0:T(8,128)(2,1)}, bf16[2,1024,128]{2,1,0:T(8,128)(2,1)S(1)}, u32[]{:S(2)}, u32[]{:S(2)}) collective-permute-start(bf16[2,1024,128]{2,1,0:T(8,128)(2,1)} %get-tuple-element.93), channel_id=1, source_target_pairs={{0,96},{8,104},{16,112},{24,120},{32,0},{40,8},{48,16},{56,24},{64... | collective-permute-start | bytes 1572872 | tf_op jit(solution)/shard_map/ppermute | solution.py:62
  8.3 24.0 %collective-permute-start.8 = (bf16[2,1024,128]{2,1,0:T(8,128)(2,1)S(1)}, bf16[2,1024,128]{2,1,0:T(8,128)(2,1)S(1)}, u32[]{:S(2)}, u32[]{:S(2)}) collective-permute-start(bf16[2,1024,128]{2,1,0:T(8,128)(2,1)S(1)} %get-tuple-element.92), channel_id=1, source_target_pairs={{0,64},{8,72},{16,80},{24,88},{32,96},{40,104},{48,112},{56,120},{... | collective-permute-start | bytes 1572872 | tf_op jit(solution)/shard_map/ppermute | solution.py:62
  10.5 17.4 %collective-permute-start.4 = (bf16[2,1024,128]{2,1,0:T(8,128)(2,1)}, bf16[2,1024,128]{2,1,0:T(8,128)(2,1)S(1)}, u32[]{:S(2)}, u32[]{:S(2)}) collective-permute-start(bf16[2,1024,128]{2,1,0:T(8,128)(2,1)} %get-tuple-element.52), channel_id=1, source_target_pairs={{0,16},{8,24},{16,0},{24,8},{32,48},{40,56},{48,32},{56,40},{64,80... | collective-permute-start | bytes 1572872 | tf_op jit(solution)/shard_map/ppermute | solution.py:57
  13.3 7.7 %copy-start.8 = (bf16[1024]{0:T(1024)(128)(2,1)S(1)}, bf16[1024]{0:T(1024)(128)(2,1)}, u32[]{:S(2)}) copy-start(bf16[1024]{0:T(1024)(128)(2,1)} %param.10) | copy-start | bytes 6148
  13.3 9.5 %copy-start.3 = (bf16[1024,256]{1,0:T(8,128)(2,1)S(1)}, bf16[1024,256]{1,0:T(8,128)(2,1)}, u32[]{:S(2)}) copy-start(bf16[1024,256]{1,0:T(8,128)(2,1)} %keyval_ref.1) | copy-start | bytes 1572868
  13.3 3.7 %collective-permute-start.1 = (bf16[2,32,128]{2,1,0:T(8,128)(2,1)S(1)}, bf16[2,32,128]{2,1,0:T(8,128)(2,1)S(1)}, u32[]{:S(2)}, u32[]{:S(2)}) collective-permute-start(bf16[2,32,128]{2,1,0:T(8,128)(2,1)S(1)} %shard_map.105.own_ref), channel_id=1, source_target_pairs={{0,1},{1,0},{2,3},{3,2},{4,5},{5,4},{6,7},{7,6},{8,9},{9,8},{10,11... | collective-permute-start | bytes 49160 | tf_op jit(solution)/shard_map/ppermute | solution.py:57
  17.1 5.8 %collective-permute-start.2 = (bf16[4,32,128]{2,1,0:T(8,128)(2,1)S(1)}, bf16[4,32,128]{2,1,0:T(8,128)(2,1)S(1)}, u32[]{:S(2)}, u32[]{:S(2)}) collective-permute-start(bf16[4,32,128]{2,1,0:T(8,128)(2,1)S(1)} %shard_map.106.near_ref), channel_id=1, source_target_pairs={{0,2},{1,3},{2,0},{3,1},{4,6},{5,7},{6,4},{7,5},{8,10},{9,11},{10,... | collective-permute-start | bytes 98312 | tf_op jit(solution)/shard_map/ppermute | solution.py:57
  26.5 1.5 %collective-permute-start.3 = (f32[16,2432]{1,0:T(8,128)S(1)}, f32[16,2432]{1,0:T(8,128)S(1)}, u32[]{:S(2)}, u32[]{:S(2)}) collective-permute-start(f32[16,2432]{1,0:T(8,128)S(1)} %get-tuple-element.51), channel_id=1, source_target_pairs={{0,8},{8,0},{16,24},{24,16},{32,40},{40,32},{48,56},{56,48},{64,72... | collective-permute-start | bytes 466952 | tf_op jit(solution)/shard_map/ppermute | solution.py:57
  28.0 6.8 %collective-permute-start.5 = (f32[8,2432]{1,0:T(8,128)S(1)}, f32[8,2432]{1,0:T(8,128)S(1)}, u32[]{:S(2)}, u32[]{:S(2)}) collective-permute-start(f32[8,2432]{1,0:T(8,128)S(1)} %get-tuple-element.56), channel_id=1, source_target_pairs={{0,16},{8,24},{16,0},{24,8},{32,48},{40,56},{48,32},{56,40},{64,80... | collective-permute-start | bytes 233480 | tf_op jit(solution)/shard_map/ppermute | solution.py:57
  28.8 21.7 %collective-permute-start.12 = (bf16[2,1024,128]{2,1,0:T(8,128)(2,1)S(1)}, bf16[2,1024,128]{2,1,0:T(8,128)(2,1)S(1)}, u32[]{:S(2)}, u32[]{:S(2)}) collective-permute-start(bf16[2,1024,128]{2,1,0:T(8,128)(2,1)S(1)} %get-tuple-element.64), channel_id=1, source_target_pairs={{0,16},{8,24},{16,0},{24,8},{32,48},{40,56},{48,32},{56,40},{64,80... | collective-permute-start | bytes 1572872 | tf_op jit(solution)/shard_map/ppermute | solution.py:57
  34.9 21.5 %collective-permute-start.15 = (bf16[5,1024,128]{2,1,0:T(8,128)(2,1)S(1)}, bf16[5,1024,128]{2,1,0:T(8,128)(2,1)S(1)}, u32[]{:S(2)}, u32[]{:S(2)}) collective-permute-start(bf16[5,1024,128]{2,1,0:T(8,128)(2,1)S(1)} %shard_map.114), channel_id=1, source_target_pairs={{0,8},{8,0},{16,24},{24,16},{32,40},{40,32},{48,56},{56,48},{64,72... | collective-permute-start | bytes 3932168 | tf_op jit(solution)/shard_map/ppermute | solution.py:57
  35.0 5.3 %collective-permute-start.9 = (f32[4,2432]{1,0:T(4,128)S(1)}, f32[4,2432]{1,0:T(4,128)S(1)}, u32[]{:S(2)}, u32[]{:S(2)}) collective-permute-start(f32[4,2432]{1,0:T(4,128)S(1)} %get-tuple-element.59), channel_id=1, source_target_pairs={{0,96},{8,104},{16,112},{24,120},{32,64},{40,72},{48,80},{56,88},{... | collective-permute-start | bytes 116744 | tf_op jit(solution)/shard_map/ppermute | solution.py:57
  36.2 14.3 %collective-permute-start.13 = (bf16[1,1024,128]{2,1,0:T(8,128)(2,1)S(1)}, bf16[1,1024,128]{2,1,0:T(8,128)(2,1)S(1)}, u32[]{:S(2)}, u32[]{:S(2)}) collective-permute-start(bf16[1,1024,128]{2,1,0:T(8,128)(2,1)S(1)} %shard_map.112), channel_id=1, source_target_pairs={{0,8},{8,0},{16,24},{24,16},{32,40},{40,32},{48,56},{56,48},{64,72... | collective-permute-start | bytes 786440 | tf_op jit(solution)/shard_map/ppermute | solution.py:57
  36.5 19.9 %collective-permute-start.14 = (bf16[2,1024,128]{2,1,0:T(8,128)(2,1)S(1)}, bf16[2,1024,128]{2,1,0:T(8,128)(2,1)S(1)}, u32[]{:S(2)}, u32[]{:S(2)}) collective-permute-start(bf16[2,1024,128]{2,1,0:T(8,128)(2,1)S(1)} %get-tuple-element.67), channel_id=1, source_target_pairs={{0,16},{8,24},{16,0},{24,8},{32,48},{40,56},{48,32},{56,40},{64,80... | collective-permute-start | bytes 1572872 | tf_op jit(solution)/shard_map/ppermute | solution.py:57
  40.3 3.9 %collective-permute-start.10 = (f32[2,2432]{1,0:T(2,128)S(1)}, f32[2,2432]{1,0:T(2,128)S(1)}, u32[]{:S(2)}, u32[]{:S(2)}) collective-permute-start(f32[2,2432]{1,0:T(2,128)S(1)} %get-tuple-element.61), channel_id=1, source_target_pairs={{0,32},{8,40},{16,48},{24,56},{32,0},{40,8},{48,16},{56,24},{64,96... | collective-permute-start | bytes 58376 | tf_op jit(solution)/shard_map/ppermute | solution.py:57
  46.8 3.7 %collective-permute-start.11 = (bf16[2,2048]{1,0:T(2,128)(2,1)S(1)}, bf16[2,2048]{1,0:T(2,128)(2,1)S(1)}, u32[]{:S(2)}, u32[]{:S(2)}) collective-permute-start(bf16[2,2048]{1,0:T(2,128)(2,1)S(1)} %shard_map.111.own_ref), channel_id=1, source_target_pairs={{0,32},{8,40},{16,48},{24,56},{32,0},{40,8},{48,16},{56,24},{64,96... | collective-permute-start | bytes 24584 | tf_op jit(solution)/shard_map/ppermute | solution.py:57
  50.5 5.9 %collective-permute-start.16 = (bf16[4,2048]{1,0:T(4,128)(2,1)S(1)}, bf16[4,2048]{1,0:T(4,128)(2,1)S(1)}, u32[]{:S(2)}, u32[]{:S(2)}) collective-permute-start(bf16[4,2048]{1,0:T(4,128)(2,1)S(1)} %shard_map.113.own_ref), channel_id=1, source_target_pairs={{0,96},{8,104},{16,112},{24,120},{32,64},{40,72},{48,80},{56,88},{... | collective-permute-start | bytes 49160 | tf_op jit(solution)/shard_map/ppermute | solution.py:57
  51.7 17.2 %collective-permute-start.20 = (bf16[2,1024,128]{2,1,0:T(8,128)(2,1)S(1)}, bf16[2,1024,128]{2,1,0:T(8,128)(2,1)S(1)}, u32[]{:S(2)}, u32[]{:S(2)}) collective-permute-start(bf16[2,1024,128]{2,1,0:T(8,128)(2,1)S(1)} %shard_map.118), channel_id=1, source_target_pairs={{0,32},{8,40},{16,48},{24,56},{32,64},{40,72},{48,80},{56,88},{64,... | collective-permute-start | bytes 1572872 | tf_op jit(solution)/shard_map/ppermute | solution.py:62
  51.8 17.1 %collective-permute-start.21 = (bf16[2,1024,128]{2,1,0:T(8,128)(2,1)S(1)}, bf16[2,1024,128]{2,1,0:T(8,128)(2,1)S(1)}, u32[]{:S(2)}, u32[]{:S(2)}) collective-permute-start(bf16[2,1024,128]{2,1,0:T(8,128)(2,1)S(1)} %collective-permute-done.12), channel_id=1, source_target_pairs={{0,96},{8,104},{16,112},{24,120},{32,0},{40,8},{48,16},{56,24},{64... | collective-permute-start | bytes 1572872 | tf_op jit(solution)/shard_map/ppermute | solution.py:62
  56.5 5.6 %collective-permute-start.25 = (bf16[1,1024,128]{2,1,0:T(8,128)(2,1)S(1)}, bf16[1,1024,128]{2,1,0:T(8,128)(2,1)S(1)}, u32[]{:S(2)}, u32[]{:S(2)}) collective-permute-start(bf16[1,1024,128]{2,1,0:T(8,128)(2,1)S(1)} %shard_map.124), channel_id=1, source_target_pairs={{0,8},{8,0},{16,24},{24,16},{32,40},{40,32},{48,56},{56,48},{64,72... | collective-permute-start | bytes 786440 | tf_op jit(solution)/shard_map/ppermute | solution.py:57
  56.6 5.5 %collective-permute-start.17 = (bf16[8,2048]{1,0:T(8,128)(2,1)S(1)}, bf16[8,2048]{1,0:T(8,128)(2,1)S(1)}, u32[]{:S(2)}, u32[]{:S(2)}) collective-permute-start(bf16[8,2048]{1,0:T(8,128)(2,1)S(1)} %shard_map.115.own_ref), channel_id=1, source_target_pairs={{0,16},{8,24},{16,0},{24,8},{32,48},{40,56},{48,32},{56,40},{64,80... | collective-permute-start | bytes 98312 | tf_op jit(solution)/shard_map/ppermute | solution.py:57
  58.3 17.1 %collective-permute-start.23 = (bf16[2,1024,128]{2,1,0:T(8,128)(2,1)S(1)}, bf16[2,1024,128]{2,1,0:T(8,128)(2,1)S(1)}, u32[]{:S(2)}, u32[]{:S(2)}) collective-permute-start(bf16[2,1024,128]{2,1,0:T(8,128)(2,1)S(1)} %shard_map.120), channel_id=1, source_target_pairs={{0,16},{8,24},{16,0},{24,8},{32,48},{40,56},{48,32},{56,40},{64,80... | collective-permute-start | bytes 1572872 | tf_op jit(solution)/shard_map/ppermute | solution.py:57
  62.1 1.7 %collective-permute-start.18 = (bf16[16,2048]{1,0:T(8,128)(2,1)S(1)}, bf16[16,2048]{1,0:T(8,128)(2,1)S(1)}, u32[]{:S(2)}, u32[]{:S(2)}) collective-permute-start(bf16[16,2048]{1,0:T(8,128)(2,1)S(1)} %shard_map.116.own_ref), channel_id=1, source_target_pairs={{0,8},{8,0},{16,24},{24,16},{32,40},{40,32},{48,56},{56,48},{64,72... | collective-permute-start | bytes 196616 | tf_op jit(solution)/shard_map/ppermute | solution.py:57
  62.2 17.6 %collective-permute-start.26 = (bf16[2,1024,128]{2,1,0:T(8,128)(2,1)S(1)}, bf16[2,1024,128]{2,1,0:T(8,128)(2,1)S(1)}, u32[]{:S(2)}, u32[]{:S(2)}) collective-permute-start(bf16[2,1024,128]{2,1,0:T(8,128)(2,1)S(1)} %shard_map.125), channel_id=1, source_target_pairs={{0,64},{8,72},{16,80},{24,88},{32,96},{40,104},{48,112},{56,120},{... | collective-permute-start | bytes 1572872 | tf_op jit(solution)/shard_map/ppermute | solution.py:62
  65.3 6.1 %collective-permute-start.19 = (f32[4,32,128]{2,1,0:T(8,128)S(1)}, f32[4,32,128]{2,1,0:T(8,128)S(1)}, u32[]{:S(2)}, u32[]{:S(2)}) collective-permute-start(f32[4,32,128]{2,1,0:T(8,128)S(1)} %get-tuple-element.75), channel_id=1, source_target_pairs={{0,2},{1,3},{2,0},{3,1},{4,6},{5,7},{6,4},{7,5},{8,10},{9,11},{10,... | collective-permute-start | bytes 196616 | tf_op jit(solution)/shard_map/ppermute | solution.py:57
  71.4 4.0 %collective-permute-start.22 = (f32[2,32,128]{2,1,0:T(8,128)S(1)}, f32[2,32,128]{2,1,0:T(8,128)S(1)}, u32[]{:S(2)}, u32[]{:S(2)}) collective-permute-start(f32[2,32,128]{2,1,0:T(8,128)S(1)} %get-tuple-element.80), channel_id=1, source_target_pairs={{0,1},{1,0},{2,3},{3,2},{4,5},{5,4},{6,7},{7,6},{8,9},{9,8},{10,11... | collective-permute-start | bytes 98312 | tf_op jit(solution)/shard_map/ppermute | solution.py:57
  72.9 7.0 %collective-permute-start.27 = (bf16[1,1024,128]{2,1,0:T(8,128)(2,1)S(1)}, bf16[1,1024,128]{2,1,0:T(8,128)(2,1)S(1)}, u32[]{:S(2)}, u32[]{:S(2)}) collective-permute-start(bf16[1,1024,128]{2,1,0:T(8,128)(2,1)S(1)} %shard_map.126), channel_id=1, source_target_pairs={{0,8},{8,0},{16,24},{24,16},{32,40},{40,32},{48,56},{56,48},{64,72... | collective-permute-start | bytes 786440 | tf_op jit(solution)/shard_map/ppermute | solution.py:57
  75.4 3.8 %collective-permute-start.24 = (f32[1,32,128]{2,1,0:T(8,128)S(1)}, f32[1,32,128]{2,1,0:T(8,128)S(1)}, u32[]{:S(2)}, u32[]{:S(2)}) collective-permute-start(f32[1,32,128]{2,1,0:T(8,128)S(1)} %get-tuple-element.84), channel_id=1, source_target_pairs={{0,4},{1,5},{2,6},{3,7},{4,0},{5,1},{6,2},{7,3},{8,12},{9,13},{10,... | collective-permute-start | bytes 49160 | tf_op jit(solution)/shard_map/ppermute | solution.py:57
  (5 other events, 19.4 us)

commit v3 on v2

--- a/solution.py
+++ b/solution.py
@@ -17,7 +17,6 @@
 
 COST = 1_000_000_000
 VMEM = pl.BlockSpec(memory_space=pltpu.VMEM)
-SMEM = pl.BlockSpec(memory_space=pltpu.SMEM)
 HBM = pl.BlockSpec(memory_space=pltpu.HBM)
 ANYWHERE = pl.BlockSpec(memory_space=pl.ANY)
 
@@ -111,8 +110,8 @@
     return number ^ (number >> 1)
 
 
-def batch_row(me_ref, place):
-    row = me_ref[0]
+def batch_row(place):
+    row = lax.axis_index("row")
     y, x_half, core = row >> 2, (row >> 1) & 1, row & 1
     device = (
         ((y ^ gray((place >> 1) & 3)) << 2)
@@ -123,17 +122,17 @@
 
 
 def project_kernel(
-    me_ref, near_ref, far_ref, gain_ref, query_ref, keyval_ref, kept_ref, sent_ref, feats_scr
+    near_ref, far_ref, gain_ref, query_ref, keyval_ref, kept_ref, sent_ref, feats_scr
 ):
     half, rows = near_ref.shape[0], near_ref.shape[1]
     feats_scr[:half] = near_ref[...]
     feats_scr[half:] = far_ref[...]
-    x_low, z = me_ref[1] >> 2, me_ref[1] & 3
+    x_low, z = lax.axis_index("col") >> 2, lax.axis_index("col") & 3
     blocks = [
         feats_scr[((part & 3) ^ z) * 2 + ((part >> 2) ^ x_low)] for part in range(2 * half)
     ]
     shape = (rows, rows)
-    order = batch_row(me_ref, lax.broadcasted_iota(jnp.int32, shape, 0))
+    order = batch_row(lax.broadcasted_iota(jnp.int32, shape, 0))
     order = jnp.where(order == lax.broadcasted_iota(jnp.int32, shape, 1), 1.0, 0.0)
     feats = jnp.dot(
         order.astype(jnp.bfloat16),
@@ -162,17 +161,17 @@
     put(columns + keyval_ref.shape[1], jnp.broadcast_to(square_sum, (rows, SQUARES)))
 
 
-def project(me, near, far, gain, query_weight, keyval_weight):
+def project(near, far, gain, query_weight, keyval_weight):
     rows = near.shape[1]
     columns = query_weight.shape[1] + keyval_weight.shape[1] + SQUARES
     half = jax.ShapeDtypeStruct((rows // 2, columns), jnp.float32)
     return call(
         project_kernel,
         [half, half],
-        [SMEM] + [VMEM] * 5,
+        [VMEM] * 5,
         [VMEM] * 2,
         [pltpu.VMEM((2 * near.shape[0],) + near.shape[1:], near.dtype)],
-    )(me, near, far, gain[None], query_weight, keyval_weight)
+    )(near, far, gain[None], query_weight, keyval_weight)
 
 
 def attend_kernel(
@@ -224,7 +223,7 @@
                 * scale
             )
             place = start + lax.broadcasted_iota(jnp.int32, scores.shape, 1)
-            scores = jnp.where(place < lengths_ref[b], scores, masked_score)
+            scores = jnp.where(place < lengths_ref[b : b + 1, :1], scores, masked_score)
             score_scr[b, :, start : start + CHUNK] = scores
             tops[b] = jnp.maximum(tops[b], scores)
     sums, numers = [], []
@@ -254,7 +253,7 @@
     return call(
         functools.partial(attend_kernel, features),
         jax.ShapeDtypeStruct((rows, heads * head_dim), jnp.bfloat16),
-        [SMEM] + [VMEM] * 6,
+        [VMEM] * 7,
         VMEM,
         [
             pltpu.VMEM(kept.shape, jnp.float32),
@@ -262,56 +261,57 @@
             pltpu.VMEM((rows, heads, positions), jnp.float32),
             pltpu.VMEM((rows, heads * head_dim), jnp.float32),
         ],
+        cost=2.2,
     )(lengths, kept, got, cosine, sine, key_cache, value_cache)
 
 
-def mix_kernel(me_ref, own_ref, other_ref, weight_ref, kept_ref, sent_ref, blocks_scr):
+def mix_kernel(own_ref, other_ref, weight_ref, kept_ref, sent_ref, blocks_scr):
     rows = 2 * own_ref.shape[0]
     shape = (rows, rows)
-    order = batch_row(me_ref, lax.broadcasted_iota(jnp.int32, shape, 1))
+    order = batch_row(lax.broadcasted_iota(jnp.int32, shape, 1))
     order = jnp.where(order == lax.broadcasted_iota(jnp.int32, shape, 0), 1.0, 0.0)
     attended = jnp.dot(
         order.astype(jnp.bfloat16),
         jnp.concatenate([own_ref[...], other_ref[...]], axis=0),
         preferred_element_type=jnp.float32,
     ).astype(jnp.bfloat16)
-    x_low, z = me_ref[1] >> 2, me_ref[1] & 3
     step, width = 256, kept_ref.shape[2]
     for start in range(0, weight_ref.shape[1], step):
         mixed = jnp.dot(
             attended, weight_ref[:, start : start + step], preferred_element_type=jnp.float32
         )
         for k in range(step // width):
-            part = start // width + k
-            place = ((part & 3) ^ z) * 2 + ((part >> 2) ^ x_low)
-            blocks_scr[place] = mixed[:, k * width : (k + 1) * width]
+            blocks_scr[start // width + k] = mixed[:, k * width : (k + 1) * width]
+    x_low, z = lax.axis_index("col") >> 2, lax.axis_index("col") & 3
     half = kept_ref.shape[0]
-    kept_ref[...] = blocks_scr[:half]
-    sent_ref[...] = blocks_scr[half:]
-
-
-def mix(me, own, other, out_weight):
+    for place in range(half):
+        kept_ref[place] = blocks_scr[((x_low ^ (place & 1)) << 2) | (z ^ (place >> 1))]
+        away = place + half
+        sent_ref[place] = blocks_scr[((x_low ^ (away & 1)) << 2) | (z ^ (away >> 1))]
+
+
+def mix(own, other, out_weight):
     rows, width = 2 * own.shape[0], out_weight.shape[1] // 8
     half = jax.ShapeDtypeStruct((4, rows, width), jnp.float32)
     return call(
         mix_kernel,
         [half, half],
-        [SMEM] + [VMEM] * 3,
+        [VMEM] * 3,
         [VMEM] * 2,
         [pltpu.VMEM((8, rows, width), jnp.float32)],
         cost=2.2,
-    )(me, own, other, out_weight)
+    )(own, other, out_weight)
 
 
 SAME, OTHER = "same", "other"
 
 
-def pick(piece_ref, slot):
+def pick(piece_ref, slot, base=0):
     if slot == SAME:
-        return piece_ref.at[lax.axis_index("row") & 1]
-    if slot == OTHER:
-        return piece_ref.at[(lax.axis_index("row") & 1) ^ 1]
-    return piece_ref.at[slot]
+        slot = lax.axis_index("row") & 1
+    elif slot == OTHER:
+        slot = (lax.axis_index("row") & 1) ^ 1
+    return piece_ref.at[base + slot]
 
 
 def start_and_wait(copies):
@@ -331,8 +331,8 @@
     pieces, out_ref, sems = refs[:count], refs[-2], refs[-1]
     start_and_wait(
         [
-            pltpu.make_async_copy(pick(pieces[p], i), out_ref.at[k], sems.at[k])
-            for k, (p, i) in enumerate(slots)
+            pltpu.make_async_copy(pick(pieces[p], *at), out_ref.at[k], sems.at[k])
+            for k, (p, *at) in enumerate(slots)
         ]
     )
 
@@ -348,9 +348,9 @@
     )(*pieces)
 
 
-def place_kernel(count, slots, me_ref, *refs):
+def place_kernel(count, slots, *refs):
     pieces, relaid_ref, sems = refs[:count], refs[-2], refs[-1]
-    row = me_ref[0]
+    row = lax.axis_index("row")
     copies = []
     for k, (piece, slot, dy, dx, other) in enumerate(slots):
         chip = ((((row >> 2) - dy) & 3) << 1) | (((row >> 1) & 1) ^ dx)
@@ -363,18 +363,18 @@
     start_and_wait(copies)
 
 
-def place(me, pieces, slots, relaid):
+def place(pieces, slots, relaid):
     rows, width = pieces[0].shape[1:]
     first = relaid is None
     return call(
         functools.partial(place_kernel, len(pieces), slots),
         jax.ShapeDtypeStruct((rows, 16 * width), jnp.bfloat16),
-        [SMEM] + [VMEM] * len(pieces) + ([] if first else [HBM]),
+        [VMEM] * len(pieces) + ([] if first else [HBM]),
         HBM,
         [pltpu.SemaphoreType.DMA((len(slots),))],
         6,
-        input_output_aliases={} if first else {len(pieces) + 1: 0},
-    )(me, *pieces, *([] if first else [relaid]))
+        input_output_aliases={} if first else {len(pieces): 0},
+    )(*pieces, *([] if first else [relaid]))
 
 
 def body(
@@ -390,19 +390,21 @@
 ):
     heads = query_weight.shape[1] // HD
     features = query_weight.shape[0] * lax.axis_size("row")
-    me = jnp.stack([lax.axis_index("row"), lax.axis_index("col")]).astype(jnp.int32)
     cosine, sine = rotary_factors(lengths, HD)
+    lengths = jnp.broadcast_to(lengths[:, None], cosine.shape)
     chunks = next_query.reshape(16, -1, next_query.shape[1])
 
     def pair(dy, dx):
         return [(dy, dx, 0), (dy, dx, 1)]
 
-    to_a, to_b, to_c, to_e = [chip_pair(chunks, *at) for at in ((1, 0), (3, 0), (2, 0), (1, 1))]
+    to_a, to_b, to_c, to_e = [
+        chip_pair(chunks, *at) for at in ((1, 0), (3, 0), (2, 0), (1, 1))
+    ]
     got_a, got_b, got_c = shift_y(to_a, 1), shift_y(to_b, 3), shift_y(to_c, 2)
 
     other = flip(tokens[None], "col", X_LOW)
     feats = fetch(tokens[None])
-    other, feats, to_e, cosine, sine = tie(other, feats, to_e, cosine, sine)
+    other, feats, to_e, cosine, sine, lengths = tie(other, feats, to_e, cosine, sine, lengths)
     via_e = flip(to_e, "row", X_HALF)
     feats = join(feats, other, 3)
     other = flip(feats, "col", Z_NEAR)
@@ -410,46 +412,44 @@
     own, to_d, to_f, to_g = [chip_pair(chunks, *at) for at in ((0, 0), (0, 1), (3, 1), (2, 1))]
     feats = join(feats, other, 1.2)
     other = flip(feats, "col", Z_FAR)
-    kept, sent = project(me, feats, other, norm_gain, query_weight, keyval_weight)
+    kept, sent = project(feats, other, norm_gain, query_weight, keyval_weight)
     got = flip(sent, "row", CORE)
     got, via_e, own, to_d, to_f, to_g = tie(got, via_e, own, to_d, to_f, to_g)
     kept, sent = add_halves(kept, got)
     got = flip(sent, "row", X_HALF)
     via_f = flip(to_f, "row", X_HALF)
     got, got_a, got_b, got_c = tie(got, got_a, got_b, got_c)
-    swap_first = pack([own, got_a, got_b, got_c, to_d], [(k, OTHER) for k in range(5)])
-    swap_first = flip(swap_first, "row", CORE)
-    kept, sent = add_halves(kept, got, 8)
+    swapped = pack(
+        [own, got_a, got_b, got_c, to_d, via_e, to_g], [(k, OTHER) for k in range(7)]
+    )
+    swapped = flip(swapped, "row", CORE)
+    kept, sent = add_halves(kept, got, 26)
     got = flip(sent, "row", Y_FAR)
-    via_g = flip(to_g, "row", X_HALF)
-    swap_e = flip(pack([via_e], [(0, OTHER)]), "row", CORE)
-    kept, sent = add_halves(kept, got, 3)
+    kept, sent = add_halves(kept, got)
     got = flip(sent, "row", Y_NEAR)
+    via_g = flip(pack([to_g, swapped], [(0, SAME), (1, 6)]), "row", X_HALF)
     attended = attend(
         lengths, kept, got, cosine, sine, key_cache, value_cache, features, heads
     )
     other = flip(attended, "row", Y_NEAR)
-    other, via_f, swap_e = tie(other, via_f, swap_e)
-    via_e = pack([via_e, swap_e], [(0, SAME), (1, 0)])
+    other, via_f = tie(other, via_f)
+    via_e = pack([via_e, swapped], [(0, SAME), (1, 5)])
     attended = join(attended, other, 3)
     other = flip(attended, "row", Y_FAR)
     got_e, got_f = shift_y(via_e, 1), shift_y(via_f, 3)
-    via_g, swap_first, other = tie(via_g, swap_first, other)
-    swap_g = flip(pack([via_g], [(0, OTHER)]), "row", CORE)
+    via_g, other = tie(via_g, other)
     attended = join(attended, other, 4.5)
     other = flip(attended, "row", X_HALF)
-    got_d = flip(pack([to_d, swap_first], [(0, SAME), (1, 4)]), "row", X_HALF)
+    got_d = flip(pack([to_d, swapped], [(0, SAME), (1, 4)]), "row", X_HALF)
     attended = join(attended, other, 1.2)
     other = flip(attended, "row", CORE)
     relaid = place(
-        me,
-        [own, got_a, got_b, got_c, swap_first],
+        [own, got_a, got_b, got_c, swapped],
         [(k, SAME, dy, 0, 0) for k, dy in enumerate((0, 1, 3, 2))]
         + [(4, k, dy, 0, 1) for k, dy in enumerate((0, 1, 3, 2))],
         None,
     )
-    kept, sent = mix(me, attended, other, out_weight)
-    via_g = pack([via_g, swap_g], [(0, SAME), (1, 0)])
+    kept, sent = mix(attended, other, out_weight)
     got = flip(sent, "col", Z_FAR)
     got_g = shift_y(via_g, 2)
     got, got_e, got_f = tie(got, got_e, got_f)
@@ -460,7 +460,6 @@
     kept, sent = add_halves(kept, got)
     got = flip(sent, "col", X_LOW)
     relaid = place(
-        me,
         [got_d, got_e, got_f],
         [(0, 0, 0, 1, 0), (1, 0, 1, 1, 0), (2, SAME, 3, 1, 0), (0, 1, 0, 1, 1), (1, 1, 1, 1, 1)],
         relaid,
@@ -468,7 +467,6 @@
     got, relaid = tie(got, relaid)
     mixed = (kept + got)[0].astype(jnp.bfloat16)
     relaid = place(
-        me,
         [got_g, swap_last],
         [(0, 0, 2, 1, 0), (0, 1, 2, 1, 1), (1, 0, 3, 1, 1)],
         relaid,

time: 81.5 us -> 79.9 us (0.980)
  Pallas kernels: 11.1 us -> 7.89 us
  waiting for transfers between devices: 25.5 us -> 28.2 us
  starting transfers between devices: 37.1 us -> 35.6 us
    ppermute x22 -> x20, waiting for transfers between devices: 24.8 us -> 26.9 us  [flip(): return lax.ppermute(block, axis, [(i, i ^ bits) for i in range(size)])]
    pallas_call x3, Pallas kernels: 5.02 us -> 3.38 us  [place(): call(functools.partial(place_kernel, len(pieces), slots), jax.ShapeDtypeS...]
    pallas_call x2, Pallas kernels: 2.93 us -> 1.85 us  [the longest x1 0.94 us: mix(): call(mix_kernel, [half, half], [VMEM] * 3, [VMEM] * 2, [pltpu.VMEM((8, ro...]
    ppermute x6, starting transfers between devices: 10.1 us -> 9.16 us  [shift_y(): lax.ppermute(block, 'row', [(i, (i + 4 * steps) % size) for i in range(si...]
    ppermute x22 -> x20, starting transfers between devices: 27 us -> 26.4 us  [flip(): return lax.ppermute(block, axis, [(i, i ^ bits) for i in range(size)])]
  transfers between devices with their start and end apart: 28 -> 26, of which waited for: 13 -> 13; matrix products, arithmetic and copies ran while one was open for 5% -> 5% of each run, Pallas kernels for 12% -> 9%
where the time goes in v3:
time: 79.9 us; the launch traced here: 79.7 us
  starting transfers between devices  35.6 us (45%)
  waiting for transfers between devices  28.2 us (35%)
  Pallas kernels  7.89 us (10%)
  local copies, waits for them, and re-layouts  6.35 us (8%)
  between operations  0.9 us (1%)
  other arithmetic  0.8 us (1%)
    ppermute x20, waiting for transfers between devices, flip(): return lax.ppermute(block, axis, [(i, i ^ bits) for i in range(size)])  26.9 us
    ppermute x20, starting transfers between devices, flip(): return lax.ppermute(block, axis, [(i, i ^ bits) for i in range(size)])  26.4 us
    ppermute x6, starting transfers between devices, shift_y(): lax.ppermute(block, 'row', [(i, (i + 4 * steps) % size) for i in range(si...  9.16 us
    unnamed x18, local copies, waits for them, and re-layouts  3.4 us
    pallas_call x3, Pallas kernels, place(): call(functools.partial(place_kernel, len(pieces), slots), jax.ShapeDtypeS...  3.38 us
    dynamic_slice x2, local copies, waits for them, and re-layouts, chip_pair(): return lax.dynamic_slice_in_dim(chunks, chip * 2, 2, 0)  2.87 us
    pallas_call x1, Pallas kernels, attend(): call(functools.partial(attend_kernel, features), jax.ShapeDtypeStruct((ro...  2.12 us
  transfers between devices with their start and end apart: 26, of which 13 were waited for; matrix products, arithmetic and copies ran while one was open for 5% of the time, Pallas kernels for 9%

profile of v3, /device:TPU:0, one launch (start us, length us, event | category | flops | bytes accessed | tf_op | source)
XLA Modules:
  0.0 79.7 jit_solution(4851181591014359605)
XLA Ops:
  0.6 1.7 %collective-permute-start = (bf16[1,32,128]{2,1,0:T(8,128)(2,1)}, bf16[1,32,128]{2,1,0:T(8,128)(2,1)S(1)}, u32[]{:S(2)}, u32[]{:S(2)}) collective-permute-start(bf16[1,32,128]{2,1,0:T(8,128)(2,1)} %bitcast.4), channel_id=1, source_target_pairs={{0,4},{1,5},{2,6},{3,7},{4,0},{5,1},{6,2},{7,3},{8,12},{9,13},{10,... | collective-permute-start | bytes 24584 | tf_op jit(solution)/shard_map/ppermute | solution.py:56
  2.3 2.7 %constant_dynamic-slice_fusion = (bf16[2,1024,128]{2,1,0:T(8,128)(2,1)S(1)}, bf16[2,1024,128]{2,1,0:T(8,128)(2,1)}, bf16[2,1024,128]{2,1,0:T(8,128)(2,1)}, bf16[2,1024,128]{2,1,0:T(8,128)(2,1)}) fusion(bf16[16,1024,128]{2,1,0:T(8,128)(2,1)} %bitcast.6, s32[]{:T(128)S(6)} %select_n.31, s32[]{:T(128)S(6)} %select_n.30, s32[]{:T(128)S(6)} %select_n.29, ...), kind=kLoop, calls=%fused_computation.2 | loop fusion | bytes 4194320 | tf_op jit(solution)/shard_map/dynamic_slice | solution.py:327
  5.0 1.6 %collective-permute-start.6 = (bf16[2,1024,128]{2,1,0:T(8,128)(2,1)}, bf16[2,1024,128]{2,1,0:T(8,128)(2,1)S(1)}, u32[]{:S(2)}, u32[]{:S(2)}) collective-permute-start(bf16[2,1024,128]{2,1,0:T(8,128)(2,1)} %get-tuple-element.92), channel_id=1, source_target_pairs={{0,32},{8,40},{16,48},{24,56},{32,64},{40,72},{48,80},{56,88},{64,... | collective-permute-start | bytes 1572872 | tf_op jit(solution)/shard_map/ppermute | solution.py:61
  6.6 1.7 %collective-permute-start.7 = (bf16[2,1024,128]{2,1,0:T(8,128)(2,1)}, bf16[2,1024,128]{2,1,0:T(8,128)(2,1)S(1)}, u32[]{:S(2)}, u32[]{:S(2)}) collective-permute-start(bf16[2,1024,128]{2,1,0:T(8,128)(2,1)} %get-tuple-element.91), channel_id=1, source_target_pairs={{0,96},{8,104},{16,112},{24,120},{32,0},{40,8},{48,16},{56,24},{64... | collective-permute-start | bytes 1572872 | tf_op jit(solution)/shard_map/ppermute | solution.py:61
  8.3 2.0 %collective-permute-start.8 = (bf16[2,1024,128]{2,1,0:T(8,128)(2,1)S(1)}, bf16[2,1024,128]{2,1,0:T(8,128)(2,1)S(1)}, u32[]{:S(2)}, u32[]{:S(2)}) collective-permute-start(bf16[2,1024,128]{2,1,0:T(8,128)(2,1)S(1)} %get-tuple-element.90), channel_id=1, source_target_pairs={{0,64},{8,72},{16,80},{24,88},{32,96},{40,104},{48,112},{56,120},{... | collective-permute-start | bytes 1572872 | tf_op jit(solution)/shard_map/ppermute | solution.py:61
  10.6 2.8 %collective-permute-start.4 = (bf16[2,1024,128]{2,1,0:T(8,128)(2,1)}, bf16[2,1024,128]{2,1,0:T(8,128)(2,1)S(1)}, u32[]{:S(2)}, u32[]{:S(2)}) collective-permute-start(bf16[2,1024,128]{2,1,0:T(8,128)(2,1)} %get-tuple-element.52), channel_id=1, source_target_pairs={{0,16},{8,24},{16,0},{24,8},{32,48},{40,56},{48,32},{56,40},{64,80... | collective-permute-start | bytes 1572872 | tf_op jit(solution)/shard_map/ppermute | solution.py:56
  13.3 1.9 %collective-permute-start.1 = (bf16[2,32,128]{2,1,0:T(8,128)(2,1)S(1)}, bf16[2,32,128]{2,1,0:T(8,128)(2,1)S(1)}, u32[]{:S(2)}, u32[]{:S(2)}) collective-permute-start(bf16[2,32,128]{2,1,0:T(8,128)(2,1)S(1)} %shard_map.105.own_ref), channel_id=1, source_target_pairs={{0,1},{1,0},{2,3},{3,2},{4,5},{5,4},{6,7},{7,6},{8,9},{9,8},{10,11... | collective-permute-start | bytes 49160 | tf_op jit(solution)/shard_map/ppermute | solution.py:56
  15.2 1.8 %collective-permute-done.1.other_ref = bf16[2,32,128]{2,1,0:T(8,128)(2,1)S(1)} collective-permute-done((bf16[2,32,128]{2,1,0:T(8,128)(2,1)S(1)}, bf16[2,32,128]{2,1,0:T(8,128)(2,1)S(1)}, u32[]{:S(2)}, u32[]{:S(2)}) %collective-permute-start.1) | collective-permute-done | bytes 16416 | tf_op jit(solution)/shard_map/ppermute | solution.py:56
  17.1 3.9 %collective-permute-start.2 = (bf16[4,32,128]{2,1,0:T(8,128)(2,1)S(1)}, bf16[4,32,128]{2,1,0:T(8,128)(2,1)S(1)}, u32[]{:S(2)}, u32[]{:S(2)}) collective-permute-start(bf16[4,32,128]{2,1,0:T(8,128)(2,1)S(1)} %shard_map.106.near_ref), channel_id=1, source_target_pairs={{0,2},{1,3},{2,0},{3,1},{4,6},{5,7},{6,4},{7,5},{8,10},{9,11},{10,... | collective-permute-start | bytes 98312 | tf_op jit(solution)/shard_map/ppermute | solution.py:56
  21.0 1.9 %collective-permute-done.2.far_ref = bf16[4,32,128]{2,1,0:T(8,128)(2,1)S(1)} collective-permute-done((bf16[4,32,128]{2,1,0:T(8,128)(2,1)S(1)}, bf16[4,32,128]{2,1,0:T(8,128)(2,1)S(1)}, u32[]{:S(2)}, u32[]{:S(2)}) %collective-permute-start.2) | collective-permute-done | bytes 32800 | tf_op jit(solution)/shard_map/ppermute | solution.py:56
  22.8 2.2 %copy-done = bf16[1024,2048]{1,0:T(8,128)(2,1)S(1)} copy-done((bf16[1024,2048]{1,0:T(8,128)(2,1)S(1)}, bf16[1024,2048]{1,0:T(8,128)(2,1)}, u32[]{:S(2)}) %copy-start) | copy-done | bytes 4194328
  26.0 1.2 %copy-done.6 = bf16[16384,128]{1,0:T(8,128)(2,1)S(1)} copy-done((bf16[16384,128]{1,0:T(8,128)(2,1)S(1)}, bf16[16384,128]{1,0:T(8,128)(2,1)}, u32[]{:S(2)}) %copy-start.6) | copy-done | bytes 4194328
  28.3 2.7 %collective-permute-start.12 = (bf16[2,1024,128]{2,1,0:T(8,128)(2,1)S(1)}, bf16[2,1024,128]{2,1,0:T(8,128)(2,1)S(1)}, u32[]{:S(2)}, u32[]{:S(2)}) collective-permute-start(bf16[2,1024,128]{2,1,0:T(8,128)(2,1)S(1)} %get-tuple-element.64), channel_id=1, source_target_pairs={{0,16},{8,24},{16,0},{24,8},{32,48},{40,56},{48,32},{56,40},{64,80... | collective-permute-start | bytes 1572872 | tf_op jit(solution)/shard_map/ppermute | solution.py:56
  31.1 1.3 %collective-permute-done.8.refs_3_ = bf16[2,1024,128]{2,1,0:T(8,128)(2,1)S(1)} collective-permute-done((bf16[2,1024,128]{2,1,0:T(8,128)(2,1)S(1)}, bf16[2,1024,128]{2,1,0:T(8,128)(2,1)S(1)}, u32[]{:S(2)}, u32[]{:S(2)}) %collective-permute-start.8) | collective-permute-done | bytes 524320 | tf_op jit(solution)/shard_map/ppermute | solution.py:61
  32.3 1.9 %collective-permute-done.5.got_ref = f32[8,2432]{1,0:T(8,128)S(1)} collective-permute-done((f32[8,2432]{1,0:T(8,128)S(1)}, f32[8,2432]{1,0:T(8,128)S(1)}, u32[]{:S(2)}, u32[]{:S(2)}) %collective-permute-start.5) | collective-permute-done | bytes 77856 | tf_op jit(solution)/shard_map/ppermute | solution.py:56
  34.6 1.1 %collective-permute-start.9 = (f32[4,2432]{1,0:T(4,128)S(1)}, f32[4,2432]{1,0:T(4,128)S(1)}, u32[]{:S(2)}, u32[]{:S(2)}) collective-permute-start(f32[4,2432]{1,0:T(4,128)S(1)} %get-tuple-element.59), channel_id=1, source_target_pairs={{0,96},{8,104},{16,112},{24,120},{32,64},{40,72},{48,80},{56,88},{... | collective-permute-start | bytes 116744 | tf_op jit(solution)/shard_map/ppermute | solution.py:56
  35.7 4.1 %collective-permute-done.9.got_ref = f32[4,2432]{1,0:T(4,128)S(1)} collective-permute-done((f32[4,2432]{1,0:T(4,128)S(1)}, f32[4,2432]{1,0:T(4,128)S(1)}, u32[]{:S(2)}, u32[]{:S(2)}) %collective-permute-start.9) | collective-permute-done | bytes 38944 | tf_op jit(solution)/shard_map/ppermute | solution.py:56
  40.9 2.8 %collective-permute-done.10.got_ref = f32[2,2432]{1,0:T(2,128)S(1)} collective-permute-done((f32[2,2432]{1,0:T(2,128)S(1)}, f32[2,2432]{1,0:T(2,128)S(1)}, u32[]{:S(2)}, u32[]{:S(2)}) %collective-permute-start.10) | collective-permute-done | bytes 19488 | tf_op jit(solution)/shard_map/ppermute | solution.py:56
  43.7 2.1 %shard_map.111.own_ref = bf16[2,2048]{1,0:T(2,128)(2,1)S(1)} custom-call(s32[2,128]{1,0:T(2,128)S(1)} %broadcast_in_dim.7.lengths_ref, f32[2,2432]{1,0:T(2,128)S(1)} %get-tuple-element.60.kept_ref, f32[2,2432]{1,0:T(2,128)S(1)} %collective-permute-done.10.got_ref, f32[2,128]{1,0:T(2,128)S(1)} %get-tuple-element.62.cos_ref, ...), custom_call_target="tpu_custom_call" | custom-call | flops 2200000000 | bytes 1 | tf_op jit(solution)/shard_map/pallas_call | solution.py:253
  46.0 3.6 %collective-permute-done.11.other_ref = bf16[2,2048]{1,0:T(2,128)(2,1)S(1)} collective-permute-done((bf16[2,2048]{1,0:T(2,128)(2,1)S(1)}, bf16[2,2048]{1,0:T(2,128)(2,1)S(1)}, u32[]{:S(2)}, u32[]{:S(2)}) %collective-permute-start.11) | collective-permute-done | bytes 8224 | tf_op jit(solution)/shard_map/ppermute | solution.py:56
  49.6 1.1 %collective-permute-start.15 = (bf16[4,2048]{1,0:T(4,128)(2,1)S(1)}, bf16[4,2048]{1,0:T(4,128)(2,1)S(1)}, u32[]{:S(2)}, u32[]{:S(2)}) collective-permute-start(bf16[4,2048]{1,0:T(4,128)(2,1)S(1)} %shard_map.112.own_ref), channel_id=1, source_target_pairs={{0,96},{8,104},{16,112},{24,120},{32,64},{40,72},{48,80},{56,88},{... | collective-permute-start | bytes 49160 | tf_op jit(solution)/shard_map/ppermute | solution.py:56
  50.7 2.2 %collective-permute-start.20 = (bf16[2,1024,128]{2,1,0:T(8,128)(2,1)S(1)}, bf16[2,1024,128]{2,1,0:T(8,128)(2,1)S(1)}, u32[]{:S(2)}, u32[]{:S(2)}) collective-permute-start(bf16[2,1024,128]{2,1,0:T(8,128)(2,1)S(1)} %collective-permute-done.12), channel_id=1, source_target_pairs={{0,96},{8,104},{16,112},{24,120},{32,0},{40,8},{48,16},{56,24},{64... | collective-permute-start | bytes 1572872 | tf_op jit(solution)/shard_map/ppermute | solution.py:61
  53.1 1.7 %collective-permute-done.15.other_ref = bf16[4,2048]{1,0:T(4,128)(2,1)S(1)} collective-permute-done((bf16[4,2048]{1,0:T(4,128)(2,1)S(1)}, bf16[4,2048]{1,0:T(4,128)(2,1)S(1)}, u32[]{:S(2)}, u32[]{:S(2)}) %collective-permute-start.15) | collective-permute-done | bytes 16416 | tf_op jit(solution)/shard_map/ppermute | solution.py:56
  55.9 1.7 %collective-permute-start.16 = (bf16[8,2048]{1,0:T(8,128)(2,1)S(1)}, bf16[8,2048]{1,0:T(8,128)(2,1)S(1)}, u32[]{:S(2)}, u32[]{:S(2)}) collective-permute-start(bf16[8,2048]{1,0:T(8,128)(2,1)S(1)} %shard_map.115.own_ref), channel_id=1, source_target_pairs={{0,16},{8,24},{16,0},{24,8},{32,48},{40,56},{48,32},{56,40},{64,80... | collective-permute-start | bytes 98312 | tf_op jit(solution)/shard_map/ppermute | solution.py:56
  57.7 2.0 %collective-permute-start.22 = (bf16[2,1024,128]{2,1,0:T(8,128)(2,1)S(1)}, bf16[2,1024,128]{2,1,0:T(8,128)(2,1)S(1)}, u32[]{:S(2)}, u32[]{:S(2)}) collective-permute-start(bf16[2,1024,128]{2,1,0:T(8,128)(2,1)S(1)} %shard_map.120), channel_id=1, source_target_pairs={{0,16},{8,24},{16,0},{24,8},{32,48},{40,56},{48,32},{56,40},{64,80... | collective-permute-start | bytes 1572872 | tf_op jit(solution)/shard_map/ppermute | solution.py:56
  59.7 2.0 %collective-permute-done.16.other_ref = bf16[8,2048]{1,0:T(8,128)(2,1)S(1)} collective-permute-done((bf16[8,2048]{1,0:T(8,128)(2,1)S(1)}, bf16[8,2048]{1,0:T(8,128)(2,1)S(1)}, u32[]{:S(2)}, u32[]{:S(2)}) %collective-permute-start.16) | collective-permute-done | bytes 32800 | tf_op jit(solution)/shard_map/ppermute | solution.py:56
  61.7 1.7 %collective-permute-start.24 = (bf16[2,1024,128]{2,1,0:T(8,128)(2,1)S(1)}, bf16[2,1024,128]{2,1,0:T(8,128)(2,1)S(1)}, u32[]{:S(2)}, u32[]{:S(2)}) collective-permute-start(bf16[2,1024,128]{2,1,0:T(8,128)(2,1)S(1)} %collective-permute-done.14), channel_id=1, source_target_pairs={{0,64},{8,72},{16,80},{24,88},{32,96},{40,104},{48,112},{56,120},{... | collective-permute-start | bytes 1572872 | tf_op jit(solution)/shard_map/ppermute | solution.py:61
  64.4 3.7 %collective-permute-start.18 = (f32[4,32,128]{2,1,0:T(8,128)S(1)}, f32[4,32,128]{2,1,0:T(8,128)S(1)}, u32[]{:S(2)}, u32[]{:S(2)}) collective-permute-start(f32[4,32,128]{2,1,0:T(8,128)S(1)} %get-tuple-element.75), channel_id=1, source_target_pairs={{0,2},{1,3},{2,0},{3,1},{4,6},{5,7},{6,4},{7,5},{8,10},{9,11},{10,... | collective-permute-start | bytes 196616 | tf_op jit(solution)/shard_map/ppermute | solution.py:56
  68.0 2.4 %collective-permute-done.18.got_ref = f32[4,32,128]{2,1,0:T(8,128)S(1)} collective-permute-done((f32[4,32,128]{2,1,0:T(8,128)S(1)}, f32[4,32,128]{2,1,0:T(8,128)S(1)}, u32[]{:S(2)}, u32[]{:S(2)}) %collective-permute-start.18) | collective-permute-done | bytes 65568 | tf_op jit(solution)/shard_map/ppermute | solution.py:56
  70.4 1.5 %collective-permute-start.21 = (f32[2,32,128]{2,1,0:T(8,128)S(1)}, f32[2,32,128]{2,1,0:T(8,128)S(1)}, u32[]{:S(2)}, u32[]{:S(2)}) collective-permute-start(f32[2,32,128]{2,1,0:T(8,128)S(1)} %get-tuple-element.79), channel_id=1, source_target_pairs={{0,1},{1,0},{2,3},{3,2},{4,5},{5,4},{6,7},{7,6},{8,9},{9,8},{10,11... | collective-permute-start | bytes 98312 | tf_op jit(solution)/shard_map/ppermute | solution.py:56
  72.0 1.4 %shard_map.121.refs_3_ = bf16[1024,2048]{1,0:T(8,128)(2,1)} custom-call(bf16[2,1024,128]{2,1,0:T(8,128)(2,1)S(1)} %get-tuple-element.67.refs_0_, bf16[2,1024,128]{2,1,0:T(8,128)(2,1)S(1)} %collective-permute-done.6.refs_1_, bf16[2,1024,128]{2,1,0:T(8,128)(2,1)S(1)} %collective-permute-done.7.refs_2_, ...), custom_call_target="tpu_custom_call" | custom-call | flops 1 | bytes 1 | tf_op jit(solution)/shard_map/pallas_call | solution.py:369
  75.7 2.5 %collective-permute-done.23 = f32[1,32,128]{2,1,0:T(8,128)S(1)} collective-permute-done((f32[1,32,128]{2,1,0:T(8,128)S(1)}, f32[1,32,128]{2,1,0:T(8,128)S(1)}, u32[]{:S(2)}, u32[]{:S(2)}) %collective-permute-start.23) | collective-permute-done | bytes 16416 | tf_op jit(solution)/shard_map/ppermute | solution.py:56
  (69 shorter events, 10.0 us)
Async XLA Ops:
  0.6 9.8 %copy-start.4 = (bf16[32,128]{1,0:T(8,128)(2,1)S(1)}, bf16[32,128]{1,0:T(8,128)(2,1)}, u32[]{:S(2)}) copy-start(bf16[32,128]{1,0:T(8,128)(2,1)} %param.9) | copy-start | bytes 24580
  0.6 9.6 %copy-start.8 = (s32[2]{0:T(128)S(1)}, s32[2]{0:T(128)}, u32[]{:S(2)}) copy-start(s32[2]{0:T(128)} %param.16) | copy-start | bytes 28
  0.6 9.8 %collective-permute-start = (bf16[1,32,128]{2,1,0:T(8,128)(2,1)}, bf16[1,32,128]{2,1,0:T(8,128)(2,1)S(1)}, u32[]{:S(2)}, u32[]{:S(2)}) collective-permute-start(bf16[1,32,128]{2,1,0:T(8,128)(2,1)} %bitcast.4), channel_id=1, source_target_pairs={{0,4},{1,5},{2,6},{3,7},{4,0},{5,1},{6,2},{7,3},{8,12},{9,13},{10,... | collective-permute-start | bytes 24584 | tf_op jit(solution)/shard_map/ppermute | solution.py:56
  5.0 26.0 %collective-permute-start.6 = (bf16[2,1024,128]{2,1,0:T(8,128)(2,1)}, bf16[2,1024,128]{2,1,0:T(8,128)(2,1)S(1)}, u32[]{:S(2)}, u32[]{:S(2)}) collective-permute-start(bf16[2,1024,128]{2,1,0:T(8,128)(2,1)} %get-tuple-element.92), channel_id=1, source_target_pairs={{0,32},{8,40},{16,48},{24,56},{32,64},{40,72},{48,80},{56,88},{64,... | collective-permute-start | bytes 1572872 | tf_op jit(solution)/shard_map/ppermute | solution.py:61
  6.6 24.5 %collective-permute-start.7 = (bf16[2,1024,128]{2,1,0:T(8,128)(2,1)}, bf16[2,1024,128]{2,1,0:T(8,128)(2,1)S(1)}, u32[]{:S(2)}, u32[]{:S(2)}) collective-permute-start(bf16[2,1024,128]{2,1,0:T(8,128)(2,1)} %get-tuple-element.91), channel_id=1, source_target_pairs={{0,96},{8,104},{16,112},{24,120},{32,0},{40,8},{48,16},{56,24},{64... | collective-permute-start | bytes 1572872 | tf_op jit(solution)/shard_map/ppermute | solution.py:61
  8.3 24.0 %collective-permute-start.8 = (bf16[2,1024,128]{2,1,0:T(8,128)(2,1)S(1)}, bf16[2,1024,128]{2,1,0:T(8,128)(2,1)S(1)}, u32[]{:S(2)}, u32[]{:S(2)}) collective-permute-start(bf16[2,1024,128]{2,1,0:T(8,128)(2,1)S(1)} %get-tuple-element.90), channel_id=1, source_target_pairs={{0,64},{8,72},{16,80},{24,88},{32,96},{40,104},{48,112},{56,120},{... | collective-permute-start | bytes 1572872 | tf_op jit(solution)/shard_map/ppermute | solution.py:61
  10.6 16.8 %collective-permute-start.4 = (bf16[2,1024,128]{2,1,0:T(8,128)(2,1)}, bf16[2,1024,128]{2,1,0:T(8,128)(2,1)S(1)}, u32[]{:S(2)}, u32[]{:S(2)}) collective-permute-start(bf16[2,1024,128]{2,1,0:T(8,128)(2,1)} %get-tuple-element.52), channel_id=1, source_target_pairs={{0,16},{8,24},{16,0},{24,8},{32,48},{40,56},{48,32},{56,40},{64,80... | collective-permute-start | bytes 1572872 | tf_op jit(solution)/shard_map/ppermute | solution.py:56
  13.3 7.6 %copy-start.7 = (bf16[1024]{0:T(1024)(128)(2,1)S(1)}, bf16[1024]{0:T(1024)(128)(2,1)}, u32[]{:S(2)}) copy-start(bf16[1024]{0:T(1024)(128)(2,1)} %param.10) | copy-start | bytes 6148
  13.3 9.5 %copy-start.3 = (bf16[1024,256]{1,0:T(8,128)(2,1)S(1)}, bf16[1024,256]{1,0:T(8,128)(2,1)}, u32[]{:S(2)}) copy-start(bf16[1024,256]{1,0:T(8,128)(2,1)} %keyval_ref.1) | copy-start | bytes 1572868
  13.3 3.7 %collective-permute-start.1 = (bf16[2,32,128]{2,1,0:T(8,128)(2,1)S(1)}, bf16[2,32,128]{2,1,0:T(8,128)(2,1)S(1)}, u32[]{:S(2)}, u32[]{:S(2)}) collective-permute-start(bf16[2,32,128]{2,1,0:T(8,128)(2,1)S(1)} %shard_map.105.own_ref), channel_id=1, source_target_pairs={{0,1},{1,0},{2,3},{3,2},{4,5},{5,4},{6,7},{7,6},{8,9},{9,8},{10,11... | collective-permute-start | bytes 49160 | tf_op jit(solution)/shard_map/ppermute | solution.py:56
  17.1 5.8 %collective-permute-start.2 = (bf16[4,32,128]{2,1,0:T(8,128)(2,1)S(1)}, bf16[4,32,128]{2,1,0:T(8,128)(2,1)S(1)}, u32[]{:S(2)}, u32[]{:S(2)}) collective-permute-start(bf16[4,32,128]{2,1,0:T(8,128)(2,1)S(1)} %shard_map.106.near_ref), channel_id=1, source_target_pairs={{0,2},{1,3},{2,0},{3,1},{4,6},{5,7},{6,4},{7,5},{8,10},{9,11},{10,... | collective-permute-start | bytes 98312 | tf_op jit(solution)/shard_map/ppermute | solution.py:56
  25.9 1.5 %collective-permute-start.3 = (f32[16,2432]{1,0:T(8,128)S(1)}, f32[16,2432]{1,0:T(8,128)S(1)}, u32[]{:S(2)}, u32[]{:S(2)}) collective-permute-start(f32[16,2432]{1,0:T(8,128)S(1)} %get-tuple-element.51), channel_id=1, source_target_pairs={{0,8},{8,0},{16,24},{24,16},{32,40},{40,32},{48,56},{56,48},{64,72... | collective-permute-start | bytes 466952 | tf_op jit(solution)/shard_map/ppermute | solution.py:56
  27.4 6.8 %collective-permute-start.5 = (f32[8,2432]{1,0:T(8,128)S(1)}, f32[8,2432]{1,0:T(8,128)S(1)}, u32[]{:S(2)}, u32[]{:S(2)}) collective-permute-start(f32[8,2432]{1,0:T(8,128)S(1)} %get-tuple-element.56), channel_id=1, source_target_pairs={{0,16},{8,24},{16,0},{24,8},{32,48},{40,56},{48,32},{56,40},{64,80... | collective-permute-start | bytes 233480 | tf_op jit(solution)/shard_map/ppermute | solution.py:56
  28.3 21.3 %collective-permute-start.12 = (bf16[2,1024,128]{2,1,0:T(8,128)(2,1)S(1)}, bf16[2,1024,128]{2,1,0:T(8,128)(2,1)S(1)}, u32[]{:S(2)}, u32[]{:S(2)}) collective-permute-start(bf16[2,1024,128]{2,1,0:T(8,128)(2,1)S(1)} %get-tuple-element.64), channel_id=1, source_target_pairs={{0,16},{8,24},{16,0},{24,8},{32,48},{40,56},{48,32},{56,40},{64,80... | collective-permute-start | bytes 1572872 | tf_op jit(solution)/shard_map/ppermute | solution.py:56
  34.4 5.5 %collective-permute-start.13 = (bf16[7,1024,128]{2,1,0:T(8,128)(2,1)S(1)}, bf16[7,1024,128]{2,1,0:T(8,128)(2,1)S(1)}, u32[]{:S(2)}, u32[]{:S(2)}) collective-permute-start(bf16[7,1024,128]{2,1,0:T(8,128)(2,1)S(1)} %shard_map.113), channel_id=1, source_target_pairs={{0,8},{8,0},{16,24},{24,16},{32,40},{40,32},{48,56},{56,48},{64,72... | collective-permute-start | bytes 5505032 | tf_op jit(solution)/shard_map/ppermute | solution.py:56
  34.5 9.2 %copy-start.1 = (bf16[2,8192,128]{2,1,0:T(8,128)(2,1)S(1)}, bf16[2,8192,128]{2,1,0:T(8,128)(2,1)}, u32[]{:S(2)}) copy-start(bf16[2,8192,128]{2,1,0:T(8,128)(2,1)} %key_ref.1) | copy-start | bytes 12582916
  34.5 9.2 %copy-start.2 = (bf16[2,8192,128]{2,1,0:T(8,128)(2,1)S(1)}, bf16[2,8192,128]{2,1,0:T(8,128)(2,1)}, u32[]{:S(2)}) copy-start(bf16[2,8192,128]{2,1,0:T(8,128)(2,1)} %value_ref.1) | copy-start | bytes 12582916
  34.6 5.3 %collective-permute-start.9 = (f32[4,2432]{1,0:T(4,128)S(1)}, f32[4,2432]{1,0:T(4,128)S(1)}, u32[]{:S(2)}, u32[]{:S(2)}) collective-permute-start(f32[4,2432]{1,0:T(4,128)S(1)} %get-tuple-element.59), channel_id=1, source_target_pairs={{0,96},{8,104},{16,112},{24,120},{32,64},{40,72},{48,80},{56,88},{... | collective-permute-start | bytes 116744 | tf_op jit(solution)/shard_map/ppermute | solution.py:56
  39.9 3.9 %collective-permute-start.10 = (f32[2,2432]{1,0:T(2,128)S(1)}, f32[2,2432]{1,0:T(2,128)S(1)}, u32[]{:S(2)}, u32[]{:S(2)}) collective-permute-start(f32[2,2432]{1,0:T(2,128)S(1)} %get-tuple-element.61), channel_id=1, source_target_pairs={{0,32},{8,40},{16,48},{24,56},{32,0},{40,8},{48,16},{56,24},{64,96... | collective-permute-start | bytes 58376 | tf_op jit(solution)/shard_map/ppermute | solution.py:56
  40.1 15.8 %collective-permute-start.14 = (bf16[2,1024,128]{2,1,0:T(8,128)(2,1)S(1)}, bf16[2,1024,128]{2,1,0:T(8,128)(2,1)S(1)}, u32[]{:S(2)}, u32[]{:S(2)}) collective-permute-start(bf16[2,1024,128]{2,1,0:T(8,128)(2,1)S(1)} %shard_map.114), channel_id=1, source_target_pairs={{0,16},{8,24},{16,0},{24,8},{32,48},{40,56},{48,32},{56,40},{64,80... | collective-permute-start | bytes 1572872 | tf_op jit(solution)/shard_map/ppermute | solution.py:56
  45.9 3.7 %collective-permute-start.11 = (bf16[2,2048]{1,0:T(2,128)(2,1)S(1)}, bf16[2,2048]{1,0:T(2,128)(2,1)S(1)}, u32[]{:S(2)}, u32[]{:S(2)}) collective-permute-start(bf16[2,2048]{1,0:T(2,128)(2,1)S(1)} %shard_map.111.own_ref), channel_id=1, source_target_pairs={{0,32},{8,40},{16,48},{24,56},{32,0},{40,8},{48,16},{56,24},{64,96... | collective-permute-start | bytes 24584 | tf_op jit(solution)/shard_map/ppermute | solution.py:56
  49.6 5.2 %collective-permute-start.15 = (bf16[4,2048]{1,0:T(4,128)(2,1)S(1)}, bf16[4,2048]{1,0:T(4,128)(2,1)S(1)}, u32[]{:S(2)}, u32[]{:S(2)}) collective-permute-start(bf16[4,2048]{1,0:T(4,128)(2,1)S(1)} %shard_map.112.own_ref), channel_id=1, source_target_pairs={{0,96},{8,104},{16,112},{24,120},{32,64},{40,72},{48,80},{56,88},{... | collective-permute-start | bytes 49160 | tf_op jit(solution)/shard_map/ppermute | solution.py:56
  50.7 17.3 %collective-permute-start.20 = (bf16[2,1024,128]{2,1,0:T(8,128)(2,1)S(1)}, bf16[2,1024,128]{2,1,0:T(8,128)(2,1)S(1)}, u32[]{:S(2)}, u32[]{:S(2)}) collective-permute-start(bf16[2,1024,128]{2,1,0:T(8,128)(2,1)S(1)} %collective-permute-done.12), channel_id=1, source_target_pairs={{0,96},{8,104},{16,112},{24,120},{32,0},{40,8},{48,16},{56,24},{64... | collective-permute-start | bytes 1572872 | tf_op jit(solution)/shard_map/ppermute | solution.py:61
  53.0 15.0 %collective-permute-start.19 = (bf16[2,1024,128]{2,1,0:T(8,128)(2,1)S(1)}, bf16[2,1024,128]{2,1,0:T(8,128)(2,1)S(1)}, u32[]{:S(2)}, u32[]{:S(2)}) collective-permute-start(bf16[2,1024,128]{2,1,0:T(8,128)(2,1)S(1)} %shard_map.118), channel_id=1, source_target_pairs={{0,32},{8,40},{16,48},{24,56},{32,64},{40,72},{48,80},{56,88},{64,... | collective-permute-start | bytes 1572872 | tf_op jit(solution)/shard_map/ppermute | solution.py:61
  55.9 5.8 %collective-permute-start.16 = (bf16[8,2048]{1,0:T(8,128)(2,1)S(1)}, bf16[8,2048]{1,0:T(8,128)(2,1)S(1)}, u32[]{:S(2)}, u32[]{:S(2)}) collective-permute-start(bf16[8,2048]{1,0:T(8,128)(2,1)S(1)} %shard_map.115.own_ref), channel_id=1, source_target_pairs={{0,16},{8,24},{16,0},{24,8},{32,48},{40,56},{48,32},{56,40},{64,80... | collective-permute-start | bytes 98312 | tf_op jit(solution)/shard_map/ppermute | solution.py:56
  57.7 15.8 %collective-permute-start.22 = (bf16[2,1024,128]{2,1,0:T(8,128)(2,1)S(1)}, bf16[2,1024,128]{2,1,0:T(8,128)(2,1)S(1)}, u32[]{:S(2)}, u32[]{:S(2)}) collective-permute-start(bf16[2,1024,128]{2,1,0:T(8,128)(2,1)S(1)} %shard_map.120), channel_id=1, source_target_pairs={{0,16},{8,24},{16,0},{24,8},{32,48},{40,56},{48,32},{56,40},{64,80... | collective-permute-start | bytes 1572872 | tf_op jit(solution)/shard_map/ppermute | solution.py:56
  61.7 1.7 %collective-permute-start.17 = (bf16[16,2048]{1,0:T(8,128)(2,1)S(1)}, bf16[16,2048]{1,0:T(8,128)(2,1)S(1)}, u32[]{:S(2)}, u32[]{:S(2)}) collective-permute-start(bf16[16,2048]{1,0:T(8,128)(2,1)S(1)} %shard_map.116.own_ref), channel_id=1, source_target_pairs={{0,8},{8,0},{16,24},{24,16},{32,40},{40,32},{48,56},{56,48},{64,72... | collective-permute-start | bytes 196616 | tf_op jit(solution)/shard_map/ppermute | solution.py:56
  61.7 17.1 %collective-permute-start.24 = (bf16[2,1024,128]{2,1,0:T(8,128)(2,1)S(1)}, bf16[2,1024,128]{2,1,0:T(8,128)(2,1)S(1)}, u32[]{:S(2)}, u32[]{:S(2)}) collective-permute-start(bf16[2,1024,128]{2,1,0:T(8,128)(2,1)S(1)} %collective-permute-done.14), channel_id=1, source_target_pairs={{0,64},{8,72},{16,80},{24,88},{32,96},{40,104},{48,112},{56,120},{... | collective-permute-start | bytes 1572872 | tf_op jit(solution)/shard_map/ppermute | solution.py:61
  64.4 6.1 %collective-permute-start.18 = (f32[4,32,128]{2,1,0:T(8,128)S(1)}, f32[4,32,128]{2,1,0:T(8,128)S(1)}, u32[]{:S(2)}, u32[]{:S(2)}) collective-permute-start(f32[4,32,128]{2,1,0:T(8,128)S(1)} %get-tuple-element.75), channel_id=1, source_target_pairs={{0,2},{1,3},{2,0},{3,1},{4,6},{5,7},{6,4},{7,5},{8,10},{9,11},{10,... | collective-permute-start | bytes 196616 | tf_op jit(solution)/shard_map/ppermute | solution.py:56
  70.4 4.0 %collective-permute-start.21 = (f32[2,32,128]{2,1,0:T(8,128)S(1)}, f32[2,32,128]{2,1,0:T(8,128)S(1)}, u32[]{:S(2)}, u32[]{:S(2)}) collective-permute-start(f32[2,32,128]{2,1,0:T(8,128)S(1)} %get-tuple-element.79), channel_id=1, source_target_pairs={{0,1},{1,0},{2,3},{3,2},{4,5},{5,4},{6,7},{7,6},{8,9},{9,8},{10,11... | collective-permute-start | bytes 98312 | tf_op jit(solution)/shard_map/ppermute | solution.py:56
  71.9 6.8 %collective-permute-start.25 = (bf16[1,1024,128]{2,1,0:T(8,128)(2,1)S(1)}, bf16[1,1024,128]{2,1,0:T(8,128)(2,1)S(1)}, u32[]{:S(2)}, u32[]{:S(2)}) collective-permute-start(bf16[1,1024,128]{2,1,0:T(8,128)(2,1)S(1)} %shard_map.124), channel_id=1, source_target_pairs={{0,8},{8,0},{16,24},{24,16},{32,40},{40,32},{48,56},{56,48},{64,72... | collective-permute-start | bytes 786440 | tf_op jit(solution)/shard_map/ppermute | solution.py:56
  74.4 3.7 %collective-permute-start.23 = (f32[1,32,128]{2,1,0:T(8,128)S(1)}, f32[1,32,128]{2,1,0:T(8,128)S(1)}, u32[]{:S(2)}, u32[]{:S(2)}) collective-permute-start(f32[1,32,128]{2,1,0:T(8,128)S(1)} %get-tuple-element.82), channel_id=1, source_target_pairs={{0,4},{1,5},{2,6},{3,7},{4,0},{5,1},{6,2},{7,3},{8,12},{9,13},{10,... | collective-permute-start | bytes 49160 | tf_op jit(solution)/shard_map/ppermute | solution.py:56
  (3 other events, 11.9 us)

commit v4 on v3

--- a/solution.py
+++ b/solution.py
@@ -327,6 +327,47 @@
     return lax.dynamic_slice_in_dim(chunks, chip * 2, 2, 0)
 
 
+def stage_kernel(groups, chunks_ref, *refs):
+    pieces, (buffer, in_sems, out_sems) = refs[: len(groups)], refs[len(groups) :]
+    row = lax.axis_index("row")
+    copies = []
+    for piece, group in zip(pieces, groups):
+        for i, (dy, dx, core) in enumerate(group):
+            chip = ((((row >> 2) + dy) & 3) << 1) | (((row >> 1) & 1) ^ dx)
+            k = len(copies)
+            copies.append(
+                (
+                    pltpu.make_async_copy(
+                        chunks_ref.at[(chip << 1) | core], buffer.at[k], in_sems.at[k]
+                    ),
+                    pltpu.make_async_copy(buffer.at[k], piece.at[i], out_sems.at[k]),
+                )
+            )
+    for fetch, _ in copies:
+        fetch.start()
+    for fetch, store in copies:
+        fetch.wait()
+        store.start()
+    for _, store in copies:
+        store.wait()
+
+
+def stage(chunks, groups):
+    count = sum(len(group) for group in groups)
+    return call(
+        functools.partial(stage_kernel, groups),
+        [like(chunks, len(group)) for group in groups],
+        [HBM],
+        [HBM] * len(groups),
+        [
+            pltpu.VMEM((count,) + chunks.shape[1:], chunks.dtype),
+            pltpu.SemaphoreType.DMA((count,)),
+            pltpu.SemaphoreType.DMA((count,)),
+        ],
+        60,
+    )(chunks)
+
+
 def pack_kernel(count, slots, *refs):
     pieces, out_ref, sems = refs[:count], refs[-2], refs[-1]
     start_and_wait(
@@ -397,9 +438,13 @@
     def pair(dy, dx):
         return [(dy, dx, 0), (dy, dx, 1)]
 
-    to_a, to_b, to_c, to_e = [
-        chip_pair(chunks, *at) for at in ((1, 0), (3, 0), (2, 0), (1, 1))
-    ]
+    to_a, to_b, to_c, to_e = stage(
+        chunks,
+        [
+            [(dy, dx, core) for core in range(2)]
+            for dy, dx in ((1, 0), (3, 0), (2, 0), (1, 1))
+        ],
+    )
     got_a, got_b, got_c = shift_y(to_a, 1), shift_y(to_b, 3), shift_y(to_c, 2)
 
     other = flip(tokens[None], "col", X_LOW)

time: 79.9 us -> 79.7 us (level)
  local copies, waits for them, and re-layouts: 6.35 us -> 3.62 us
  Pallas kernels: 7.89 us -> 10.3 us
    dynamic_slice x2 -> x1, local copies, waits for them, and re-layouts: 2.87 us -> 0.15 us  [chip_pair(): return lax.dynamic_slice_in_dim(chunks, chip * 2, 2, 0)]
    pallas_call x0 -> x1, Pallas kernels: none -> 2.41 us  [stage(): call(functools.partial(stage_kernel, groups), [like(chunks, len(group)) f...]
  transfers between devices with their start and end apart: 26 -> 26, of which waited for: 13 -> 13; matrix products, arithmetic and copies ran while one was open for 5% -> 1% of each run, Pallas kernels for 9% -> 12%
where the time goes in v4:
time: 79.7 us; the launch traced here: 79.5 us
  starting transfers between devices  35.6 us (45%)
  waiting for transfers between devices  28.2 us (35%)
  Pallas kernels  10.3 us (13%)
  local copies, waits for them, and re-layouts  3.62 us (5%)
  between operations  0.91 us (1%)
  other arithmetic  0.8 us (1%)
    ppermute x20, waiting for transfers between devices, flip(): return lax.ppermute(block, axis, [(i, i ^ bits) for i in range(size)])  26.9 us
    ppermute x20, starting transfers between devices, flip(): return lax.ppermute(block, axis, [(i, i ^ bits) for i in range(size)])  26.4 us
    ppermute x6, starting transfers between devices, shift_y(): lax.ppermute(block, 'row', [(i, (i + 4 * steps) % size) for i in range(si...  9.24 us
    unnamed x18, local copies, waits for them, and re-layouts  3.4 us
    pallas_call x3, Pallas kernels, place(): call(functools.partial(place_kernel, len(pieces), slots), jax.ShapeDtypeS...  3.38 us
    pallas_call x1, Pallas kernels, stage(): call(functools.partial(stage_kernel, groups), [like(chunks, len(group)) f...  2.41 us
    pallas_call x1, Pallas kernels, attend(): call(functools.partial(attend_kernel, features), jax.ShapeDtypeStruct((ro...  2.12 us
  transfers between devices with their start and end apart: 26, of which 13 were waited for; matrix products, arithmetic and copies ran while one was open for 1% of the time, Pallas kernels for 12%

profile of v4, /device:TPU:0, one launch (start us, length us, event | category | flops | bytes accessed | tf_op | source)
XLA Modules:
  0.0 79.5 jit_solution(14965061439629590840)
XLA Ops:
  0.6 1.7 %collective-permute-start = (bf16[1,32,128]{2,1,0:T(8,128)(2,1)}, bf16[1,32,128]{2,1,0:T(8,128)(2,1)S(1)}, u32[]{:S(2)}, u32[]{:S(2)}) collective-permute-start(bf16[1,32,128]{2,1,0:T(8,128)(2,1)} %bitcast.4), channel_id=1, source_target_pairs={{0,4},{1,5},{2,6},{3,7},{4,0},{5,1},{6,2},{7,3},{8,12},{9,13},{10,... | collective-permute-start | bytes 24584 | tf_op jit(solution)/shard_map/ppermute | solution.py:56
  2.3 2.4 %shard_map.105 = (bf16[2,1024,128]{2,1,0:T(8,128)(2,1)}, bf16[2,1024,128]{2,1,0:T(8,128)(2,1)}, bf16[2,1024,128]{2,1,0:T(8,128)(2,1)}, bf16[2,1024,128]{2,1,0:T(8,128)(2,1)}) custom-call(bf16[16,1024,128]{2,1,0:T(8,128)(2,1)} %bitcast.6), custom_call_target="tpu_custom_call" | custom-call | flops 1 | bytes 1 | tf_op jit(solution)/shard_map/pallas_call | solution.py:357
  4.7 1.6 %collective-permute-start.6 = (bf16[2,1024,128]{2,1,0:T(8,128)(2,1)}, bf16[2,1024,128]{2,1,0:T(8,128)(2,1)S(1)}, u32[]{:S(2)}, u32[]{:S(2)}) collective-permute-start(bf16[2,1024,128]{2,1,0:T(8,128)(2,1)} %get-tuple-element.62), channel_id=1, source_target_pairs={{0,32},{8,40},{16,48},{24,56},{32,64},{40,72},{48,80},{56,88},{64,... | collective-permute-start | bytes 1572872 | tf_op jit(solution)/shard_map/ppermute | solution.py:61
  6.4 1.7 %collective-permute-start.7 = (bf16[2,1024,128]{2,1,0:T(8,128)(2,1)}, bf16[2,1024,128]{2,1,0:T(8,128)(2,1)S(1)}, u32[]{:S(2)}, u32[]{:S(2)}) collective-permute-start(bf16[2,1024,128]{2,1,0:T(8,128)(2,1)} %get-tuple-element.63), channel_id=1, source_target_pairs={{0,96},{8,104},{16,112},{24,120},{32,0},{40,8},{48,16},{56,24},{64... | collective-permute-start | bytes 1572872 | tf_op jit(solution)/shard_map/ppermute | solution.py:61
  8.0 2.0 %collective-permute-start.8 = (bf16[2,1024,128]{2,1,0:T(8,128)(2,1)}, bf16[2,1024,128]{2,1,0:T(8,128)(2,1)S(1)}, u32[]{:S(2)}, u32[]{:S(2)}) collective-permute-start(bf16[2,1024,128]{2,1,0:T(8,128)(2,1)} %get-tuple-element.64), channel_id=1, source_target_pairs={{0,64},{8,72},{16,80},{24,88},{32,96},{40,104},{48,112},{56,120},{... | collective-permute-start | bytes 1572872 | tf_op jit(solution)/shard_map/ppermute | solution.py:61
  10.3 2.8 %collective-permute-start.4 = (bf16[2,1024,128]{2,1,0:T(8,128)(2,1)}, bf16[2,1024,128]{2,1,0:T(8,128)(2,1)S(1)}, u32[]{:S(2)}, u32[]{:S(2)}) collective-permute-start(bf16[2,1024,128]{2,1,0:T(8,128)(2,1)} %get-tuple-element.57), channel_id=1, source_target_pairs={{0,16},{8,24},{16,0},{24,8},{32,48},{40,56},{48,32},{56,40},{64,80... | collective-permute-start | bytes 1572872 | tf_op jit(solution)/shard_map/ppermute | solution.py:56
  13.1 1.9 %collective-permute-start.1 = (bf16[2,32,128]{2,1,0:T(8,128)(2,1)S(1)}, bf16[2,32,128]{2,1,0:T(8,128)(2,1)S(1)}, u32[]{:S(2)}, u32[]{:S(2)}) collective-permute-start(bf16[2,32,128]{2,1,0:T(8,128)(2,1)S(1)} %shard_map.106.own_ref), channel_id=1, source_target_pairs={{0,1},{1,0},{2,3},{3,2},{4,5},{5,4},{6,7},{7,6},{8,9},{9,8},{10,11... | collective-permute-start | bytes 49160 | tf_op jit(solution)/shard_map/ppermute | solution.py:56
  15.0 1.8 %collective-permute-done.1.other_ref = bf16[2,32,128]{2,1,0:T(8,128)(2,1)S(1)} collective-permute-done((bf16[2,32,128]{2,1,0:T(8,128)(2,1)S(1)}, bf16[2,32,128]{2,1,0:T(8,128)(2,1)S(1)}, u32[]{:S(2)}, u32[]{:S(2)}) %collective-permute-start.1) | collective-permute-done | bytes 16416 | tf_op jit(solution)/shard_map/ppermute | solution.py:56
  16.8 3.9 %collective-permute-start.2 = (bf16[4,32,128]{2,1,0:T(8,128)(2,1)S(1)}, bf16[4,32,128]{2,1,0:T(8,128)(2,1)S(1)}, u32[]{:S(2)}, u32[]{:S(2)}) collective-permute-start(bf16[4,32,128]{2,1,0:T(8,128)(2,1)S(1)} %shard_map.107.near_ref), channel_id=1, source_target_pairs={{0,2},{1,3},{2,0},{3,1},{4,6},{5,7},{6,4},{7,5},{8,10},{9,11},{10,... | collective-permute-start | bytes 98312 | tf_op jit(solution)/shard_map/ppermute | solution.py:56
  20.7 1.9 %collective-permute-done.2.far_ref = bf16[4,32,128]{2,1,0:T(8,128)(2,1)S(1)} collective-permute-done((bf16[4,32,128]{2,1,0:T(8,128)(2,1)S(1)}, bf16[4,32,128]{2,1,0:T(8,128)(2,1)S(1)}, u32[]{:S(2)}, u32[]{:S(2)}) %collective-permute-start.2) | collective-permute-done | bytes 32800 | tf_op jit(solution)/shard_map/ppermute | solution.py:56
  22.6 2.2 %copy-done = bf16[1024,2048]{1,0:T(8,128)(2,1)S(1)} copy-done((bf16[1024,2048]{1,0:T(8,128)(2,1)S(1)}, bf16[1024,2048]{1,0:T(8,128)(2,1)}, u32[]{:S(2)}) %copy-start) | copy-done | bytes 4194328
  25.8 1.2 %copy-done.6 = bf16[16384,128]{1,0:T(8,128)(2,1)S(1)} copy-done((bf16[16384,128]{1,0:T(8,128)(2,1)S(1)}, bf16[16384,128]{1,0:T(8,128)(2,1)}, u32[]{:S(2)}) %copy-start.6) | copy-done | bytes 4194328
  28.1 2.7 %collective-permute-start.12 = (bf16[2,1024,128]{2,1,0:T(8,128)(2,1)S(1)}, bf16[2,1024,128]{2,1,0:T(8,128)(2,1)S(1)}, u32[]{:S(2)}, u32[]{:S(2)}) collective-permute-start(bf16[2,1024,128]{2,1,0:T(8,128)(2,1)S(1)} %get-tuple-element.72), channel_id=1, source_target_pairs={{0,16},{8,24},{16,0},{24,8},{32,48},{40,56},{48,32},{56,40},{64,80... | collective-permute-start | bytes 1572872 | tf_op jit(solution)/shard_map/ppermute | solution.py:56
  30.8 1.3 %collective-permute-done.8.refs_3_ = bf16[2,1024,128]{2,1,0:T(8,128)(2,1)S(1)} collective-permute-done((bf16[2,1024,128]{2,1,0:T(8,128)(2,1)}, bf16[2,1024,128]{2,1,0:T(8,128)(2,1)S(1)}, u32[]{:S(2)}, u32[]{:S(2)}) %collective-permute-start.8) | collective-permute-done | bytes 524320 | tf_op jit(solution)/shard_map/ppermute | solution.py:61
  32.1 1.9 %collective-permute-done.5.got_ref = f32[8,2432]{1,0:T(8,128)S(1)} collective-permute-done((f32[8,2432]{1,0:T(8,128)S(1)}, f32[8,2432]{1,0:T(8,128)S(1)}, u32[]{:S(2)}, u32[]{:S(2)}) %collective-permute-start.5) | collective-permute-done | bytes 77856 | tf_op jit(solution)/shard_map/ppermute | solution.py:56
  34.3 1.1 %collective-permute-start.9 = (f32[4,2432]{1,0:T(4,128)S(1)}, f32[4,2432]{1,0:T(4,128)S(1)}, u32[]{:S(2)}, u32[]{:S(2)}) collective-permute-start(f32[4,2432]{1,0:T(4,128)S(1)} %get-tuple-element.67), channel_id=1, source_target_pairs={{0,96},{8,104},{16,112},{24,120},{32,64},{40,72},{48,80},{56,88},{... | collective-permute-start | bytes 116744 | tf_op jit(solution)/shard_map/ppermute | solution.py:56
  35.5 4.1 %collective-permute-done.9.got_ref = f32[4,2432]{1,0:T(4,128)S(1)} collective-permute-done((f32[4,2432]{1,0:T(4,128)S(1)}, f32[4,2432]{1,0:T(4,128)S(1)}, u32[]{:S(2)}, u32[]{:S(2)}) %collective-permute-start.9) | collective-permute-done | bytes 38944 | tf_op jit(solution)/shard_map/ppermute | solution.py:56
  40.7 2.8 %collective-permute-done.10.got_ref = f32[2,2432]{1,0:T(2,128)S(1)} collective-permute-done((f32[2,2432]{1,0:T(2,128)S(1)}, f32[2,2432]{1,0:T(2,128)S(1)}, u32[]{:S(2)}, u32[]{:S(2)}) %collective-permute-start.10) | collective-permute-done | bytes 19488 | tf_op jit(solution)/shard_map/ppermute | solution.py:56
  43.5 2.1 %shard_map.112.own_ref = bf16[2,2048]{1,0:T(2,128)(2,1)S(1)} custom-call(s32[2,128]{1,0:T(2,128)S(1)} %broadcast_in_dim.7.lengths_ref, f32[2,2432]{1,0:T(2,128)S(1)} %get-tuple-element.68.kept_ref, f32[2,2432]{1,0:T(2,128)S(1)} %collective-permute-done.10.got_ref, f32[2,128]{1,0:T(2,128)S(1)} %get-tuple-element.70.cos_ref, ...), custom_call_target="tpu_custom_call" | custom-call | flops 2200000000 | bytes 1 | tf_op jit(solution)/shard_map/pallas_call | solution.py:253
  45.7 3.6 %collective-permute-done.11.other_ref = bf16[2,2048]{1,0:T(2,128)(2,1)S(1)} collective-permute-done((bf16[2,2048]{1,0:T(2,128)(2,1)S(1)}, bf16[2,2048]{1,0:T(2,128)(2,1)S(1)}, u32[]{:S(2)}, u32[]{:S(2)}) %collective-permute-start.11) | collective-permute-done | bytes 8224 | tf_op jit(solution)/shard_map/ppermute | solution.py:56
  49.4 1.1 %collective-permute-start.15 = (bf16[4,2048]{1,0:T(4,128)(2,1)S(1)}, bf16[4,2048]{1,0:T(4,128)(2,1)S(1)}, u32[]{:S(2)}, u32[]{:S(2)}) collective-permute-start(bf16[4,2048]{1,0:T(4,128)(2,1)S(1)} %shard_map.113.own_ref), channel_id=1, source_target_pairs={{0,96},{8,104},{16,112},{24,120},{32,64},{40,72},{48,80},{56,88},{... | collective-permute-start | bytes 49160 | tf_op jit(solution)/shard_map/ppermute | solution.py:56
  50.5 2.2 %collective-permute-start.20 = (bf16[2,1024,128]{2,1,0:T(8,128)(2,1)S(1)}, bf16[2,1024,128]{2,1,0:T(8,128)(2,1)S(1)}, u32[]{:S(2)}, u32[]{:S(2)}) collective-permute-start(bf16[2,1024,128]{2,1,0:T(8,128)(2,1)S(1)} %collective-permute-done.12), channel_id=1, source_target_pairs={{0,96},{8,104},{16,112},{24,120},{32,0},{40,8},{48,16},{56,24},{64... | collective-permute-start | bytes 1572872 | tf_op jit(solution)/shard_map/ppermute | solution.py:61
  52.8 1.7 %collective-permute-done.15.other_ref = bf16[4,2048]{1,0:T(4,128)(2,1)S(1)} collective-permute-done((bf16[4,2048]{1,0:T(4,128)(2,1)S(1)}, bf16[4,2048]{1,0:T(4,128)(2,1)S(1)}, u32[]{:S(2)}, u32[]{:S(2)}) %collective-permute-start.15) | collective-permute-done | bytes 16416 | tf_op jit(solution)/shard_map/ppermute | solution.py:56
  55.7 1.7 %collective-permute-start.16 = (bf16[8,2048]{1,0:T(8,128)(2,1)S(1)}, bf16[8,2048]{1,0:T(8,128)(2,1)S(1)}, u32[]{:S(2)}, u32[]{:S(2)}) collective-permute-start(bf16[8,2048]{1,0:T(8,128)(2,1)S(1)} %shard_map.116.own_ref), channel_id=1, source_target_pairs={{0,16},{8,24},{16,0},{24,8},{32,48},{40,56},{48,32},{56,40},{64,80... | collective-permute-start | bytes 98312 | tf_op jit(solution)/shard_map/ppermute | solution.py:56
  57.4 2.0 %collective-permute-start.22 = (bf16[2,1024,128]{2,1,0:T(8,128)(2,1)S(1)}, bf16[2,1024,128]{2,1,0:T(8,128)(2,1)S(1)}, u32[]{:S(2)}, u32[]{:S(2)}) collective-permute-start(bf16[2,1024,128]{2,1,0:T(8,128)(2,1)S(1)} %shard_map.121), channel_id=1, source_target_pairs={{0,16},{8,24},{16,0},{24,8},{32,48},{40,56},{48,32},{56,40},{64,80... | collective-permute-start | bytes 1572872 | tf_op jit(solution)/shard_map/ppermute | solution.py:56
  59.4 2.0 %collective-permute-done.16.other_ref = bf16[8,2048]{1,0:T(8,128)(2,1)S(1)} collective-permute-done((bf16[8,2048]{1,0:T(8,128)(2,1)S(1)}, bf16[8,2048]{1,0:T(8,128)(2,1)S(1)}, u32[]{:S(2)}, u32[]{:S(2)}) %collective-permute-start.16) | collective-permute-done | bytes 32800 | tf_op jit(solution)/shard_map/ppermute | solution.py:56
  61.5 1.7 %collective-permute-start.24 = (bf16[2,1024,128]{2,1,0:T(8,128)(2,1)S(1)}, bf16[2,1024,128]{2,1,0:T(8,128)(2,1)S(1)}, u32[]{:S(2)}, u32[]{:S(2)}) collective-permute-start(bf16[2,1024,128]{2,1,0:T(8,128)(2,1)S(1)} %collective-permute-done.14), channel_id=1, source_target_pairs={{0,64},{8,72},{16,80},{24,88},{32,96},{40,104},{48,112},{56,120},{... | collective-permute-start | bytes 1572872 | tf_op jit(solution)/shard_map/ppermute | solution.py:61
  64.1 3.6 %collective-permute-start.18 = (f32[4,32,128]{2,1,0:T(8,128)S(1)}, f32[4,32,128]{2,1,0:T(8,128)S(1)}, u32[]{:S(2)}, u32[]{:S(2)}) collective-permute-start(f32[4,32,128]{2,1,0:T(8,128)S(1)} %get-tuple-element.83), channel_id=1, source_target_pairs={{0,2},{1,3},{2,0},{3,1},{4,6},{5,7},{6,4},{7,5},{8,10},{9,11},{10,... | collective-permute-start | bytes 196616 | tf_op jit(solution)/shard_map/ppermute | solution.py:56
  67.8 2.4 %collective-permute-done.18.got_ref = f32[4,32,128]{2,1,0:T(8,128)S(1)} collective-permute-done((f32[4,32,128]{2,1,0:T(8,128)S(1)}, f32[4,32,128]{2,1,0:T(8,128)S(1)}, u32[]{:S(2)}, u32[]{:S(2)}) %collective-permute-start.18) | collective-permute-done | bytes 65568 | tf_op jit(solution)/shard_map/ppermute | solution.py:56
  70.2 1.5 %collective-permute-start.21 = (f32[2,32,128]{2,1,0:T(8,128)S(1)}, f32[2,32,128]{2,1,0:T(8,128)S(1)}, u32[]{:S(2)}, u32[]{:S(2)}) collective-permute-start(f32[2,32,128]{2,1,0:T(8,128)S(1)} %get-tuple-element.87), channel_id=1, source_target_pairs={{0,1},{1,0},{2,3},{3,2},{4,5},{5,4},{6,7},{7,6},{8,9},{9,8},{10,11... | collective-permute-start | bytes 98312 | tf_op jit(solution)/shard_map/ppermute | solution.py:56
  71.8 1.4 %shard_map.122.refs_3_ = bf16[1024,2048]{1,0:T(8,128)(2,1)} custom-call(bf16[2,1024,128]{2,1,0:T(8,128)(2,1)S(1)} %get-tuple-element.75.refs_0_, bf16[2,1024,128]{2,1,0:T(8,128)(2,1)S(1)} %collective-permute-done.6.refs_1_, bf16[2,1024,128]{2,1,0:T(8,128)(2,1)S(1)} %collective-permute-done.7.refs_2_, ...), custom_call_target="tpu_custom_call" | custom-call | flops 1 | bytes 1 | tf_op jit(solution)/shard_map/pallas_call | solution.py:410
  75.5 2.5 %collective-permute-done.23 = f32[1,32,128]{2,1,0:T(8,128)S(1)} collective-permute-done((f32[1,32,128]{2,1,0:T(8,128)S(1)}, f32[1,32,128]{2,1,0:T(8,128)S(1)}, u32[]{:S(2)}, u32[]{:S(2)}) %collective-permute-start.23) | collective-permute-done | bytes 16416 | tf_op jit(solution)/shard_map/ppermute | solution.py:56
  (69 shorter events, 10.0 us)
Async XLA Ops:
  0.6 9.6 %copy-start.4 = (bf16[32,128]{1,0:T(8,128)(2,1)S(1)}, bf16[32,128]{1,0:T(8,128)(2,1)}, u32[]{:S(2)}) copy-start(bf16[32,128]{1,0:T(8,128)(2,1)} %param.9) | copy-start | bytes 24580
  0.6 9.4 %copy-start.8 = (s32[2]{0:T(128)S(1)}, s32[2]{0:T(128)}, u32[]{:S(2)}) copy-start(s32[2]{0:T(128)} %param.16) | copy-start | bytes 28
  0.6 9.6 %collective-permute-start = (bf16[1,32,128]{2,1,0:T(8,128)(2,1)}, bf16[1,32,128]{2,1,0:T(8,128)(2,1)S(1)}, u32[]{:S(2)}, u32[]{:S(2)}) collective-permute-start(bf16[1,32,128]{2,1,0:T(8,128)(2,1)} %bitcast.4), channel_id=1, source_target_pairs={{0,4},{1,5},{2,6},{3,7},{4,0},{5,1},{6,2},{7,3},{8,12},{9,13},{10,... | collective-permute-start | bytes 24584 | tf_op jit(solution)/shard_map/ppermute | solution.py:56
  4.7 26.1 %collective-permute-start.6 = (bf16[2,1024,128]{2,1,0:T(8,128)(2,1)}, bf16[2,1024,128]{2,1,0:T(8,128)(2,1)S(1)}, u32[]{:S(2)}, u32[]{:S(2)}) collective-permute-start(bf16[2,1024,128]{2,1,0:T(8,128)(2,1)} %get-tuple-element.62), channel_id=1, source_target_pairs={{0,32},{8,40},{16,48},{24,56},{32,64},{40,72},{48,80},{56,88},{64,... | collective-permute-start | bytes 1572872 | tf_op jit(solution)/shard_map/ppermute | solution.py:61
  6.4 24.5 %collective-permute-start.7 = (bf16[2,1024,128]{2,1,0:T(8,128)(2,1)}, bf16[2,1024,128]{2,1,0:T(8,128)(2,1)S(1)}, u32[]{:S(2)}, u32[]{:S(2)}) collective-permute-start(bf16[2,1024,128]{2,1,0:T(8,128)(2,1)} %get-tuple-element.63), channel_id=1, source_target_pairs={{0,96},{8,104},{16,112},{24,120},{32,0},{40,8},{48,16},{56,24},{64... | collective-permute-start | bytes 1572872 | tf_op jit(solution)/shard_map/ppermute | solution.py:61
  8.0 24.0 %collective-permute-start.8 = (bf16[2,1024,128]{2,1,0:T(8,128)(2,1)}, bf16[2,1024,128]{2,1,0:T(8,128)(2,1)S(1)}, u32[]{:S(2)}, u32[]{:S(2)}) collective-permute-start(bf16[2,1024,128]{2,1,0:T(8,128)(2,1)} %get-tuple-element.64), channel_id=1, source_target_pairs={{0,64},{8,72},{16,80},{24,88},{32,96},{40,104},{48,112},{56,120},{... | collective-permute-start | bytes 1572872 | tf_op jit(solution)/shard_map/ppermute | solution.py:61
  10.3 16.8 %collective-permute-start.4 = (bf16[2,1024,128]{2,1,0:T(8,128)(2,1)}, bf16[2,1024,128]{2,1,0:T(8,128)(2,1)S(1)}, u32[]{:S(2)}, u32[]{:S(2)}) collective-permute-start(bf16[2,1024,128]{2,1,0:T(8,128)(2,1)} %get-tuple-element.57), channel_id=1, source_target_pairs={{0,16},{8,24},{16,0},{24,8},{32,48},{40,56},{48,32},{56,40},{64,80... | collective-permute-start | bytes 1572872 | tf_op jit(solution)/shard_map/ppermute | solution.py:56
  13.1 7.6 %copy-start.7 = (bf16[1024]{0:T(1024)(128)(2,1)S(1)}, bf16[1024]{0:T(1024)(128)(2,1)}, u32[]{:S(2)}) copy-start(bf16[1024]{0:T(1024)(128)(2,1)} %param.10) | copy-start | bytes 6148
  13.1 9.5 %copy-start.3 = (bf16[1024,256]{1,0:T(8,128)(2,1)S(1)}, bf16[1024,256]{1,0:T(8,128)(2,1)}, u32[]{:S(2)}) copy-start(bf16[1024,256]{1,0:T(8,128)(2,1)} %keyval_ref.1) | copy-start | bytes 1572868
  13.1 3.7 %collective-permute-start.1 = (bf16[2,32,128]{2,1,0:T(8,128)(2,1)S(1)}, bf16[2,32,128]{2,1,0:T(8,128)(2,1)S(1)}, u32[]{:S(2)}, u32[]{:S(2)}) collective-permute-start(bf16[2,32,128]{2,1,0:T(8,128)(2,1)S(1)} %shard_map.106.own_ref), channel_id=1, source_target_pairs={{0,1},{1,0},{2,3},{3,2},{4,5},{5,4},{6,7},{7,6},{8,9},{9,8},{10,11... | collective-permute-start | bytes 49160 | tf_op jit(solution)/shard_map/ppermute | solution.py:56
  16.8 5.8 %collective-permute-start.2 = (bf16[4,32,128]{2,1,0:T(8,128)(2,1)S(1)}, bf16[4,32,128]{2,1,0:T(8,128)(2,1)S(1)}, u32[]{:S(2)}, u32[]{:S(2)}) collective-permute-start(bf16[4,32,128]{2,1,0:T(8,128)(2,1)S(1)} %shard_map.107.near_ref), channel_id=1, source_target_pairs={{0,2},{1,3},{2,0},{3,1},{4,6},{5,7},{6,4},{7,5},{8,10},{9,11},{10,... | collective-permute-start | bytes 98312 | tf_op jit(solution)/shard_map/ppermute | solution.py:56
  25.7 1.5 %collective-permute-start.3 = (f32[16,2432]{1,0:T(8,128)S(1)}, f32[16,2432]{1,0:T(8,128)S(1)}, u32[]{:S(2)}, u32[]{:S(2)}) collective-permute-start(f32[16,2432]{1,0:T(8,128)S(1)} %get-tuple-element.56), channel_id=1, source_target_pairs={{0,8},{8,0},{16,24},{24,16},{32,40},{40,32},{48,56},{56,48},{64,72... | collective-permute-start | bytes 466952 | tf_op jit(solution)/shard_map/ppermute | solution.py:56
  27.2 6.8 %collective-permute-start.5 = (f32[8,2432]{1,0:T(8,128)S(1)}, f32[8,2432]{1,0:T(8,128)S(1)}, u32[]{:S(2)}, u32[]{:S(2)}) collective-permute-start(f32[8,2432]{1,0:T(8,128)S(1)} %get-tuple-element.61), channel_id=1, source_target_pairs={{0,16},{8,24},{16,0},{24,8},{32,48},{40,56},{48,32},{56,40},{64,80... | collective-permute-start | bytes 233480 | tf_op jit(solution)/shard_map/ppermute | solution.py:56
  28.1 21.3 %collective-permute-start.12 = (bf16[2,1024,128]{2,1,0:T(8,128)(2,1)S(1)}, bf16[2,1024,128]{2,1,0:T(8,128)(2,1)S(1)}, u32[]{:S(2)}, u32[]{:S(2)}) collective-permute-start(bf16[2,1024,128]{2,1,0:T(8,128)(2,1)S(1)} %get-tuple-element.72), channel_id=1, source_target_pairs={{0,16},{8,24},{16,0},{24,8},{32,48},{40,56},{48,32},{56,40},{64,80... | collective-permute-start | bytes 1572872 | tf_op jit(solution)/shard_map/ppermute | solution.py:56
  34.2 5.5 %collective-permute-start.13 = (bf16[7,1024,128]{2,1,0:T(8,128)(2,1)S(1)}, bf16[7,1024,128]{2,1,0:T(8,128)(2,1)S(1)}, u32[]{:S(2)}, u32[]{:S(2)}) collective-permute-start(bf16[7,1024,128]{2,1,0:T(8,128)(2,1)S(1)} %shard_map.114), channel_id=1, source_target_pairs={{0,8},{8,0},{16,24},{24,16},{32,40},{40,32},{48,56},{56,48},{64,72... | collective-permute-start | bytes 5505032 | tf_op jit(solution)/shard_map/ppermute | solution.py:56
  34.3 9.2 %copy-start.1 = (bf16[2,8192,128]{2,1,0:T(8,128)(2,1)S(1)}, bf16[2,8192,128]{2,1,0:T(8,128)(2,1)}, u32[]{:S(2)}) copy-start(bf16[2,8192,128]{2,1,0:T(8,128)(2,1)} %key_ref.1) | copy-start | bytes 12582916
  34.3 9.2 %copy-start.2 = (bf16[2,8192,128]{2,1,0:T(8,128)(2,1)S(1)}, bf16[2,8192,128]{2,1,0:T(8,128)(2,1)}, u32[]{:S(2)}) copy-start(bf16[2,8192,128]{2,1,0:T(8,128)(2,1)} %value_ref.1) | copy-start | bytes 12582916
  34.3 5.3 %collective-permute-start.9 = (f32[4,2432]{1,0:T(4,128)S(1)}, f32[4,2432]{1,0:T(4,128)S(1)}, u32[]{:S(2)}, u32[]{:S(2)}) collective-permute-start(f32[4,2432]{1,0:T(4,128)S(1)} %get-tuple-element.67), channel_id=1, source_target_pairs={{0,96},{8,104},{16,112},{24,120},{32,64},{40,72},{48,80},{56,88},{... | collective-permute-start | bytes 116744 | tf_op jit(solution)/shard_map/ppermute | solution.py:56
  39.6 3.9 %collective-permute-start.10 = (f32[2,2432]{1,0:T(2,128)S(1)}, f32[2,2432]{1,0:T(2,128)S(1)}, u32[]{:S(2)}, u32[]{:S(2)}) collective-permute-start(f32[2,2432]{1,0:T(2,128)S(1)} %get-tuple-element.69), channel_id=1, source_target_pairs={{0,32},{8,40},{16,48},{24,56},{32,0},{40,8},{48,16},{56,24},{64,96... | collective-permute-start | bytes 58376 | tf_op jit(solution)/shard_map/ppermute | solution.py:56
  39.8 15.8 %collective-permute-start.14 = (bf16[2,1024,128]{2,1,0:T(8,128)(2,1)S(1)}, bf16[2,1024,128]{2,1,0:T(8,128)(2,1)S(1)}, u32[]{:S(2)}, u32[]{:S(2)}) collective-permute-start(bf16[2,1024,128]{2,1,0:T(8,128)(2,1)S(1)} %shard_map.115), channel_id=1, source_target_pairs={{0,16},{8,24},{16,0},{24,8},{32,48},{40,56},{48,32},{56,40},{64,80... | collective-permute-start | bytes 1572872 | tf_op jit(solution)/shard_map/ppermute | solution.py:56
  45.6 3.7 %collective-permute-start.11 = (bf16[2,2048]{1,0:T(2,128)(2,1)S(1)}, bf16[2,2048]{1,0:T(2,128)(2,1)S(1)}, u32[]{:S(2)}, u32[]{:S(2)}) collective-permute-start(bf16[2,2048]{1,0:T(2,128)(2,1)S(1)} %shard_map.112.own_ref), channel_id=1, source_target_pairs={{0,32},{8,40},{16,48},{24,56},{32,0},{40,8},{48,16},{56,24},{64,96... | collective-permute-start | bytes 24584 | tf_op jit(solution)/shard_map/ppermute | solution.py:56
  49.4 5.2 %collective-permute-start.15 = (bf16[4,2048]{1,0:T(4,128)(2,1)S(1)}, bf16[4,2048]{1,0:T(4,128)(2,1)S(1)}, u32[]{:S(2)}, u32[]{:S(2)}) collective-permute-start(bf16[4,2048]{1,0:T(4,128)(2,1)S(1)} %shard_map.113.own_ref), channel_id=1, source_target_pairs={{0,96},{8,104},{16,112},{24,120},{32,64},{40,72},{48,80},{56,88},{... | collective-permute-start | bytes 49160 | tf_op jit(solution)/shard_map/ppermute | solution.py:56
  50.5 17.3 %collective-permute-start.20 = (bf16[2,1024,128]{2,1,0:T(8,128)(2,1)S(1)}, bf16[2,1024,128]{2,1,0:T(8,128)(2,1)S(1)}, u32[]{:S(2)}, u32[]{:S(2)}) collective-permute-start(bf16[2,1024,128]{2,1,0:T(8,128)(2,1)S(1)} %collective-permute-done.12), channel_id=1, source_target_pairs={{0,96},{8,104},{16,112},{24,120},{32,0},{40,8},{48,16},{56,24},{64... | collective-permute-start | bytes 1572872 | tf_op jit(solution)/shard_map/ppermute | solution.py:61
  52.7 15.0 %collective-permute-start.19 = (bf16[2,1024,128]{2,1,0:T(8,128)(2,1)S(1)}, bf16[2,1024,128]{2,1,0:T(8,128)(2,1)S(1)}, u32[]{:S(2)}, u32[]{:S(2)}) collective-permute-start(bf16[2,1024,128]{2,1,0:T(8,128)(2,1)S(1)} %shard_map.119), channel_id=1, source_target_pairs={{0,32},{8,40},{16,48},{24,56},{32,64},{40,72},{48,80},{56,88},{64,... | collective-permute-start | bytes 1572872 | tf_op jit(solution)/shard_map/ppermute | solution.py:61
  55.7 5.8 %collective-permute-start.16 = (bf16[8,2048]{1,0:T(8,128)(2,1)S(1)}, bf16[8,2048]{1,0:T(8,128)(2,1)S(1)}, u32[]{:S(2)}, u32[]{:S(2)}) collective-permute-start(bf16[8,2048]{1,0:T(8,128)(2,1)S(1)} %shard_map.116.own_ref), channel_id=1, source_target_pairs={{0,16},{8,24},{16,0},{24,8},{32,48},{40,56},{48,32},{56,40},{64,80... | collective-permute-start | bytes 98312 | tf_op jit(solution)/shard_map/ppermute | solution.py:56
  57.4 15.8 %collective-permute-start.22 = (bf16[2,1024,128]{2,1,0:T(8,128)(2,1)S(1)}, bf16[2,1024,128]{2,1,0:T(8,128)(2,1)S(1)}, u32[]{:S(2)}, u32[]{:S(2)}) collective-permute-start(bf16[2,1024,128]{2,1,0:T(8,128)(2,1)S(1)} %shard_map.121), channel_id=1, source_target_pairs={{0,16},{8,24},{16,0},{24,8},{32,48},{40,56},{48,32},{56,40},{64,80... | collective-permute-start | bytes 1572872 | tf_op jit(solution)/shard_map/ppermute | solution.py:56
  61.5 1.7 %collective-permute-start.17 = (bf16[16,2048]{1,0:T(8,128)(2,1)S(1)}, bf16[16,2048]{1,0:T(8,128)(2,1)S(1)}, u32[]{:S(2)}, u32[]{:S(2)}) collective-permute-start(bf16[16,2048]{1,0:T(8,128)(2,1)S(1)} %shard_map.117.own_ref), channel_id=1, source_target_pairs={{0,8},{8,0},{16,24},{24,16},{32,40},{40,32},{48,56},{56,48},{64,72... | collective-permute-start | bytes 196616 | tf_op jit(solution)/shard_map/ppermute | solution.py:56
  61.5 17.1 %collective-permute-start.24 = (bf16[2,1024,128]{2,1,0:T(8,128)(2,1)S(1)}, bf16[2,1024,128]{2,1,0:T(8,128)(2,1)S(1)}, u32[]{:S(2)}, u32[]{:S(2)}) collective-permute-start(bf16[2,1024,128]{2,1,0:T(8,128)(2,1)S(1)} %collective-permute-done.14), channel_id=1, source_target_pairs={{0,64},{8,72},{16,80},{24,88},{32,96},{40,104},{48,112},{56,120},{... | collective-permute-start | bytes 1572872 | tf_op jit(solution)/shard_map/ppermute | solution.py:61
  64.1 6.1 %collective-permute-start.18 = (f32[4,32,128]{2,1,0:T(8,128)S(1)}, f32[4,32,128]{2,1,0:T(8,128)S(1)}, u32[]{:S(2)}, u32[]{:S(2)}) collective-permute-start(f32[4,32,128]{2,1,0:T(8,128)S(1)} %get-tuple-element.83), channel_id=1, source_target_pairs={{0,2},{1,3},{2,0},{3,1},{4,6},{5,7},{6,4},{7,5},{8,10},{9,11},{10,... | collective-permute-start | bytes 196616 | tf_op jit(solution)/shard_map/ppermute | solution.py:56
  70.2 4.0 %collective-permute-start.21 = (f32[2,32,128]{2,1,0:T(8,128)S(1)}, f32[2,32,128]{2,1,0:T(8,128)S(1)}, u32[]{:S(2)}, u32[]{:S(2)}) collective-permute-start(f32[2,32,128]{2,1,0:T(8,128)S(1)} %get-tuple-element.87), channel_id=1, source_target_pairs={{0,1},{1,0},{2,3},{3,2},{4,5},{5,4},{6,7},{7,6},{8,9},{9,8},{10,11... | collective-permute-start | bytes 98312 | tf_op jit(solution)/shard_map/ppermute | solution.py:56
  71.7 6.8 %collective-permute-start.25 = (bf16[1,1024,128]{2,1,0:T(8,128)(2,1)S(1)}, bf16[1,1024,128]{2,1,0:T(8,128)(2,1)S(1)}, u32[]{:S(2)}, u32[]{:S(2)}) collective-permute-start(bf16[1,1024,128]{2,1,0:T(8,128)(2,1)S(1)} %shard_map.125), channel_id=1, source_target_pairs={{0,8},{8,0},{16,24},{24,16},{32,40},{40,32},{48,56},{56,48},{64,72... | collective-permute-start | bytes 786440 | tf_op jit(solution)/shard_map/ppermute | solution.py:56
  74.2 3.7 %collective-permute-start.23 = (f32[1,32,128]{2,1,0:T(8,128)S(1)}, f32[1,32,128]{2,1,0:T(8,128)S(1)}, u32[]{:S(2)}, u32[]{:S(2)}) collective-permute-start(f32[1,32,128]{2,1,0:T(8,128)S(1)} %get-tuple-element.90), channel_id=1, source_target_pairs={{0,4},{1,5},{2,6},{3,7},{4,0},{5,1},{6,2},{7,3},{8,12},{9,13},{10,... | collective-permute-start | bytes 49160 | tf_op jit(solution)/shard_map/ppermute | solution.py:56
  (3 other events, 11.9 us)

commit v5 on v4

--- a/solution.py
+++ b/solution.py
@@ -454,9 +454,11 @@
     feats = join(feats, other, 3)
     other = flip(feats, "col", Z_NEAR)
     other, chunks = tie(other, chunks)
-    own, to_d, to_f, to_g = [chip_pair(chunks, *at) for at in ((0, 0), (0, 1), (3, 1), (2, 1))]
+    own, to_d, to_f = [chip_pair(chunks, *at) for at in ((0, 0), (0, 1), (3, 1))]
     feats = join(feats, other, 1.2)
     other = flip(feats, "col", Z_FAR)
+    other, chunks = tie(other, chunks)
+    to_g = chip_pair(chunks, 2, 1)
     kept, sent = project(feats, other, norm_gain, query_weight, keyval_weight)
     got = flip(sent, "row", CORE)
     got, via_e, own, to_d, to_f, to_g = tie(got, via_e, own, to_d, to_f, to_g)

time: 79.7 us -> 79.7 us (level)
  no operation moved by 1% of the time
where the time goes in v5:
time: 79.7 us; the launch traced here: 79.5 us
  starting transfers between devices  35.6 us (45%)
  waiting for transfers between devices  28.2 us (35%)
  Pallas kernels  10.3 us (13%)
  local copies, waits for them, and re-layouts  3.62 us (5%)
  between operations  0.91 us (1%)
  other arithmetic  0.8 us (1%)
    ppermute x20, waiting for transfers between devices, flip(): return lax.ppermute(block, axis, [(i, i ^ bits) for i in range(size)])  26.9 us
    ppermute x20, starting transfers between devices, flip(): return lax.ppermute(block, axis, [(i, i ^ bits) for i in range(size)])  26.4 us
    ppermute x6, starting transfers between devices, shift_y(): lax.ppermute(block, 'row', [(i, (i + 4 * steps) % size) for i in range(si...  9.24 us
    unnamed x18, local copies, waits for them, and re-layouts  3.4 us
    pallas_call x3, Pallas kernels, place(): call(functools.partial(place_kernel, len(pieces), slots), jax.ShapeDtypeS...  3.38 us
    pallas_call x1, Pallas kernels, stage(): call(functools.partial(stage_kernel, groups), [like(chunks, len(group)) f...  2.41 us
    pallas_call x1, Pallas kernels, attend(): call(functools.partial(attend_kernel, features), jax.ShapeDtypeStruct((ro...  2.12 us
  transfers between devices with their start and end apart: 26, of which 13 were waited for; matrix products, arithmetic and copies ran while one was open for 1% of the time, Pallas kernels for 12%

profile of v5, /device:TPU:0, one launch (start us, length us, event | category | flops | bytes accessed | tf_op | source)
XLA Modules:
  0.0 79.5 jit_solution(2676245312871557253)
XLA Ops:
  0.6 1.7 %collective-permute-start = (bf16[1,32,128]{2,1,0:T(8,128)(2,1)}, bf16[1,32,128]{2,1,0:T(8,128)(2,1)S(1)}, u32[]{:S(2)}, u32[]{:S(2)}) collective-permute-start(bf16[1,32,128]{2,1,0:T(8,128)(2,1)} %bitcast.4), channel_id=1, source_target_pairs={{0,4},{1,5},{2,6},{3,7},{4,0},{5,1},{6,2},{7,3},{8,12},{9,13},{10,... | collective-permute-start | bytes 24584 | tf_op jit(solution)/shard_map/ppermute | solution.py:56
  2.3 2.4 %shard_map.105 = (bf16[2,1024,128]{2,1,0:T(8,128)(2,1)}, bf16[2,1024,128]{2,1,0:T(8,128)(2,1)}, bf16[2,1024,128]{2,1,0:T(8,128)(2,1)}, bf16[2,1024,128]{2,1,0:T(8,128)(2,1)}) custom-call(bf16[16,1024,128]{2,1,0:T(8,128)(2,1)} %bitcast.6), custom_call_target="tpu_custom_call" | custom-call | flops 1 | bytes 1 | tf_op jit(solution)/shard_map/pallas_call | solution.py:357
  4.7 1.6 %collective-permute-start.6 = (bf16[2,1024,128]{2,1,0:T(8,128)(2,1)}, bf16[2,1024,128]{2,1,0:T(8,128)(2,1)S(1)}, u32[]{:S(2)}, u32[]{:S(2)}) collective-permute-start(bf16[2,1024,128]{2,1,0:T(8,128)(2,1)} %get-tuple-element.66), channel_id=1, source_target_pairs={{0,32},{8,40},{16,48},{24,56},{32,64},{40,72},{48,80},{56,88},{64,... | collective-permute-start | bytes 1572872 | tf_op jit(solution)/shard_map/ppermute | solution.py:61
  6.4 1.7 %collective-permute-start.7 = (bf16[2,1024,128]{2,1,0:T(8,128)(2,1)}, bf16[2,1024,128]{2,1,0:T(8,128)(2,1)S(1)}, u32[]{:S(2)}, u32[]{:S(2)}) collective-permute-start(bf16[2,1024,128]{2,1,0:T(8,128)(2,1)} %get-tuple-element.67), channel_id=1, source_target_pairs={{0,96},{8,104},{16,112},{24,120},{32,0},{40,8},{48,16},{56,24},{64... | collective-permute-start | bytes 1572872 | tf_op jit(solution)/shard_map/ppermute | solution.py:61
  8.0 2.0 %collective-permute-start.8 = (bf16[2,1024,128]{2,1,0:T(8,128)(2,1)}, bf16[2,1024,128]{2,1,0:T(8,128)(2,1)S(1)}, u32[]{:S(2)}, u32[]{:S(2)}) collective-permute-start(bf16[2,1024,128]{2,1,0:T(8,128)(2,1)} %get-tuple-element.68), channel_id=1, source_target_pairs={{0,64},{8,72},{16,80},{24,88},{32,96},{40,104},{48,112},{56,120},{... | collective-permute-start | bytes 1572872 | tf_op jit(solution)/shard_map/ppermute | solution.py:61
  10.3 2.8 %collective-permute-start.4 = (bf16[2,1024,128]{2,1,0:T(8,128)(2,1)}, bf16[2,1024,128]{2,1,0:T(8,128)(2,1)S(1)}, u32[]{:S(2)}, u32[]{:S(2)}) collective-permute-start(bf16[2,1024,128]{2,1,0:T(8,128)(2,1)} %get-tuple-element.61), channel_id=1, source_target_pairs={{0,16},{8,24},{16,0},{24,8},{32,48},{40,56},{48,32},{56,40},{64,80... | collective-permute-start | bytes 1572872 | tf_op jit(solution)/shard_map/ppermute | solution.py:56
  13.1 1.9 %collective-permute-start.1 = (bf16[2,32,128]{2,1,0:T(8,128)(2,1)S(1)}, bf16[2,32,128]{2,1,0:T(8,128)(2,1)S(1)}, u32[]{:S(2)}, u32[]{:S(2)}) collective-permute-start(bf16[2,32,128]{2,1,0:T(8,128)(2,1)S(1)} %shard_map.106.own_ref), channel_id=1, source_target_pairs={{0,1},{1,0},{2,3},{3,2},{4,5},{5,4},{6,7},{7,6},{8,9},{9,8},{10,11... | collective-permute-start | bytes 49160 | tf_op jit(solution)/shard_map/ppermute | solution.py:56
  15.0 1.8 %collective-permute-done.1.other_ref = bf16[2,32,128]{2,1,0:T(8,128)(2,1)S(1)} collective-permute-done((bf16[2,32,128]{2,1,0:T(8,128)(2,1)S(1)}, bf16[2,32,128]{2,1,0:T(8,128)(2,1)S(1)}, u32[]{:S(2)}, u32[]{:S(2)}) %collective-permute-start.1) | collective-permute-done | bytes 16416 | tf_op jit(solution)/shard_map/ppermute | solution.py:56
  16.8 3.9 %collective-permute-start.2 = (bf16[4,32,128]{2,1,0:T(8,128)(2,1)S(1)}, bf16[4,32,128]{2,1,0:T(8,128)(2,1)S(1)}, u32[]{:S(2)}, u32[]{:S(2)}) collective-permute-start(bf16[4,32,128]{2,1,0:T(8,128)(2,1)S(1)} %shard_map.107.near_ref), channel_id=1, source_target_pairs={{0,2},{1,3},{2,0},{3,1},{4,6},{5,7},{6,4},{7,5},{8,10},{9,11},{10,... | collective-permute-start | bytes 98312 | tf_op jit(solution)/shard_map/ppermute | solution.py:56
  20.7 1.9 %collective-permute-done.2.far_ref = bf16[4,32,128]{2,1,0:T(8,128)(2,1)S(1)} collective-permute-done((bf16[4,32,128]{2,1,0:T(8,128)(2,1)S(1)}, bf16[4,32,128]{2,1,0:T(8,128)(2,1)S(1)}, u32[]{:S(2)}, u32[]{:S(2)}) %collective-permute-start.2) | collective-permute-done | bytes 32800 | tf_op jit(solution)/shard_map/ppermute | solution.py:56
  22.6 2.2 %copy-done = bf16[1024,2048]{1,0:T(8,128)(2,1)S(1)} copy-done((bf16[1024,2048]{1,0:T(8,128)(2,1)S(1)}, bf16[1024,2048]{1,0:T(8,128)(2,1)}, u32[]{:S(2)}) %copy-start) | copy-done | bytes 4194328
  25.8 1.2 %copy-done.6 = bf16[16384,128]{1,0:T(8,128)(2,1)S(1)} copy-done((bf16[16384,128]{1,0:T(8,128)(2,1)S(1)}, bf16[16384,128]{1,0:T(8,128)(2,1)}, u32[]{:S(2)}) %copy-start.6) | copy-done | bytes 4194328
  28.1 2.7 %collective-permute-start.12 = (bf16[2,1024,128]{2,1,0:T(8,128)(2,1)S(1)}, bf16[2,1024,128]{2,1,0:T(8,128)(2,1)S(1)}, u32[]{:S(2)}, u32[]{:S(2)}) collective-permute-start(bf16[2,1024,128]{2,1,0:T(8,128)(2,1)S(1)} %get-tuple-element.76), channel_id=1, source_target_pairs={{0,16},{8,24},{16,0},{24,8},{32,48},{40,56},{48,32},{56,40},{64,80... | collective-permute-start | bytes 1572872 | tf_op jit(solution)/shard_map/ppermute | solution.py:56
  30.8 1.3 %collective-permute-done.8.refs_3_ = bf16[2,1024,128]{2,1,0:T(8,128)(2,1)S(1)} collective-permute-done((bf16[2,1024,128]{2,1,0:T(8,128)(2,1)}, bf16[2,1024,128]{2,1,0:T(8,128)(2,1)S(1)}, u32[]{:S(2)}, u32[]{:S(2)}) %collective-permute-start.8) | collective-permute-done | bytes 524320 | tf_op jit(solution)/shard_map/ppermute | solution.py:61
  32.1 1.9 %collective-permute-done.5.got_ref = f32[8,2432]{1,0:T(8,128)S(1)} collective-permute-done((f32[8,2432]{1,0:T(8,128)S(1)}, f32[8,2432]{1,0:T(8,128)S(1)}, u32[]{:S(2)}, u32[]{:S(2)}) %collective-permute-start.5) | collective-permute-done | bytes 77856 | tf_op jit(solution)/shard_map/ppermute | solution.py:56
  34.3 1.1 %collective-permute-start.9 = (f32[4,2432]{1,0:T(4,128)S(1)}, f32[4,2432]{1,0:T(4,128)S(1)}, u32[]{:S(2)}, u32[]{:S(2)}) collective-permute-start(f32[4,2432]{1,0:T(4,128)S(1)} %get-tuple-element.71), channel_id=1, source_target_pairs={{0,96},{8,104},{16,112},{24,120},{32,64},{40,72},{48,80},{56,88},{... | collective-permute-start | bytes 116744 | tf_op jit(solution)/shard_map/ppermute | solution.py:56
  35.5 4.1 %collective-permute-done.9.got_ref = f32[4,2432]{1,0:T(4,128)S(1)} collective-permute-done((f32[4,2432]{1,0:T(4,128)S(1)}, f32[4,2432]{1,0:T(4,128)S(1)}, u32[]{:S(2)}, u32[]{:S(2)}) %collective-permute-start.9) | collective-permute-done | bytes 38944 | tf_op jit(solution)/shard_map/ppermute | solution.py:56
  40.7 2.8 %collective-permute-done.10.got_ref = f32[2,2432]{1,0:T(2,128)S(1)} collective-permute-done((f32[2,2432]{1,0:T(2,128)S(1)}, f32[2,2432]{1,0:T(2,128)S(1)}, u32[]{:S(2)}, u32[]{:S(2)}) %collective-permute-start.10) | collective-permute-done | bytes 19488 | tf_op jit(solution)/shard_map/ppermute | solution.py:56
  43.5 2.1 %shard_map.112.own_ref = bf16[2,2048]{1,0:T(2,128)(2,1)S(1)} custom-call(s32[2,128]{1,0:T(2,128)S(1)} %broadcast_in_dim.7.lengths_ref, f32[2,2432]{1,0:T(2,128)S(1)} %get-tuple-element.72.kept_ref, f32[2,2432]{1,0:T(2,128)S(1)} %collective-permute-done.10.got_ref, f32[2,128]{1,0:T(2,128)S(1)} %get-tuple-element.74.cos_ref, ...), custom_call_target="tpu_custom_call" | custom-call | flops 2200000000 | bytes 1 | tf_op jit(solution)/shard_map/pallas_call | solution.py:253
  45.7 3.6 %collective-permute-done.11.other_ref = bf16[2,2048]{1,0:T(2,128)(2,1)S(1)} collective-permute-done((bf16[2,2048]{1,0:T(2,128)(2,1)S(1)}, bf16[2,2048]{1,0:T(2,128)(2,1)S(1)}, u32[]{:S(2)}, u32[]{:S(2)}) %collective-permute-start.11) | collective-permute-done | bytes 8224 | tf_op jit(solution)/shard_map/ppermute | solution.py:56
  49.4 1.1 %collective-permute-start.15 = (bf16[4,2048]{1,0:T(4,128)(2,1)S(1)}, bf16[4,2048]{1,0:T(4,128)(2,1)S(1)}, u32[]{:S(2)}, u32[]{:S(2)}) collective-permute-start(bf16[4,2048]{1,0:T(4,128)(2,1)S(1)} %shard_map.113.own_ref), channel_id=1, source_target_pairs={{0,96},{8,104},{16,112},{24,120},{32,64},{40,72},{48,80},{56,88},{... | collective-permute-start | bytes 49160 | tf_op jit(solution)/shard_map/ppermute | solution.py:56
  50.5 2.2 %collective-permute-start.20 = (bf16[2,1024,128]{2,1,0:T(8,128)(2,1)S(1)}, bf16[2,1024,128]{2,1,0:T(8,128)(2,1)S(1)}, u32[]{:S(2)}, u32[]{:S(2)}) collective-permute-start(bf16[2,1024,128]{2,1,0:T(8,128)(2,1)S(1)} %collective-permute-done.12), channel_id=1, source_target_pairs={{0,96},{8,104},{16,112},{24,120},{32,0},{40,8},{48,16},{56,24},{64... | collective-permute-start | bytes 1572872 | tf_op jit(solution)/shard_map/ppermute | solution.py:61
  52.8 1.7 %collective-permute-done.15.other_ref = bf16[4,2048]{1,0:T(4,128)(2,1)S(1)} collective-permute-done((bf16[4,2048]{1,0:T(4,128)(2,1)S(1)}, bf16[4,2048]{1,0:T(4,128)(2,1)S(1)}, u32[]{:S(2)}, u32[]{:S(2)}) %collective-permute-start.15) | collective-permute-done | bytes 16416 | tf_op jit(solution)/shard_map/ppermute | solution.py:56
  55.7 1.7 %collective-permute-start.16 = (bf16[8,2048]{1,0:T(8,128)(2,1)S(1)}, bf16[8,2048]{1,0:T(8,128)(2,1)S(1)}, u32[]{:S(2)}, u32[]{:S(2)}) collective-permute-start(bf16[8,2048]{1,0:T(8,128)(2,1)S(1)} %shard_map.116.own_ref), channel_id=1, source_target_pairs={{0,16},{8,24},{16,0},{24,8},{32,48},{40,56},{48,32},{56,40},{64,80... | collective-permute-start | bytes 98312 | tf_op jit(solution)/shard_map/ppermute | solution.py:56
  57.4 2.0 %collective-permute-start.22 = (bf16[2,1024,128]{2,1,0:T(8,128)(2,1)S(1)}, bf16[2,1024,128]{2,1,0:T(8,128)(2,1)S(1)}, u32[]{:S(2)}, u32[]{:S(2)}) collective-permute-start(bf16[2,1024,128]{2,1,0:T(8,128)(2,1)S(1)} %shard_map.121), channel_id=1, source_target_pairs={{0,16},{8,24},{16,0},{24,8},{32,48},{40,56},{48,32},{56,40},{64,80... | collective-permute-start | bytes 1572872 | tf_op jit(solution)/shard_map/ppermute | solution.py:56
  59.4 2.0 %collective-permute-done.16.other_ref = bf16[8,2048]{1,0:T(8,128)(2,1)S(1)} collective-permute-done((bf16[8,2048]{1,0:T(8,128)(2,1)S(1)}, bf16[8,2048]{1,0:T(8,128)(2,1)S(1)}, u32[]{:S(2)}, u32[]{:S(2)}) %collective-permute-start.16) | collective-permute-done | bytes 32800 | tf_op jit(solution)/shard_map/ppermute | solution.py:56
  61.5 1.7 %collective-permute-start.24 = (bf16[2,1024,128]{2,1,0:T(8,128)(2,1)S(1)}, bf16[2,1024,128]{2,1,0:T(8,128)(2,1)S(1)}, u32[]{:S(2)}, u32[]{:S(2)}) collective-permute-start(bf16[2,1024,128]{2,1,0:T(8,128)(2,1)S(1)} %collective-permute-done.14), channel_id=1, source_target_pairs={{0,64},{8,72},{16,80},{24,88},{32,96},{40,104},{48,112},{56,120},{... | collective-permute-start | bytes 1572872 | tf_op jit(solution)/shard_map/ppermute | solution.py:61
  64.1 3.6 %collective-permute-start.18 = (f32[4,32,128]{2,1,0:T(8,128)S(1)}, f32[4,32,128]{2,1,0:T(8,128)S(1)}, u32[]{:S(2)}, u32[]{:S(2)}) collective-permute-start(f32[4,32,128]{2,1,0:T(8,128)S(1)} %get-tuple-element.87), channel_id=1, source_target_pairs={{0,2},{1,3},{2,0},{3,1},{4,6},{5,7},{6,4},{7,5},{8,10},{9,11},{10,... | collective-permute-start | bytes 196616 | tf_op jit(solution)/shard_map/ppermute | solution.py:56
  67.8 2.4 %collective-permute-done.18.got_ref = f32[4,32,128]{2,1,0:T(8,128)S(1)} collective-permute-done((f32[4,32,128]{2,1,0:T(8,128)S(1)}, f32[4,32,128]{2,1,0:T(8,128)S(1)}, u32[]{:S(2)}, u32[]{:S(2)}) %collective-permute-start.18) | collective-permute-done | bytes 65568 | tf_op jit(solution)/shard_map/ppermute | solution.py:56
  70.2 1.5 %collective-permute-start.21 = (f32[2,32,128]{2,1,0:T(8,128)S(1)}, f32[2,32,128]{2,1,0:T(8,128)S(1)}, u32[]{:S(2)}, u32[]{:S(2)}) collective-permute-start(f32[2,32,128]{2,1,0:T(8,128)S(1)} %get-tuple-element.91), channel_id=1, source_target_pairs={{0,1},{1,0},{2,3},{3,2},{4,5},{5,4},{6,7},{7,6},{8,9},{9,8},{10,11... | collective-permute-start | bytes 98312 | tf_op jit(solution)/shard_map/ppermute | solution.py:56
  71.8 1.4 %shard_map.122.refs_3_ = bf16[1024,2048]{1,0:T(8,128)(2,1)} custom-call(bf16[2,1024,128]{2,1,0:T(8,128)(2,1)S(1)} %get-tuple-element.79.refs_0_, bf16[2,1024,128]{2,1,0:T(8,128)(2,1)S(1)} %collective-permute-done.6.refs_1_, bf16[2,1024,128]{2,1,0:T(8,128)(2,1)S(1)} %collective-permute-done.7.refs_2_, ...), custom_call_target="tpu_custom_call" | custom-call | flops 1 | bytes 1 | tf_op jit(solution)/shard_map/pallas_call | solution.py:410
  75.5 2.5 %collective-permute-done.23 = f32[1,32,128]{2,1,0:T(8,128)S(1)} collective-permute-done((f32[1,32,128]{2,1,0:T(8,128)S(1)}, f32[1,32,128]{2,1,0:T(8,128)S(1)}, u32[]{:S(2)}, u32[]{:S(2)}) %collective-permute-start.23) | collective-permute-done | bytes 16416 | tf_op jit(solution)/shard_map/ppermute | solution.py:56
  (70 shorter events, 10.0 us)
Async XLA Ops:
  0.6 9.6 %copy-start.4 = (bf16[32,128]{1,0:T(8,128)(2,1)S(1)}, bf16[32,128]{1,0:T(8,128)(2,1)}, u32[]{:S(2)}) copy-start(bf16[32,128]{1,0:T(8,128)(2,1)} %param.9) | copy-start | bytes 24580
  0.6 9.4 %copy-start.8 = (s32[2]{0:T(128)S(1)}, s32[2]{0:T(128)}, u32[]{:S(2)}) copy-start(s32[2]{0:T(128)} %param.16) | copy-start | bytes 28
  0.6 9.6 %collective-permute-start = (bf16[1,32,128]{2,1,0:T(8,128)(2,1)}, bf16[1,32,128]{2,1,0:T(8,128)(2,1)S(1)}, u32[]{:S(2)}, u32[]{:S(2)}) collective-permute-start(bf16[1,32,128]{2,1,0:T(8,128)(2,1)} %bitcast.4), channel_id=1, source_target_pairs={{0,4},{1,5},{2,6},{3,7},{4,0},{5,1},{6,2},{7,3},{8,12},{9,13},{10,... | collective-permute-start | bytes 24584 | tf_op jit(solution)/shard_map/ppermute | solution.py:56
  4.7 26.1 %collective-permute-start.6 = (bf16[2,1024,128]{2,1,0:T(8,128)(2,1)}, bf16[2,1024,128]{2,1,0:T(8,128)(2,1)S(1)}, u32[]{:S(2)}, u32[]{:S(2)}) collective-permute-start(bf16[2,1024,128]{2,1,0:T(8,128)(2,1)} %get-tuple-element.66), channel_id=1, source_target_pairs={{0,32},{8,40},{16,48},{24,56},{32,64},{40,72},{48,80},{56,88},{64,... | collective-permute-start | bytes 1572872 | tf_op jit(solution)/shard_map/ppermute | solution.py:61
  6.4 24.5 %collective-permute-start.7 = (bf16[2,1024,128]{2,1,0:T(8,128)(2,1)}, bf16[2,1024,128]{2,1,0:T(8,128)(2,1)S(1)}, u32[]{:S(2)}, u32[]{:S(2)}) collective-permute-start(bf16[2,1024,128]{2,1,0:T(8,128)(2,1)} %get-tuple-element.67), channel_id=1, source_target_pairs={{0,96},{8,104},{16,112},{24,120},{32,0},{40,8},{48,16},{56,24},{64... | collective-permute-start | bytes 1572872 | tf_op jit(solution)/shard_map/ppermute | solution.py:61
  8.0 24.0 %collective-permute-start.8 = (bf16[2,1024,128]{2,1,0:T(8,128)(2,1)}, bf16[2,1024,128]{2,1,0:T(8,128)(2,1)S(1)}, u32[]{:S(2)}, u32[]{:S(2)}) collective-permute-start(bf16[2,1024,128]{2,1,0:T(8,128)(2,1)} %get-tuple-element.68), channel_id=1, source_target_pairs={{0,64},{8,72},{16,80},{24,88},{32,96},{40,104},{48,112},{56,120},{... | collective-permute-start | bytes 1572872 | tf_op jit(solution)/shard_map/ppermute | solution.py:61
  10.3 16.8 %collective-permute-start.4 = (bf16[2,1024,128]{2,1,0:T(8,128)(2,1)}, bf16[2,1024,128]{2,1,0:T(8,128)(2,1)S(1)}, u32[]{:S(2)}, u32[]{:S(2)}) collective-permute-start(bf16[2,1024,128]{2,1,0:T(8,128)(2,1)} %get-tuple-element.61), channel_id=1, source_target_pairs={{0,16},{8,24},{16,0},{24,8},{32,48},{40,56},{48,32},{56,40},{64,80... | collective-permute-start | bytes 1572872 | tf_op jit(solution)/shard_map/ppermute | solution.py:56
  13.1 7.6 %copy-start.7 = (bf16[1024]{0:T(1024)(128)(2,1)S(1)}, bf16[1024]{0:T(1024)(128)(2,1)}, u32[]{:S(2)}) copy-start(bf16[1024]{0:T(1024)(128)(2,1)} %param.10) | copy-start | bytes 6148
  13.1 9.5 %copy-start.3 = (bf16[1024,256]{1,0:T(8,128)(2,1)S(1)}, bf16[1024,256]{1,0:T(8,128)(2,1)}, u32[]{:S(2)}) copy-start(bf16[1024,256]{1,0:T(8,128)(2,1)} %keyval_ref.1) | copy-start | bytes 1572868
  13.1 3.7 %collective-permute-start.1 = (bf16[2,32,128]{2,1,0:T(8,128)(2,1)S(1)}, bf16[2,32,128]{2,1,0:T(8,128)(2,1)S(1)}, u32[]{:S(2)}, u32[]{:S(2)}) collective-permute-start(bf16[2,32,128]{2,1,0:T(8,128)(2,1)S(1)} %shard_map.106.own_ref), channel_id=1, source_target_pairs={{0,1},{1,0},{2,3},{3,2},{4,5},{5,4},{6,7},{7,6},{8,9},{9,8},{10,11... | collective-permute-start | bytes 49160 | tf_op jit(solution)/shard_map/ppermute | solution.py:56
  16.8 5.8 %collective-permute-start.2 = (bf16[4,32,128]{2,1,0:T(8,128)(2,1)S(1)}, bf16[4,32,128]{2,1,0:T(8,128)(2,1)S(1)}, u32[]{:S(2)}, u32[]{:S(2)}) collective-permute-start(bf16[4,32,128]{2,1,0:T(8,128)(2,1)S(1)} %shard_map.107.near_ref), channel_id=1, source_target_pairs={{0,2},{1,3},{2,0},{3,1},{4,6},{5,7},{6,4},{7,5},{8,10},{9,11},{10,... | collective-permute-start | bytes 98312 | tf_op jit(solution)/shard_map/ppermute | solution.py:56
  25.7 1.5 %collective-permute-start.3 = (f32[16,2432]{1,0:T(8,128)S(1)}, f32[16,2432]{1,0:T(8,128)S(1)}, u32[]{:S(2)}, u32[]{:S(2)}) collective-permute-start(f32[16,2432]{1,0:T(8,128)S(1)} %get-tuple-element.60), channel_id=1, source_target_pairs={{0,8},{8,0},{16,24},{24,16},{32,40},{40,32},{48,56},{56,48},{64,72... | collective-permute-start | bytes 466952 | tf_op jit(solution)/shard_map/ppermute | solution.py:56
  27.2 6.8 %collective-permute-start.5 = (f32[8,2432]{1,0:T(8,128)S(1)}, f32[8,2432]{1,0:T(8,128)S(1)}, u32[]{:S(2)}, u32[]{:S(2)}) collective-permute-start(f32[8,2432]{1,0:T(8,128)S(1)} %get-tuple-element.65), channel_id=1, source_target_pairs={{0,16},{8,24},{16,0},{24,8},{32,48},{40,56},{48,32},{56,40},{64,80... | collective-permute-start | bytes 233480 | tf_op jit(solution)/shard_map/ppermute | solution.py:56
  28.1 21.3 %collective-permute-start.12 = (bf16[2,1024,128]{2,1,0:T(8,128)(2,1)S(1)}, bf16[2,1024,128]{2,1,0:T(8,128)(2,1)S(1)}, u32[]{:S(2)}, u32[]{:S(2)}) collective-permute-start(bf16[2,1024,128]{2,1,0:T(8,128)(2,1)S(1)} %get-tuple-element.76), channel_id=1, source_target_pairs={{0,16},{8,24},{16,0},{24,8},{32,48},{40,56},{48,32},{56,40},{64,80... | collective-permute-start | bytes 1572872 | tf_op jit(solution)/shard_map/ppermute | solution.py:56
  34.2 5.5 %collective-permute-start.13 = (bf16[7,1024,128]{2,1,0:T(8,128)(2,1)S(1)}, bf16[7,1024,128]{2,1,0:T(8,128)(2,1)S(1)}, u32[]{:S(2)}, u32[]{:S(2)}) collective-permute-start(bf16[7,1024,128]{2,1,0:T(8,128)(2,1)S(1)} %shard_map.114), channel_id=1, source_target_pairs={{0,8},{8,0},{16,24},{24,16},{32,40},{40,32},{48,56},{56,48},{64,72... | collective-permute-start | bytes 5505032 | tf_op jit(solution)/shard_map/ppermute | solution.py:56
  34.3 9.2 %copy-start.1 = (bf16[2,8192,128]{2,1,0:T(8,128)(2,1)S(1)}, bf16[2,8192,128]{2,1,0:T(8,128)(2,1)}, u32[]{:S(2)}) copy-start(bf16[2,8192,128]{2,1,0:T(8,128)(2,1)} %key_ref.1) | copy-start | bytes 12582916
  34.3 9.2 %copy-start.2 = (bf16[2,8192,128]{2,1,0:T(8,128)(2,1)S(1)}, bf16[2,8192,128]{2,1,0:T(8,128)(2,1)}, u32[]{:S(2)}) copy-start(bf16[2,8192,128]{2,1,0:T(8,128)(2,1)} %value_ref.1) | copy-start | bytes 12582916
  34.3 5.3 %collective-permute-start.9 = (f32[4,2432]{1,0:T(4,128)S(1)}, f32[4,2432]{1,0:T(4,128)S(1)}, u32[]{:S(2)}, u32[]{:S(2)}) collective-permute-start(f32[4,2432]{1,0:T(4,128)S(1)} %get-tuple-element.71), channel_id=1, source_target_pairs={{0,96},{8,104},{16,112},{24,120},{32,64},{40,72},{48,80},{56,88},{... | collective-permute-start | bytes 116744 | tf_op jit(solution)/shard_map/ppermute | solution.py:56
  39.6 3.9 %collective-permute-start.10 = (f32[2,2432]{1,0:T(2,128)S(1)}, f32[2,2432]{1,0:T(2,128)S(1)}, u32[]{:S(2)}, u32[]{:S(2)}) collective-permute-start(f32[2,2432]{1,0:T(2,128)S(1)} %get-tuple-element.73), channel_id=1, source_target_pairs={{0,32},{8,40},{16,48},{24,56},{32,0},{40,8},{48,16},{56,24},{64,96... | collective-permute-start | bytes 58376 | tf_op jit(solution)/shard_map/ppermute | solution.py:56
  39.8 15.8 %collective-permute-start.14 = (bf16[2,1024,128]{2,1,0:T(8,128)(2,1)S(1)}, bf16[2,1024,128]{2,1,0:T(8,128)(2,1)S(1)}, u32[]{:S(2)}, u32[]{:S(2)}) collective-permute-start(bf16[2,1024,128]{2,1,0:T(8,128)(2,1)S(1)} %shard_map.115), channel_id=1, source_target_pairs={{0,16},{8,24},{16,0},{24,8},{32,48},{40,56},{48,32},{56,40},{64,80... | collective-permute-start | bytes 1572872 | tf_op jit(solution)/shard_map/ppermute | solution.py:56
  45.6 3.7 %collective-permute-start.11 = (bf16[2,2048]{1,0:T(2,128)(2,1)S(1)}, bf16[2,2048]{1,0:T(2,128)(2,1)S(1)}, u32[]{:S(2)}, u32[]{:S(2)}) collective-permute-start(bf16[2,2048]{1,0:T(2,128)(2,1)S(1)} %shard_map.112.own_ref), channel_id=1, source_target_pairs={{0,32},{8,40},{16,48},{24,56},{32,0},{40,8},{48,16},{56,24},{64,96... | collective-permute-start | bytes 24584 | tf_op jit(solution)/shard_map/ppermute | solution.py:56
  49.4 5.2 %collective-permute-start.15 = (bf16[4,2048]{1,0:T(4,128)(2,1)S(1)}, bf16[4,2048]{1,0:T(4,128)(2,1)S(1)}, u32[]{:S(2)}, u32[]{:S(2)}) collective-permute-start(bf16[4,2048]{1,0:T(4,128)(2,1)S(1)} %shard_map.113.own_ref), channel_id=1, source_target_pairs={{0,96},{8,104},{16,112},{24,120},{32,64},{40,72},{48,80},{56,88},{... | collective-permute-start | bytes 49160 | tf_op jit(solution)/shard_map/ppermute | solution.py:56
  50.5 17.3 %collective-permute-start.20 = (bf16[2,1024,128]{2,1,0:T(8,128)(2,1)S(1)}, bf16[2,1024,128]{2,1,0:T(8,128)(2,1)S(1)}, u32[]{:S(2)}, u32[]{:S(2)}) collective-permute-start(bf16[2,1024,128]{2,1,0:T(8,128)(2,1)S(1)} %collective-permute-done.12), channel_id=1, source_target_pairs={{0,96},{8,104},{16,112},{24,120},{32,0},{40,8},{48,16},{56,24},{64... | collective-permute-start | bytes 1572872 | tf_op jit(solution)/shard_map/ppermute | solution.py:61
  52.7 15.0 %collective-permute-start.19 = (bf16[2,1024,128]{2,1,0:T(8,128)(2,1)S(1)}, bf16[2,1024,128]{2,1,0:T(8,128)(2,1)S(1)}, u32[]{:S(2)}, u32[]{:S(2)}) collective-permute-start(bf16[2,1024,128]{2,1,0:T(8,128)(2,1)S(1)} %shard_map.119), channel_id=1, source_target_pairs={{0,32},{8,40},{16,48},{24,56},{32,64},{40,72},{48,80},{56,88},{64,... | collective-permute-start | bytes 1572872 | tf_op jit(solution)/shard_map/ppermute | solution.py:61
  55.7 5.8 %collective-permute-start.16 = (bf16[8,2048]{1,0:T(8,128)(2,1)S(1)}, bf16[8,2048]{1,0:T(8,128)(2,1)S(1)}, u32[]{:S(2)}, u32[]{:S(2)}) collective-permute-start(bf16[8,2048]{1,0:T(8,128)(2,1)S(1)} %shard_map.116.own_ref), channel_id=1, source_target_pairs={{0,16},{8,24},{16,0},{24,8},{32,48},{40,56},{48,32},{56,40},{64,80... | collective-permute-start | bytes 98312 | tf_op jit(solution)/shard_map/ppermute | solution.py:56
  57.4 15.8 %collective-permute-start.22 = (bf16[2,1024,128]{2,1,0:T(8,128)(2,1)S(1)}, bf16[2,1024,128]{2,1,0:T(8,128)(2,1)S(1)}, u32[]{:S(2)}, u32[]{:S(2)}) collective-permute-start(bf16[2,1024,128]{2,1,0:T(8,128)(2,1)S(1)} %shard_map.121), channel_id=1, source_target_pairs={{0,16},{8,24},{16,0},{24,8},{32,48},{40,56},{48,32},{56,40},{64,80... | collective-permute-start | bytes 1572872 | tf_op jit(solution)/shard_map/ppermute | solution.py:56
  61.5 1.7 %collective-permute-start.17 = (bf16[16,2048]{1,0:T(8,128)(2,1)S(1)}, bf16[16,2048]{1,0:T(8,128)(2,1)S(1)}, u32[]{:S(2)}, u32[]{:S(2)}) collective-permute-start(bf16[16,2048]{1,0:T(8,128)(2,1)S(1)} %shard_map.117.own_ref), channel_id=1, source_target_pairs={{0,8},{8,0},{16,24},{24,16},{32,40},{40,32},{48,56},{56,48},{64,72... | collective-permute-start | bytes 196616 | tf_op jit(solution)/shard_map/ppermute | solution.py:56
  61.5 17.1 %collective-permute-start.24 = (bf16[2,1024,128]{2,1,0:T(8,128)(2,1)S(1)}, bf16[2,1024,128]{2,1,0:T(8,128)(2,1)S(1)}, u32[]{:S(2)}, u32[]{:S(2)}) collective-permute-start(bf16[2,1024,128]{2,1,0:T(8,128)(2,1)S(1)} %collective-permute-done.14), channel_id=1, source_target_pairs={{0,64},{8,72},{16,80},{24,88},{32,96},{40,104},{48,112},{56,120},{... | collective-permute-start | bytes 1572872 | tf_op jit(solution)/shard_map/ppermute | solution.py:61
  64.1 6.1 %collective-permute-start.18 = (f32[4,32,128]{2,1,0:T(8,128)S(1)}, f32[4,32,128]{2,1,0:T(8,128)S(1)}, u32[]{:S(2)}, u32[]{:S(2)}) collective-permute-start(f32[4,32,128]{2,1,0:T(8,128)S(1)} %get-tuple-element.87), channel_id=1, source_target_pairs={{0,2},{1,3},{2,0},{3,1},{4,6},{5,7},{6,4},{7,5},{8,10},{9,11},{10,... | collective-permute-start | bytes 196616 | tf_op jit(solution)/shard_map/ppermute | solution.py:56
  70.2 4.0 %collective-permute-start.21 = (f32[2,32,128]{2,1,0:T(8,128)S(1)}, f32[2,32,128]{2,1,0:T(8,128)S(1)}, u32[]{:S(2)}, u32[]{:S(2)}) collective-permute-start(f32[2,32,128]{2,1,0:T(8,128)S(1)} %get-tuple-element.91), channel_id=1, source_target_pairs={{0,1},{1,0},{2,3},{3,2},{4,5},{5,4},{6,7},{7,6},{8,9},{9,8},{10,11... | collective-permute-start | bytes 98312 | tf_op jit(solution)/shard_map/ppermute | solution.py:56
  71.7 6.8 %collective-permute-start.25 = (bf16[1,1024,128]{2,1,0:T(8,128)(2,1)S(1)}, bf16[1,1024,128]{2,1,0:T(8,128)(2,1)S(1)}, u32[]{:S(2)}, u32[]{:S(2)}) collective-permute-start(bf16[1,1024,128]{2,1,0:T(8,128)(2,1)S(1)} %shard_map.125), channel_id=1, source_target_pairs={{0,8},{8,0},{16,24},{24,16},{32,40},{40,32},{48,56},{56,48},{64,72... | collective-permute-start | bytes 786440 | tf_op jit(solution)/shard_map/ppermute | solution.py:56
  74.2 3.7 %collective-permute-start.23 = (f32[1,32,128]{2,1,0:T(8,128)S(1)}, f32[1,32,128]{2,1,0:T(8,128)S(1)}, u32[]{:S(2)}, u32[]{:S(2)}) collective-permute-start(f32[1,32,128]{2,1,0:T(8,128)S(1)} %get-tuple-element.94), channel_id=1, source_target_pairs={{0,4},{1,5},{2,6},{3,7},{4,0},{5,1},{6,2},{7,3},{8,12},{9,13},{10,... | collective-permute-start | bytes 49160 | tf_op jit(solution)/shard_map/ppermute | solution.py:56
  (3 other events, 11.9 us)
